TPU v7x, 512 devices: a whole 4x8x8 slice. The times are simulated.
512 devices in a mesh: gx: 64 (over x, z, y_lo), gz: 8 (over y_hi, core).
Axes of the slice: x: 4, y: 8 (y_hi: 4, y_lo: 2; y = y_hi * 2 + y_lo), z: 8, core: 2. Of those that a mesh axis runs over, the one named last changes fastest.
Arguments:
- velocity: float32 [3, 1024, 64, 256], P(None, 'gx', 'gz'), may hold values from -6 to 6
- pressure: float32 [1024, 64, 256], P('gx', 'gz'), may hold values from 1 to 3
- stress_old: float32 [6, 1024, 64, 256], P(None, 'gx', 'gz'), may hold values from -6 to 6
- plastic: float32 [1024, 64, 256], P('gx', 'gz'), may hold values from 0 to 2
- viscosity: float32 [1024, 64, 256], P('gx', 'gz'), may hold values from 1 to 30
- weak_seed: int32 [1024, 64, 256], P('gx', 'gz'), may hold values 0 or 1
Outputs:
- velocity_out: float32 [3, 1024, 64, 256], P(None, 'gx', 'gz')
- pressure_out: float32 [1024, 64, 256], P('gx', 'gz')
- stress_out: float32 [6, 1024, 64, 256], P(None, 'gx', 'gz')
- plastic_out: float32 [1024, 64, 256], P('gx', 'gz')
- yield_peak: float32 [2], replicated
All inputs are finite; a program needn't handle non-finite values. No bound on the sum of `weak_seed` on one device may be relied on, other than what follows from the above.
Results may differ from a plain program's by a relative error of at most 0.000059.
Values sent between devices are 32-bit elements; how exact they have to be, the bound alone decides.
No kernel may reach another device: no remote copies, remote signals or barrier semaphores. Data moves between devices by JAX's collectives and lax.ppermute only.
A program may use at most 64 MiB of HBM per device.

v0:
```python
import math

import jax
import jax.numpy as jnp
from jax import lax
from jax.sharding import Mesh
from jax.sharding import PartitionSpec as P

ITERS = 2
GX = ("gx_0", "gx_1", "gx_2")
GZ = ("gz_0", "gz_1")
GX_GZ = ("gx_0", "gx_1", "gx_2", "gz_0", "gz_1")


unnormalized_weights = [math.exp(-(k * k) / 18.0) for k in range(-6, 7)]
weight_total = sum(unnormalized_weights)
gauss_weights = [value / weight_total for value in unnormalized_weights]
shear_time_increment = 20.0


def padded_2(block, sides, width):
    for axis, dim in sides:
        count = lax.axis_size(axis)
        forward = [(i, i + 1) for i in range(count - 1)]
        backward = [(target, source) for source, target in forward]
        low = lax.ppermute(
            lax.slice_in_dim(block, block.shape[dim] - width, None, axis=dim), axis, forward
        )
        high = lax.ppermute(lax.slice_in_dim(block, 0, width, axis=dim), axis, backward)
        block = jnp.concatenate([low, block, high], axis=dim)
    return block


def with_halo(shard, sides, width):
    edges = {}
    for axis, dim in sides:
        devices, length = (lax.axis_size(axis), shard.shape[dim])
        up = [(i, (i + 1) % devices) for i in range(devices - 1)]
        last = lax.slice_in_dim(shard, length - width, length, axis=dim)
        initial = lax.slice_in_dim(shard, 0, width, axis=dim)
        edges[dim] = (
            lax.ppermute(last, axis, up),
            lax.ppermute(initial, axis, [(b, a) for a, b in up]),
        )
    done = []
    for _, dim in sides:
        low, high = edges[dim]
        around = [(width, width) if d in done else (0, 0) for d in range(shard.ndim)]
        shard = jnp.concatenate([jnp.pad(low, around), shard, jnp.pad(high, around)], axis=dim)
        done.append(dim)
    return shard


def one_axis_at_a_time(shard, axes):
    for axis in axes:
        shard = lax.pmax(shard, axis)
    return shard


def smooth_slices(padded, axis, count):
    total = gauss_weights[0] * lax.slice_in_dim(padded, 0, count, axis=axis)
    for index in range(1, 13):
        total = total + gauss_weights[index] * lax.slice_in_dim(
            padded, index, index + count, axis=axis
        )
    return total


def y_matrix(length):
    places = jnp.arange(length)
    gap = (places[:, None] - places[None, :]).astype(jnp.float32)
    return jnp.where(jnp.abs(gap) <= 6.0, jnp.exp(-gap * gap / 18.0) / weight_total, 0.0)


def smooth_y(field):
    length = field.shape[-1]
    flat = field.reshape(-1, length)
    return jnp.dot(flat, y_matrix(length), precision=lax.Precision.HIGHEST).reshape(field.shape)


def diff_y(field):
    widths = [(0, 0)] * (field.ndim - 1) + [(1, 1)]
    padded = jnp.pad(field, widths)
    return (padded[..., 2:] - padded[..., :-2]) * 0.5


def return_map(
    velocity_x_spacing, velocity_z_spacing, dyv, stress_old, eta_ve, pres, cohesion_strength
):
    divv = velocity_x_spacing[0] + velocity_z_spacing[1] + dyv[2]
    pres = pres - 0.25 * divv
    strain = jnp.stack(
        [
            velocity_x_spacing[0] - divv / 3.0,
            velocity_z_spacing[1] - divv / 3.0,
            dyv[2] - divv / 3.0,
            0.5 * (velocity_x_spacing[1] + velocity_z_spacing[0]),
            0.5 * (velocity_x_spacing[2] + dyv[0]),
            0.5 * (velocity_z_spacing[2] + dyv[1]),
        ]
    )
    trial = 2.0 * eta_ve * (strain + stress_old / (2.0 * shear_time_increment))
    tau_ii = jnp.sqrt(
        0.5 * (trial[0] ** 2 + trial[1] ** 2 + trial[2] ** 2)
        + trial[3] ** 2
        + trial[4] ** 2
        + trial[5] ** 2
    )
    yield_f = tau_ii - 0.5 * jnp.maximum(pres, 0.0) - 0.8660254 * cohesion_strength
    dlam = jnp.maximum(yield_f, 0.0) / (eta_ve + 0.5)
    shrink = 1.0 - eta_ve * dlam / jnp.maximum(tau_ii, 0.5)
    return (pres, trial * shrink, shrink, yield_f, dlam)


def per_device(velocity, pressure, stress_old, plastic, viscosity, weak_seed):
    rows_x = plastic.shape[0]
    rows_z = plastic.shape[1]
    padded = padded_2(plastic, ((GX, 0),), 6)
    along_x_direction = smooth_slices(padded, 0, rows_x)
    padded_z = padded_2(along_x_direction, ((GZ, 1),), 6)
    along_z = smooth_slices(padded_z, 1, rows_z)
    smoothed = smooth_y(along_z)
    eta_ve = 1.0 / (1.0 / viscosity + 1.0 / shear_time_increment)
    seeded = weak_seed.astype(jnp.float32)
    cohesion_strength = (1.0 - 0.6 * seeded) / (1.0 + 2.0 * smoothed)
    pres = pressure
    plastic_sum = plastic
    peaks = []
    tau = stress_old
    for step_index in range(ITERS):
        velocity_padded = with_halo(velocity, ((GX, 1), (GZ, 2)), 1)
        velocity_x_spacing = (velocity_padded[:, 2:, 1:-1] - velocity_padded[:, :-2, 1:-1]) * 0.5
        velocity_z_spacing = (velocity_padded[:, 1:-1, 2:] - velocity_padded[:, 1:-1, :-2]) * 0.5
        dyv = diff_y(velocity)
        pres, tau, shrink, yield_f, dlam = return_map(
            velocity_x_spacing, velocity_z_spacing, dyv, stress_old, eta_ve, pres, cohesion_strength
        )
        plastic_sum = plastic_sum + dlam
        maximum_yield_stress, peak_eta = (
            one_axis_at_a_time(jnp.max(yield_f), GX_GZ),
            one_axis_at_a_time(jnp.max(eta_ve * shrink), GX_GZ),
        )
        peaks.append(maximum_yield_stress)
        step = 0.125 / peak_eta
        sxx = tau[0] - pres
        szz = tau[1] - pres
        syy = tau[2] - pres
        xpad = padded_2(jnp.stack([sxx, tau[4], tau[3]]), ((GX, 1),), 1)
        dxs = (xpad[:, 2:] - xpad[:, :-2]) * 0.5
        zpad = padded_2(jnp.stack([tau[3], tau[5], szz]), ((GZ, 2),), 1)
        dzs = (zpad[:, :, 2:] - zpad[:, :, :-2]) * 0.5
        dys = diff_y(jnp.stack([tau[4], tau[5], syy]))
        rx = dxs[0] + dzs[0] + dys[0]
        rz = dxs[2] + dzs[2] + dys[1]
        ry = dxs[1] + dzs[1] + dys[2]
        velocity = velocity + step * jnp.stack([rx, rz, ry])
    return (velocity, pres, tau, plastic_sum, jnp.stack(peaks))


def solution(mesh):
    split = Mesh(mesh.devices.reshape(4, 8, 2, 4, 2), ("gx_0", "gx_1", "gx_2", "gz_0", "gz_1"))
    return jax.shard_map(
        per_device,
        mesh=split,
        in_specs=(
            P(None, GX, GZ, None),
            P(GX, GZ, None),
            P(None, GX, GZ, None),
            P(GX, GZ, None),
            P(GX, GZ, None),
            P(GX, GZ, None),
        ),
        out_specs=(
            P(None, GX, GZ, None),
            P(GX, GZ, None),
            P(None, GX, GZ, None),
            P(GX, GZ, None),
            P(),
        ),
        check_vma=False,
    )
```

profile of v0, /device:TPU:1, one launch (start us, length us, event | category | flops | bytes accessed | tf_op | source)
XLA Modules:
  0.0 195.1 jit_solution(11376816298680893446)
XLA Ops:
  2.7 4.7 %collective-permute-start.1 = (f32[3,1,8,256]{3,2,1,0:T(8,128)S(1)}, f32[3,1,8,256]{3,2,1,0:T(8,128)S(1)}, u32[]{:S(2)}, u32[]{:S(2)}) collective-permute-start(f32[3,1,8,256]{3,2,1,0:T(8,128)S(1)} %get-tuple-element.75), channel_id=1, source_target_pairs={{0,8},{8,16},{16,24},{24,32},{32,40},{40,48},{48,56},{56,64},{64,7... | collective-permute-start | bytes 73736 | tf_op jit(solution)/shard_map/ppermute | solution.py:42
  8.2 4.2 %collective-permute-start.4 = (f32[6,8,256]{2,1,0:T(8,128)S(1)}, f32[6,8,256]{2,1,0:T(8,128)S(1)}, u32[]{:S(2)}, u32[]{:S(2)}) collective-permute-start(f32[6,8,256]{2,1,0:T(8,128)S(1)} %get-tuple-element.85), channel_id=1, source_target_pairs={{0,8},{8,16},{16,24},{24,32},{32,40},{40,48},{48,56},{56,64},{64,7... | collective-permute-start | bytes 147464 | tf_op jit(solution)/shard_map/ppermute | solution.py:26
  15.0 6.3 %collective-permute-start.2 = (f32[3,16,1,256]{3,2,1,0:T(1,128)S(1)}, f32[3,16,1,256]{3,2,1,0:T(1,128)S(1)}, u32[]{:S(2)}, u32[]{:S(2)}) collective-permute-start(f32[3,16,1,256]{3,2,1,0:T(1,128)S(1)} %get-tuple-element.69), channel_id=1, source_target_pairs={{1,0},{2,1},{3,2},{4,3},{5,4},{6,5},{7,6},{9,8},{10,9},{11,10},{12... | collective-permute-start | bytes 147464 | tf_op jit(solution)/shard_map/ppermute | solution.py:43
  27.6 2.4 %collective-permute-start.7 = (f32[16,6,256]{2,1,0:T(8,128)S(1)}, f32[16,6,256]{2,1,0:T(8,128)S(1)}, u32[]{:S(2)}, u32[]{:S(2)}) collective-permute-start(f32[16,6,256]{2,1,0:T(8,128)S(1)} %get-tuple-element.82), channel_id=1, source_target_pairs={{1,0},{2,1},{3,2},{4,3},{5,4},{6,5},{7,6},{9,8},{10,9},{11,10},{12... | collective-permute-start | bytes 294920 | tf_op jit(solution)/shard_map/ppermute | solution.py:29
  31.6 3.2 %collective-permute-done.7 = f32[16,6,256]{2,1,0:T(8,128)S(1)} collective-permute-done((f32[16,6,256]{2,1,0:T(8,128)S(1)}, f32[16,6,256]{2,1,0:T(8,128)S(1)}, u32[]{:S(2)}, u32[]{:S(2)}) %collective-permute-start.7) | collective-permute-done | bytes 98336 | tf_op jit(solution)/shard_map/ppermute | solution.py:29
  37.2 20.3 %pmax.140 = f32[]{:T(128)} all-reduce(f32[]{:T(128)} %get-tuple-element.32), channel_id=1, replica_groups=mesh['gx_0'=4,'gx_1'=8,'gx_2'=2,'gz_0'=4,'gz_1'=2] {'gx_0'}, use_global_device_ids=true, to_apply=%region_1.2 | all-reduce | flops 1 | bytes 8 | tf_op jit(solution)/shard_map/pmax | solution.py:56
  57.5 11.3 %pmax.141 = f32[]{:T(128)} all-reduce(f32[]{:T(128)} %pmax.140), channel_id=1, replica_groups=mesh['gx_0'=4,'gx_1'=8,'gx_2'=2,'gz_0'=4,'gz_1'=2] {'gx_1'}, use_global_device_ids=true, to_apply=%region_2.3 | all-reduce | flops 1 | bytes 8 | tf_op jit(solution)/shard_map/pmax | solution.py:56
  68.8 4.4 %pmax.142 = f32[]{:T(128)} all-reduce(f32[]{:T(128)} %pmax.141), channel_id=1, replica_groups=mesh['gx_0'=4,'gx_1'=8,'gx_2'=2,'gz_0'=4,'gz_1'=2] {'gx_2'}, use_global_device_ids=true, to_apply=%region_3.4 | all-reduce | flops 1 | bytes 8 | tf_op jit(solution)/shard_map/pmax | solution.py:56
  73.4 11.4 %pmax.143 = f32[]{:T(128)} all-reduce(f32[]{:T(128)} %pmax.142), channel_id=1, replica_groups=mesh['gx_0'=4,'gx_1'=8,'gx_2'=2,'gz_0'=4,'gz_1'=2] {'gz_0'}, use_global_device_ids=true, to_apply=%region_4.5 | all-reduce | flops 1 | bytes 8 | tf_op jit(solution)/shard_map/pmax | solution.py:56
  86.2 4.0 %collective-permute-start.9 = (f32[3,1,8,256]{3,2,1,0:T(8,128)S(1)}, f32[3,1,8,256]{3,2,1,0:T(8,128)S(1)}, u32[]{:S(2)}, u32[]{:S(2)}) collective-permute-start(f32[3,1,8,256]{3,2,1,0:T(8,128)S(1)} %get-tuple-element.66), channel_id=1, source_target_pairs={{0,8},{8,16},{16,24},{24,32},{32,40},{40,48},{48,56},{56,64},{64,7... | collective-permute-start | bytes 73736 | tf_op jit(solution)/shard_map/ppermute | solution.py:26
  90.3 8.3 %collective-permute-start.10 = (f32[3,16,1,256]{3,2,1,0:T(1,128)S(1)}, f32[3,16,1,256]{3,2,1,0:T(1,128)S(1)}, u32[]{:S(2)}, u32[]{:S(2)}) collective-permute-start(f32[3,16,1,256]{3,2,1,0:T(1,128)S(1)} %get-tuple-element.67), channel_id=1, source_target_pairs={{1,0},{2,1},{3,2},{4,3},{5,4},{6,5},{7,6},{9,8},{10,9},{11,10},{12... | collective-permute-start | bytes 147464 | tf_op jit(solution)/shard_map/ppermute | solution.py:29
  98.6 3.6 %collective-permute-start.11 = (f32[3,16,1,256]{3,2,1,0:T(1,128)S(1)}, f32[3,16,1,256]{3,2,1,0:T(1,128)}, u32[]{:S(2)}, u32[]{:S(2)}) collective-permute-start(f32[3,16,1,256]{3,2,1,0:T(1,128)S(1)} %get-tuple-element.68), channel_id=1, source_target_pairs={{0,1},{1,2},{2,3},{3,4},{4,5},{5,6},{6,7},{8,9},{9,10},{10,11},{11... | collective-permute-start | bytes 147464 | tf_op jit(solution)/shard_map/ppermute | solution.py:26
  102.6 3.1 %pmax.144 = f32[]{:T(128)} all-reduce(f32[]{:T(128)} %pmax.143), channel_id=1, replica_groups=mesh['gx_0'=4,'gx_1'=8,'gx_2'=2,'gz_0'=4,'gz_1'=2] {'gz_1'}, use_global_device_ids=true, to_apply=%region_5.6 | all-reduce | flops 1 | bytes 8 | tf_op jit(solution)/shard_map/pmax | solution.py:56
  109.8 2.1 %collective-permute-start.14 = (f32[3,16,1,256]{3,2,1,0:T(1,128)S(1)}, f32[3,16,1,256]{3,2,1,0:T(1,128)S(1)}, u32[]{:S(2)}, u32[]{:S(2)}) collective-permute-start(f32[3,16,1,256]{3,2,1,0:T(1,128)S(1)} %get-tuple-element.61), channel_id=1, source_target_pairs={{1,0},{2,1},{3,2},{4,3},{5,4},{6,5},{7,6},{9,8},{10,9},{11,10},{12... | collective-permute-start | bytes 147464 | tf_op jit(solution)/shard_map/ppermute | solution.py:43
  111.8 4.4 %collective-permute-start.15 = (f32[3,16,1,256]{3,2,1,0:T(1,128)S(1)}, f32[3,16,1,256]{3,2,1,0:T(1,128)S(1)}, u32[]{:S(2)}, u32[]{:S(2)}) collective-permute-start(f32[3,16,1,256]{3,2,1,0:T(1,128)S(1)} %get-tuple-element.62), channel_id=1, source_target_pairs={{0,1},{1,2},{2,3},{3,4},{4,5},{5,6},{6,7},{8,9},{9,10},{10,11},{11... | collective-permute-start | bytes 147464 | tf_op jit(solution)/shard_map/ppermute | solution.py:42
  117.5 4.1 %collective-permute-start.13 = (f32[3,1,8,256]{3,2,1,0:T(8,128)S(1)}, f32[3,1,8,256]{3,2,1,0:T(8,128)S(1)}, u32[]{:S(2)}, u32[]{:S(2)}) collective-permute-start(f32[3,1,8,256]{3,2,1,0:T(8,128)S(1)} %get-tuple-element.64), channel_id=1, source_target_pairs={{0,8},{8,16},{16,24},{24,32},{32,40},{40,48},{48,56},{56,64},{64,7... | collective-permute-start | bytes 73736 | tf_op jit(solution)/shard_map/ppermute | solution.py:42
  128.1 4.9 %collective-permute-start.17 = (f32[3,1,8,256]{3,2,1,0:T(8,128)S(1)}, f32[3,1,8,256]{3,2,1,0:T(8,128)S(1)}, u32[]{:S(2)}, u32[]{:S(2)}) collective-permute-start(f32[3,1,8,256]{3,2,1,0:T(8,128)S(1)} %get-tuple-element.57), channel_id=1, source_target_pairs={{0,8},{8,16},{16,24},{24,32},{32,40},{40,48},{48,56},{56,64},{64,7... | collective-permute-start | bytes 73736 | tf_op jit(solution)/shard_map/ppermute | solution.py:26
  133.0 1.9 collective-permute-start.18
  135.0 4.5 %collective-permute-start.19 = (f32[3,16,1,256]{3,2,1,0:T(1,128)S(1)}, f32[3,16,1,256]{3,2,1,0:T(1,128)S(1)}, u32[]{:S(2)}, u32[]{:S(2)}) collective-permute-start(f32[3,16,1,256]{3,2,1,0:T(1,128)S(1)} %get-tuple-element.59), channel_id=1, source_target_pairs={{0,1},{1,2},{2,3},{3,4},{4,5},{5,6},{6,7},{8,9},{9,10},{10,11},{11... | collective-permute-start | bytes 147464 | tf_op jit(solution)/shard_map/ppermute | solution.py:26
  139.9 14.1 %all-reduce.10 = (f32[]{:T(128)}, f32[]{:T(128)}, f32[]{:T(128)}) all-reduce(f32[]{:T(128)} %get-tuple-element.28, f32[]{:T(128)} %get-tuple-element.76, f32[]{:T(128)} %get-tuple-element.24), channel_id=1, replica_groups=mesh['gx_0'=4,'gx_1'=8,'gx_2'=2,'gz_0'=4,'gz_1'=2] {'gx_0'}, use_global_device_ids=true, to_apply=%region_7.8 | all-reduce | flops 3 | bytes 24 | tf_op jit(solution)/shard_map/pmax | solution.py:56
  154.0 11.3 %all-reduce.8 = (f32[]{:T(128)}, f32[]{:T(128)}, f32[]{:T(128)}) all-reduce(f32[]{:T(128)} %get-tuple-element.11, f32[]{:T(128)} %get-tuple-element.12, f32[]{:T(128)} %get-tuple-element.13), channel_id=1, replica_groups=mesh['gx_0'=4,'gx_1'=8,'gx_2'=2,'gz_0'=4,'gz_1'=2] {'gx_1'}, use_global_device_ids=true, to_apply=%region_8.9 | all-reduce | flops 3 | bytes 24 | tf_op jit(solution)/shard_map/pmax | solution.py:56
  165.4 5.1 %all-reduce.12 = (f32[]{:T(128)}, f32[]{:T(128)}, f32[]{:T(128)}) all-reduce(f32[]{:T(128)} %get-tuple-element.5, f32[]{:T(128)} %get-tuple-element.6, f32[]{:T(128)} %get-tuple-element.7), channel_id=1, replica_groups=mesh['gx_0'=4,'gx_1'=8,'gx_2'=2,'gz_0'=4,'gz_1'=2] {'gx_2'}, use_global_device_ids=true, to_apply=%region_9.10 | all-reduce | flops 3 | bytes 24 | tf_op jit(solution)/shard_map/pmax | solution.py:56
  170.5 11.0 %all-reduce.9 = (f32[]{:T(128)}, f32[]{:T(128)}, f32[]{:T(128)}) all-reduce(f32[]{:T(128)} %get-tuple-element.17, f32[]{:T(128)} %get-tuple-element.18, f32[]{:T(128)} %get-tuple-element.19), channel_id=1, replica_groups=mesh['gx_0'=4,'gx_1'=8,'gx_2'=2,'gz_0'=4,'gz_1'=2] {'gz_0'}, use_global_device_ids=true, to_apply=%region_10.11 | all-reduce | flops 3 | bytes 24 | tf_op jit(solution)/shard_map/pmax | solution.py:56
  181.5 9.0 %all-reduce.11 = (f32[]{:T(128)}, f32[1]{0:T(128)}, f32[1]{0:T(128)}) all-reduce(f32[]{:T(128)} %get-tuple-element.8, f32[1]{0:T(128)} %bitcast.18, f32[1]{0:T(128)} %bitcast.17), channel_id=1, replica_groups=mesh['gx_0'=4,'gx_1'=8,'gx_2'=2,'gz_0'=4,'gz_1'=2] {'gz_1'}, use_global_device_ids=true, to_apply=%region_11.12 | all-reduce | flops 3 | bytes 24 | tf_op jit(solution)/shard_map/pmax | solution.py:56
  (124 shorter events, 32.6 us)
Async XLA Ops:
  0.6 23.6 %copy-start = (f32[3,16,8,256]{3,2,1,0:T(8,128)S(1)}, f32[3,16,8,256]{3,2,1,0:T(8,128)}, u32[]{:S(2)}) copy-start(f32[3,16,8,256]{3,2,1,0:T(8,128)} %param.6) | copy-start | bytes 1179652
  1.5 22.8 %collective-permute-start = (f32[3,1,8,256]{3,2,1,0:T(8,128)S(1)}, f32[3,1,8,256]{3,2,1,0:T(8,128)S(1)}, u32[]{:S(2)}, u32[]{:S(2)}) collective-permute-start(f32[3,1,8,256]{3,2,1,0:T(8,128)S(1)} %get-tuple-element.74), channel_id=1, source_target_pairs={{8,0},{16,8},{24,16},{32,24},{40,32},{48,40},{56,48},{64,56},{72,6... | collective-permute-start | bytes 73736 | tf_op jit(solution)/shard_map/ppermute | solution.py:43
  2.7 19.6 %collective-permute-start.1 = (f32[3,1,8,256]{3,2,1,0:T(8,128)S(1)}, f32[3,1,8,256]{3,2,1,0:T(8,128)S(1)}, u32[]{:S(2)}, u32[]{:S(2)}) collective-permute-start(f32[3,1,8,256]{3,2,1,0:T(8,128)S(1)} %get-tuple-element.75), channel_id=1, source_target_pairs={{0,8},{8,16},{16,24},{24,32},{32,40},{40,48},{48,56},{56,64},{64,7... | collective-permute-start | bytes 73736 | tf_op jit(solution)/shard_map/ppermute | solution.py:42
  8.2 16.3 %collective-permute-start.4 = (f32[6,8,256]{2,1,0:T(8,128)S(1)}, f32[6,8,256]{2,1,0:T(8,128)S(1)}, u32[]{:S(2)}, u32[]{:S(2)}) collective-permute-start(f32[6,8,256]{2,1,0:T(8,128)S(1)} %get-tuple-element.85), channel_id=1, source_target_pairs={{0,8},{8,16},{16,24},{24,32},{32,40},{40,48},{48,56},{56,64},{64,7... | collective-permute-start | bytes 147464 | tf_op jit(solution)/shard_map/ppermute | solution.py:26
  12.5 13.0 %collective-permute-start.5 = (f32[6,8,256]{2,1,0:T(8,128)S(1)}, f32[6,8,256]{2,1,0:T(8,128)S(1)}, u32[]{:S(2)}, u32[]{:S(2)}) collective-permute-start(f32[6,8,256]{2,1,0:T(8,128)S(1)} %get-tuple-element.86), channel_id=1, source_target_pairs={{8,0},{16,8},{24,16},{32,24},{40,32},{48,40},{56,48},{64,56},{72,6... | collective-permute-start | bytes 147464 | tf_op jit(solution)/shard_map/ppermute | solution.py:29
  15.0 15.0 %collective-permute-start.2 = (f32[3,16,1,256]{3,2,1,0:T(1,128)S(1)}, f32[3,16,1,256]{3,2,1,0:T(1,128)S(1)}, u32[]{:S(2)}, u32[]{:S(2)}) collective-permute-start(f32[3,16,1,256]{3,2,1,0:T(1,128)S(1)} %get-tuple-element.69), channel_id=1, source_target_pairs={{1,0},{2,1},{3,2},{4,3},{5,4},{6,5},{7,6},{9,8},{10,9},{11,10},{12... | collective-permute-start | bytes 147464 | tf_op jit(solution)/shard_map/ppermute | solution.py:43
  22.3 7.7 %collective-permute-start.3 = (f32[3,16,1,256]{3,2,1,0:T(1,128)S(1)}, f32[3,16,1,256]{3,2,1,0:T(1,128)S(1)}, u32[]{:S(2)}, u32[]{:S(2)}) collective-permute-start(f32[3,16,1,256]{3,2,1,0:T(1,128)S(1)} %get-tuple-element.70), channel_id=1, source_target_pairs={{0,1},{1,2},{2,3},{3,4},{4,5},{5,6},{6,7},{8,9},{9,10},{10,11},{11... | collective-permute-start | bytes 147464 | tf_op jit(solution)/shard_map/ppermute | solution.py:42
  25.7 5.9 %collective-permute-start.6 = (f32[16,6,256]{2,1,0:T(8,128)S(1)}, f32[16,6,256]{2,1,0:T(8,128)S(1)}, u32[]{:S(2)}, u32[]{:S(2)}) collective-permute-start(f32[16,6,256]{2,1,0:T(8,128)S(1)} %get-tuple-element.81), channel_id=1, source_target_pairs={{0,1},{1,2},{2,3},{3,4},{4,5},{5,6},{6,7},{8,9},{9,10},{10,11},{11... | collective-permute-start | bytes 294920 | tf_op jit(solution)/shard_map/ppermute | solution.py:26
  27.6 7.2 %collective-permute-start.7 = (f32[16,6,256]{2,1,0:T(8,128)S(1)}, f32[16,6,256]{2,1,0:T(8,128)S(1)}, u32[]{:S(2)}, u32[]{:S(2)}) collective-permute-start(f32[16,6,256]{2,1,0:T(8,128)S(1)} %get-tuple-element.82), channel_id=1, source_target_pairs={{1,0},{2,1},{3,2},{4,3},{5,4},{6,5},{7,6},{9,8},{10,9},{11,10},{12... | collective-permute-start | bytes 294920 | tf_op jit(solution)/shard_map/ppermute | solution.py:29
  73.4 16.9 %copy-start.10 = (f32[1,16,8,256]{3,2,1,0:T(8,128)}, f32[1,16,8,256]{3,2,1,0:T(8,128)S(1)}, u32[]{:S(2)}) copy-start(f32[1,16,8,256]{3,2,1,0:T(8,128)S(1)} %get-tuple-element.52) | copy-start | bytes 393220
  84.8 17.4 %slice-start.1 = ((f32[6,16,8,256]{3,2,1,0:T(8,128)}), f32[2,16,8,256]{3,2,1,0:T(8,128)S(1)}, s32[]{:S(2)}) async-start(f32[6,16,8,256]{3,2,1,0:T(8,128)} %copy-done.2), calls=%async_computation.1 | async-start | bytes 524288 | tf_op jit(solution)/shard_map/slice | solution.py:148
  84.8 21.6 %collective-permute-start.8 = (f32[3,1,8,256]{3,2,1,0:T(8,128)S(1)}, f32[3,1,8,256]{3,2,1,0:T(8,128)S(1)}, u32[]{:S(2)}, u32[]{:S(2)}) collective-permute-start(f32[3,1,8,256]{3,2,1,0:T(8,128)S(1)} %get-tuple-element.65), channel_id=1, source_target_pairs={{8,0},{16,8},{24,16},{32,24},{40,32},{48,40},{56,48},{64,56},{72,6... | collective-permute-start | bytes 73736 | tf_op jit(solution)/shard_map/ppermute | solution.py:29
  86.2 20.2 %collective-permute-start.9 = (f32[3,1,8,256]{3,2,1,0:T(8,128)S(1)}, f32[3,1,8,256]{3,2,1,0:T(8,128)S(1)}, u32[]{:S(2)}, u32[]{:S(2)}) collective-permute-start(f32[3,1,8,256]{3,2,1,0:T(8,128)S(1)} %get-tuple-element.66), channel_id=1, source_target_pairs={{0,8},{8,16},{16,24},{24,32},{32,40},{40,48},{48,56},{56,64},{64,7... | collective-permute-start | bytes 73736 | tf_op jit(solution)/shard_map/ppermute | solution.py:26
  90.3 16.2 %collective-permute-start.10 = (f32[3,16,1,256]{3,2,1,0:T(1,128)S(1)}, f32[3,16,1,256]{3,2,1,0:T(1,128)S(1)}, u32[]{:S(2)}, u32[]{:S(2)}) collective-permute-start(f32[3,16,1,256]{3,2,1,0:T(1,128)S(1)} %get-tuple-element.67), channel_id=1, source_target_pairs={{1,0},{2,1},{3,2},{4,3},{5,4},{6,5},{7,6},{9,8},{10,9},{11,10},{12... | collective-permute-start | bytes 147464 | tf_op jit(solution)/shard_map/ppermute | solution.py:29
  98.6 9.1 %collective-permute-start.11 = (f32[3,16,1,256]{3,2,1,0:T(1,128)S(1)}, f32[3,16,1,256]{3,2,1,0:T(1,128)}, u32[]{:S(2)}, u32[]{:S(2)}) collective-permute-start(f32[3,16,1,256]{3,2,1,0:T(1,128)S(1)} %get-tuple-element.68), channel_id=1, source_target_pairs={{0,1},{1,2},{2,3},{3,4},{4,5},{5,6},{6,7},{8,9},{9,10},{10,11},{11... | collective-permute-start | bytes 147464 | tf_op jit(solution)/shard_map/ppermute | solution.py:26
  109.8 12.8 %collective-permute-start.14 = (f32[3,16,1,256]{3,2,1,0:T(1,128)S(1)}, f32[3,16,1,256]{3,2,1,0:T(1,128)S(1)}, u32[]{:S(2)}, u32[]{:S(2)}) collective-permute-start(f32[3,16,1,256]{3,2,1,0:T(1,128)S(1)} %get-tuple-element.61), channel_id=1, source_target_pairs={{1,0},{2,1},{3,2},{4,3},{5,4},{6,5},{7,6},{9,8},{10,9},{11,10},{12... | collective-permute-start | bytes 147464 | tf_op jit(solution)/shard_map/ppermute | solution.py:43
  111.8 10.7 %collective-permute-start.15 = (f32[3,16,1,256]{3,2,1,0:T(1,128)S(1)}, f32[3,16,1,256]{3,2,1,0:T(1,128)S(1)}, u32[]{:S(2)}, u32[]{:S(2)}) collective-permute-start(f32[3,16,1,256]{3,2,1,0:T(1,128)S(1)} %get-tuple-element.62), channel_id=1, source_target_pairs={{0,1},{1,2},{2,3},{3,4},{4,5},{5,6},{6,7},{8,9},{9,10},{10,11},{11... | collective-permute-start | bytes 147464 | tf_op jit(solution)/shard_map/ppermute | solution.py:42
  116.2 5.4 %collective-permute-start.12 = (f32[3,1,8,256]{3,2,1,0:T(8,128)S(1)}, f32[3,1,8,256]{3,2,1,0:T(8,128)S(1)}, u32[]{:S(2)}, u32[]{:S(2)}) collective-permute-start(f32[3,1,8,256]{3,2,1,0:T(8,128)S(1)} %get-tuple-element.63), channel_id=1, source_target_pairs={{8,0},{16,8},{24,16},{32,24},{40,32},{48,40},{56,48},{64,56},{72,6... | collective-permute-start | bytes 73736 | tf_op jit(solution)/shard_map/ppermute | solution.py:43
  117.5 5.0 %collective-permute-start.13 = (f32[3,1,8,256]{3,2,1,0:T(8,128)S(1)}, f32[3,1,8,256]{3,2,1,0:T(8,128)S(1)}, u32[]{:S(2)}, u32[]{:S(2)}) collective-permute-start(f32[3,1,8,256]{3,2,1,0:T(8,128)S(1)} %get-tuple-element.64), channel_id=1, source_target_pairs={{0,8},{8,16},{16,24},{24,32},{32,40},{40,48},{48,56},{56,64},{64,7... | collective-permute-start | bytes 73736 | tf_op jit(solution)/shard_map/ppermute | solution.py:42
  126.6 12.9 %slice-start = ((f32[6,16,8,256]{3,2,1,0:T(8,128)}), f32[2,16,8,256]{3,2,1,0:T(8,128)S(1)}, s32[]{:S(2)}) async-start(f32[6,16,8,256]{3,2,1,0:T(8,128)} %copy-done.1), calls=%async_computation | async-start | bytes 524288 | tf_op jit(solution)/shard_map/slice | solution.py:148
  126.6 66.4 %collective-permute-start.16 = (f32[3,1,8,256]{3,2,1,0:T(8,128)S(1)}, f32[3,1,8,256]{3,2,1,0:T(8,128)S(1)}, u32[]{:S(2)}, u32[]{:S(2)}) collective-permute-start(f32[3,1,8,256]{3,2,1,0:T(8,128)S(1)} %get-tuple-element.56), channel_id=1, source_target_pairs={{8,0},{16,8},{24,16},{32,24},{40,32},{48,40},{56,48},{64,56},{72,6... | collective-permute-start | bytes 73736 | tf_op jit(solution)/shard_map/ppermute | solution.py:29
  128.1 65.0 %collective-permute-start.17 = (f32[3,1,8,256]{3,2,1,0:T(8,128)S(1)}, f32[3,1,8,256]{3,2,1,0:T(8,128)S(1)}, u32[]{:S(2)}, u32[]{:S(2)}) collective-permute-start(f32[3,1,8,256]{3,2,1,0:T(8,128)S(1)} %get-tuple-element.57), channel_id=1, source_target_pairs={{0,8},{8,16},{16,24},{24,32},{32,40},{40,48},{48,56},{56,64},{64,7... | collective-permute-start | bytes 73736 | tf_op jit(solution)/shard_map/ppermute | solution.py:26
  133.0 60.1 %collective-permute-start.18 = (f32[3,16,1,256]{3,2,1,0:T(1,128)S(1)}, f32[3,16,1,256]{3,2,1,0:T(1,128)S(1)}, u32[]{:S(2)}, u32[]{:S(2)}) collective-permute-start(f32[3,16,1,256]{3,2,1,0:T(1,128)S(1)} %get-tuple-element.58), channel_id=1, source_target_pairs={{1,0},{2,1},{3,2},{4,3},{5,4},{6,5},{7,6},{9,8},{10,9},{11,10},{12... | collective-permute-start | bytes 147464 | tf_op jit(solution)/shard_map/ppermute | solution.py:29
  135.0 58.1 %collective-permute-start.19 = (f32[3,16,1,256]{3,2,1,0:T(1,128)S(1)}, f32[3,16,1,256]{3,2,1,0:T(1,128)S(1)}, u32[]{:S(2)}, u32[]{:S(2)}) collective-permute-start(f32[3,16,1,256]{3,2,1,0:T(1,128)S(1)} %get-tuple-element.59), channel_id=1, source_target_pairs={{0,1},{1,2},{2,3},{3,4},{4,5},{5,6},{6,7},{8,9},{9,10},{10,11},{11... | collective-permute-start | bytes 147464 | tf_op jit(solution)/shard_map/ppermute | solution.py:26
  (17 other events, 30.2 us)
where the time goes:
time: 196 us; the launch traced here: 195 us
  blocking collectives  101 us (52%)
  starting transfers between devices  66 us (34%)
  other arithmetic  10.8 us (6%)
  local copies, waits for them, and re-layouts  9.46 us (5%)
  waiting for transfers between devices  4.17 us (2%)
  between operations  2.81 us (1%)
    pmax x10, blocking collectives, one_axis_at_a_time(): shard = lax.pmax(shard, axis)  101 us
    ppermute x6, starting transfers between devices, padded_2(): lax.ppermute(lax.slice_in_dim(block, block.shape[dim] - width, None, axis...  23.2 us
    ppermute x6, starting transfers between devices, padded_2(): lax.ppermute(lax.slice_in_dim(block, 0, width, axis=dim), axis, backward)  16.8 us
    ppermute x4, starting transfers between devices, with_halo(): lax.ppermute(last, axis, up)  15 us
    ppermute x4, starting transfers between devices, with_halo(): lax.ppermute(initial, axis, [(b, a) for a, b in up])  11 us
    unnamed x40, local copies, waits for them, and re-layouts  6.44 us
  transfers between devices with their start and end apart: 20, of which 2 were waited for; matrix products, arithmetic and copies ran while one was open for 3% of the time, Pallas kernels for 0%

commit v1 on v0

v1 whole, which is shorter than its diff:
```python
import math

import jax
import jax.numpy as jnp
from jax import lax
from jax.sharding import Mesh
from jax.sharding import PartitionSpec as P

ITERS = 2
GX = ("gx_0", "gx_1", "gx_2")
GZ = ("gz_0", "gz_1")
YCORE = ("gx_2", "gz_0", "gz_1")
XZ = ("gx_0", "gx_1")


unnormalized_weights = [math.exp(-(k * k) / 18.0) for k in range(-6, 7)]
weight_total = sum(unnormalized_weights)
gauss_weights = [value / weight_total for value in unnormalized_weights]
shear_time_increment = 20.0


def pairs(count, first):
    out = []
    for i in range(first, count - 1, 2):
        out += [(i, i + 1), (i + 1, i)]
    return out


def exchange(axis, first, last):
    count = lax.axis_size(axis)
    even = lax.axis_index(axis) % 2 == 0
    far = lax.ppermute(jnp.where(even, first, last), axis, pairs(count, 1))
    near = lax.ppermute(jnp.where(even, last, first), axis, pairs(count, 0))
    return jnp.where(even, far, near), jnp.where(even, near, far)


def global_max(a, b):
    row = jnp.where(jnp.arange(128) == 0, a, b)
    for axes in (YCORE, XZ):
        count = lax.axis_size(axes)
        sent = jnp.broadcast_to(row, (count, 1, 128))
        row = jnp.max(lax.all_to_all(sent, axes, 0, 0, tiled=True), axis=(0, 1))
    return row[0], row[1]


def smooth_slices(padded, axis, count):
    total = gauss_weights[0] * lax.slice_in_dim(padded, 0, count, axis=axis)
    for index in range(1, 13):
        total = total + gauss_weights[index] * lax.slice_in_dim(
            padded, index, index + count, axis=axis
        )
    return total


def y_matrix(length):
    places = jnp.arange(length)
    gap = (places[:, None] - places[None, :]).astype(jnp.float32)
    return jnp.where(jnp.abs(gap) <= 6.0, jnp.exp(-gap * gap / 18.0) / weight_total, 0.0)


def smooth_y(field):
    length = field.shape[-1]
    flat = field.reshape(-1, length)
    return jnp.dot(flat, y_matrix(length), precision=lax.Precision.HIGHEST).reshape(field.shape)


def diff_y(field):
    widths = [(0, 0)] * (field.ndim - 1) + [(1, 1)]
    padded = jnp.pad(field, widths)
    return (padded[..., 2:] - padded[..., :-2]) * 0.5


def diff(field, halo, dim):
    low, high = halo
    padded = jnp.concatenate([low, field, high], axis=dim)
    count = field.shape[dim]
    return (
        lax.slice_in_dim(padded, 2, count + 2, axis=dim)
        - lax.slice_in_dim(padded, 0, count, axis=dim)
    ) * 0.5


def edges(field, dim, width):
    count = field.shape[dim]
    return (
        lax.slice_in_dim(field, 0, width, axis=dim),
        lax.slice_in_dim(field, count - width, count, axis=dim),
    )


def return_map(dxv, dzv, dyv, stress_old, eta_ve, pres, cohesion_strength):
    divv = dxv[0] + dzv[1] + dyv[2]
    pres = pres - 0.25 * divv
    strain = jnp.stack(
        [
            dxv[0] - divv / 3.0,
            dzv[1] - divv / 3.0,
            dyv[2] - divv / 3.0,
            0.5 * (dxv[1] + dzv[0]),
            0.5 * (dxv[2] + dyv[0]),
            0.5 * (dzv[2] + dyv[1]),
        ]
    )
    trial = 2.0 * eta_ve * (strain + stress_old / (2.0 * shear_time_increment))
    tau_ii = jnp.sqrt(
        0.5 * (trial[0] ** 2 + trial[1] ** 2 + trial[2] ** 2)
        + trial[3] ** 2
        + trial[4] ** 2
        + trial[5] ** 2
    )
    yield_f = tau_ii - 0.5 * jnp.maximum(pres, 0.0) - 0.8660254 * cohesion_strength
    dlam = jnp.maximum(yield_f, 0.0) / (eta_ve + 0.5)
    shrink = 1.0 - eta_ve * dlam / jnp.maximum(tau_ii, 0.5)
    return (pres, trial * shrink, shrink, yield_f, dlam)


def per_device(velocity, pressure, stress_old, plastic, viscosity, weak_seed):
    rows_x, rows_z, length = plastic.shape
    v_first, v_last = edges(velocity, 1, 1)
    p_first, p_last = edges(plastic, 0, 6)
    x_low, x_high = exchange(
        GX,
        jnp.concatenate([v_first[:, 0], p_first]),
        jnp.concatenate([v_last[:, 0], p_last]),
    )
    v_x = (x_low[:3][:, None], x_high[:3][:, None])
    along_x = smooth_slices(jnp.concatenate([x_low[3:], plastic, x_high[3:]]), 0, rows_x)
    v_first, v_last = edges(velocity, 2, 1)
    p_first, p_last = edges(along_x, 1, 6)
    z_low, z_high = exchange(
        GZ,
        jnp.concatenate([v_first[:, :, 0], jnp.swapaxes(p_first, 0, 1)]),
        jnp.concatenate([v_last[:, :, 0], jnp.swapaxes(p_last, 0, 1)]),
    )
    v_z = (z_low[:3][:, :, None], z_high[:3][:, :, None])
    along_z = smooth_slices(
        jnp.concatenate(
            [jnp.swapaxes(z_low[3:], 0, 1), along_x, jnp.swapaxes(z_high[3:], 0, 1)], axis=1
        ),
        1,
        rows_z,
    )
    smoothed = smooth_y(along_z)
    eta_ve = 1.0 / (1.0 / viscosity + 1.0 / shear_time_increment)
    seeded = weak_seed.astype(jnp.float32)
    cohesion_strength = (1.0 - 0.6 * seeded) / (1.0 + 2.0 * smoothed)
    pres = pressure
    plastic_sum = plastic
    peaks = []
    dxv = diff(velocity, v_x, 1)
    dzv = diff(velocity, v_z, 2)
    dyv = diff_y(velocity)
    for step_index in range(ITERS):
        pres, tau, shrink, yield_f, dlam = return_map(
            dxv, dzv, dyv, stress_old, eta_ve, pres, cohesion_strength
        )
        plastic_sum = plastic_sum + dlam
        sxx = tau[0] - pres
        szz = tau[1] - pres
        syy = tau[2] - pres
        xs = jnp.stack([sxx, tau[3], tau[4]])
        zs = jnp.stack([tau[3], szz, tau[5]])
        ys = jnp.stack([tau[4], tau[5], syy])
        x_low, x_high = exchange(GX, *[e[:, 0] for e in edges(xs, 1, 1)])
        z_low, z_high = exchange(GZ, *[e[:, :, 0] for e in edges(zs, 2, 1)])
        top_yield, peak_eta = global_max(jnp.max(yield_f), jnp.max(eta_ve * shrink))
        peaks.append(top_yield)
        step = 0.125 / peak_eta
        residual = (
            diff(xs, (x_low[:, None], x_high[:, None]), 1)
            + diff(zs, (z_low[:, :, None], z_high[:, :, None]), 2)
            + diff_y(ys)
        )
        if step_index + 1 < ITERS:
            x_low, x_high = exchange(GX, *[e[:, 0] for e in edges(residual, 1, 1)])
            z_low, z_high = exchange(GZ, *[e[:, :, 0] for e in edges(residual, 2, 1)])
            dxv = dxv + step * diff(residual, (x_low[:, None], x_high[:, None]), 1)
            dzv = dzv + step * diff(residual, (z_low[:, :, None], z_high[:, :, None]), 2)
            dyv = dyv + step * diff_y(residual)
        velocity = velocity + step * residual
    return (velocity, pres, tau, plastic_sum, jnp.stack(peaks))


def solution(mesh):
    split = Mesh(mesh.devices.reshape(4, 8, 2, 4, 2), ("gx_0", "gx_1", "gx_2", "gz_0", "gz_1"))
    return jax.shard_map(
        per_device,
        mesh=split,
        in_specs=(
            P(None, GX, GZ, None),
            P(GX, GZ, None),
            P(None, GX, GZ, None),
            P(GX, GZ, None),
            P(GX, GZ, None),
            P(GX, GZ, None),
        ),
        out_specs=(
            P(None, GX, GZ, None),
            P(GX, GZ, None),
            P(None, GX, GZ, None),
            P(GX, GZ, None),
            P(),
        ),
        check_vma=False,
    )
```

time: 196 us -> 144 us (0.73)
  blocking collectives: 101 us -> 0 us
  starting transfers between devices: 66 us -> 88.2 us
  waiting for transfers between devices: 4.17 us -> 23.6 us
  other arithmetic: 10.8 us -> 16.1 us
  local copies, waits for them, and re-layouts: 9.46 us -> 11.6 us
    pmax x10 -> x0, blocking collectives: 101 us -> none  [one_axis_at_a_time(): shard = lax.pmax(shard, axis)]
    all_to_all x0 -> x4, starting transfers between devices: none -> 34.6 us  [global_max(): row = jnp.max(lax.all_to_all(sent, axes, 0, 0, tiled=True), axis=(0, 1))]
    all_to_all x0 -> x4, waiting for transfers between devices: none -> 16.4 us  [global_max(): row = jnp.max(lax.all_to_all(sent, axes, 0, 0, tiled=True), axis=(0, 1))]
    ppermute x20 -> x16, starting transfers between devices: 66 us -> 53.6 us  [the longest x8 30.1 us: exchange(): near = lax.ppermute(jnp.where(even, last, first), axis, pairs(count, 0))]
    select_n x0 -> x15, other arithmetic: none -> 3.36 us  [the longest x2 2.53 us: global_max(): row = jnp.where(jnp.arange(128) == 0, a, b)]
    ppermute x20 -> x16, waiting for transfers between devices: 4.17 us -> 7.21 us  [the longest x8 4.16 us: exchange(): far = lax.ppermute(jnp.where(even, first, last), axis, pairs(count, 1))]
    broadcast_in_dim x0 -> x17, local copies, waits for them, and re-layouts: none -> 2.87 us  [the longest x4 2.45 us: global_max(): sent = jnp.broadcast_to(row, (count, 1, 128))]
    unnamed x40 -> x51, local copies, waits for them, and re-layouts: 6.44 us -> 4.95 us
  transfers between devices with their start and end apart: 20 -> 20, of which waited for: 2 -> 5; matrix products, arithmetic and copies ran while one was open for 3% -> 5% of each run, Pallas kernels for 0% -> 0%
where the time goes in v1:
time: 144 us; the launch traced here: 143 us
  starting transfers between devices  88.2 us (61%)
  waiting for transfers between devices  23.6 us (16%)
  other arithmetic  16.1 us (11%)
  local copies, waits for them, and re-layouts  11.6 us (8%)
  between operations  3.11 us (2%)
    all_to_all x4, starting transfers between devices, global_max(): row = jnp.max(lax.all_to_all(sent, axes, 0, 0, tiled=True), axis=(0, 1))  34.6 us
    ppermute x8, starting transfers between devices, exchange(): near = lax.ppermute(jnp.where(even, last, first), axis, pairs(count, 0))  30.1 us
    ppermute x8, starting transfers between devices, exchange(): far = lax.ppermute(jnp.where(even, first, last), axis, pairs(count, 1))  23.6 us
    all_to_all x4, waiting for transfers between devices, global_max(): row = jnp.max(lax.all_to_all(sent, axes, 0, 0, tiled=True), axis=(0, 1))  16.4 us
    unnamed x51, local copies, waits for them, and re-layouts  4.95 us
    ppermute x8, waiting for transfers between devices, exchange(): far = lax.ppermute(jnp.where(even, first, last), axis, pairs(count, 1))  4.16 us
    ppermute x8, waiting for transfers between devices, exchange(): near = lax.ppermute(jnp.where(even, last, first), axis, pairs(count, 0))  3.05 us
  transfers between devices with their start and end apart: 20, of which 5 were waited for; matrix products, arithmetic and copies ran while one was open for 5% of the time, Pallas kernels for 0%

profile of v1, /device:TPU:1, one launch (start us, length us, event | category | flops | bytes accessed | tf_op | source)
XLA Modules:
  0.0 143.1 jit_solution(5380965201959318951)
XLA Ops:
  2.5 7.3 %collective-permute-start = (f32[9,8,256]{2,0,1:T(8,128)S(1)}, f32[9,8,256]{2,0,1:T(8,128)S(1)}, u32[]{:S(2)}, u32[]{:S(2)}) collective-permute-start(f32[9,8,256]{2,0,1:T(8,128)S(1)} %get-tuple-element.68), channel_id=1, source_target_pairs={{0,8},{8,0},{16,24},{24,16},{32,40},{40,32},{48,56},{56,48},{64,72... | collective-permute-start | bytes 221192 | tf_op jit(solution)/shard_map/ppermute | solution.py:33
  10.0 3.0 %collective-permute-done = f32[9,8,256]{2,0,1:T(8,128)S(1)} collective-permute-done((f32[9,8,256]{2,0,1:T(8,128)S(1)}, f32[9,8,256]{2,0,1:T(8,128)S(1)}, u32[]{:S(2)}, u32[]{:S(2)}) %collective-permute-start) | collective-permute-done | bytes 73760 | tf_op jit(solution)/shard_map/ppermute | solution.py:33
  13.5 6.2 %collective-permute-start.3 = (f32[9,16,256]{2,1,0:T(8,128)S(1)}, f32[9,16,256]{2,1,0:T(8,128)S(1)}, u32[]{:S(2)}, u32[]{:S(2)}) collective-permute-start(f32[9,16,256]{2,1,0:T(8,128)S(1)} %get-tuple-element.63), channel_id=1, source_target_pairs={{1,2},{2,1},{3,4},{4,3},{5,6},{6,5},{9,10},{10,9},{11,12},{12,11},... | collective-permute-start | bytes 442376 | tf_op jit(solution)/shard_map/ppermute | solution.py:32
  19.7 1.9 %collective-permute-start.2 = (f32[9,16,256]{2,1,0:T(8,128)S(1)}, f32[9,16,256]{2,1,0:T(8,128)S(1)}, u32[]{:S(2)}, u32[]{:S(2)}) collective-permute-start(f32[9,16,256]{2,1,0:T(8,128)S(1)} %get-tuple-element.64), channel_id=1, source_target_pairs={{0,1},{1,0},{2,3},{3,2},{4,5},{5,4},{6,7},{7,6},{8,9},{9,8},{10,11... | collective-permute-start | bytes 442376 | tf_op jit(solution)/shard_map/ppermute | solution.py:33
  21.6 2.4 %collective-permute-done.3 = f32[9,16,256]{2,1,0:T(8,128)S(1)} collective-permute-done((f32[9,16,256]{2,1,0:T(8,128)S(1)}, f32[9,16,256]{2,1,0:T(8,128)S(1)}, u32[]{:S(2)}, u32[]{:S(2)}) %collective-permute-start.3) | collective-permute-done | bytes 147488 | tf_op jit(solution)/shard_map/ppermute | solution.py:32
  27.1 1.4 fusion.161
  30.7 1.3 compare_select_fusion.1
  32.6 8.2 %all-to-all-start = ((f32[16,1,128]{2,1,0:T(1,128)}), f32[16,1,128]{2,1,0:T(1,128)S(1)}, u32[]{:S(2)}, u32[]{:S(2)}) async-start(f32[16,1,128]{2,1,0:T(1,128)} %broadcast_in_dim.95), calls=%async_computation | async-start | bytes 16384 | tf_op jit(solution)/shard_map/all_to_all | solution.py:42
  43.7 5.9 %collective-permute-start.4 = (f32[3,8,256]{2,1,0:T(8,128)S(1)}, f32[3,8,256]{2,1,0:T(8,128)}, u32[]{:S(2)}, u32[]{:S(2)}) collective-permute-start(f32[3,8,256]{2,1,0:T(8,128)S(1)} %get-tuple-element.24), channel_id=1, source_target_pairs={{0,8},{8,0},{16,24},{24,16},{32,40},{40,32},{48,56},{56,48},{64,72... | collective-permute-start | bytes 73736 | tf_op jit(solution)/shard_map/ppermute | solution.py:33
  50.3 2.5 %collective-permute-start.6 = (f32[3,16,256]{2,1,0:T(8,128)}, f32[3,16,256]{2,1,0:T(8,128)}, u32[]{:S(2)}, u32[]{:S(2)}) collective-permute-start(f32[3,16,256]{2,1,0:T(8,128)} %get-tuple-element.84), channel_id=1, source_target_pairs={{0,1},{1,0},{2,3},{3,2},{4,5},{5,4},{6,7},{7,6},{8,9},{9,8},{10,11... | collective-permute-start | bytes 147464 | tf_op jit(solution)/shard_map/ppermute | solution.py:33
  52.8 4.3 %collective-permute-start.7 = (f32[3,16,256]{2,1,0:T(8,128)}, f32[3,16,256]{2,1,0:T(8,128)}, u32[]{:S(2)}, u32[]{:S(2)}) collective-permute-start(f32[3,16,256]{2,1,0:T(8,128)} %get-tuple-element.85), channel_id=1, source_target_pairs={{1,2},{2,1},{3,4},{4,3},{5,6},{6,5},{9,10},{10,9},{11,12},{12,11},... | collective-permute-start | bytes 147464 | tf_op jit(solution)/shard_map/ppermute | solution.py:32
  58.1 12.1 %all-to-all-start.1 = ((f32[32,1,128]{2,1,0:T(1,128)}), f32[32,1,128]{2,1,0:T(1,128)S(1)}, u32[]{:S(2)}, u32[]{:S(2)}) async-start(f32[32,1,128]{2,1,0:T(1,128)} %broadcast_in_dim.96), calls=%async_computation.1 | async-start | bytes 32768 | tf_op jit(solution)/shard_map/all_to_all | solution.py:42
  70.9 7.8 %all-to-all-done.1 = f32[32,1,128]{2,1,0:T(1,128)S(1)} async-done(((f32[32,1,128]{2,1,0:T(1,128)}), f32[32,1,128]{2,1,0:T(1,128)S(1)}, u32[]{:S(2)}, u32[]{:S(2)}) %all-to-all-start.1) | async-done | bytes 16416 | tf_op jit(solution)/shard_map/all_to_all | solution.py:42
  83.0 2.4 %collective-permute-start.8 = (f32[3,8,256]{2,1,0:T(8,128)S(1)}, f32[3,8,256]{2,1,0:T(8,128)S(1)}, u32[]{:S(2)}, u32[]{:S(2)}) collective-permute-start(f32[3,8,256]{2,1,0:T(8,128)S(1)} %get-tuple-element.50), channel_id=1, source_target_pairs={{0,8},{8,0},{16,24},{24,16},{32,40},{40,32},{48,56},{56,48},{64,72... | collective-permute-start | bytes 73736 | tf_op jit(solution)/shard_map/ppermute | solution.py:33
  86.0 1.9 %collective-permute-start.10 = (f32[3,16,256]{2,1,0:T(8,128)S(1)}, f32[3,16,256]{2,1,0:T(8,128)S(1)}, u32[]{:S(2)}, u32[]{:S(2)}) collective-permute-start(f32[3,16,256]{2,1,0:T(8,128)S(1)} %get-tuple-element.80), channel_id=1, source_target_pairs={{0,1},{1,0},{2,3},{3,2},{4,5},{5,4},{6,7},{7,6},{8,9},{9,8},{10,11... | collective-permute-start | bytes 147464 | tf_op jit(solution)/shard_map/ppermute | solution.py:33
  87.9 5.2 %collective-permute-start.11 = (f32[3,16,256]{2,1,0:T(8,128)S(1)}, f32[3,16,256]{2,1,0:T(8,128)S(1)}, u32[]{:S(2)}, u32[]{:S(2)}) collective-permute-start(f32[3,16,256]{2,1,0:T(8,128)S(1)} %get-tuple-element.81), channel_id=1, source_target_pairs={{1,2},{2,1},{3,4},{4,3},{5,6},{6,5},{9,10},{10,9},{11,12},{12,11},... | collective-permute-start | bytes 147464 | tf_op jit(solution)/shard_map/ppermute | solution.py:32
  93.1 1.7 %collective-permute-done.11 = f32[3,16,256]{2,1,0:T(8,128)S(1)} collective-permute-done((f32[3,16,256]{2,1,0:T(8,128)S(1)}, f32[3,16,256]{2,1,0:T(8,128)S(1)}, u32[]{:S(2)}, u32[]{:S(2)}) %collective-permute-start.11) | collective-permute-done | bytes 49184 | tf_op jit(solution)/shard_map/ppermute | solution.py:32
  101.1 9.5 %all-to-all-start.2 = ((f32[16,1,128]{2,1,0:T(1,128)}), f32[16,1,128]{2,1,0:T(1,128)S(1)}, u32[]{:S(2)}, u32[]{:S(2)}) async-start(f32[16,1,128]{2,1,0:T(1,128)} %broadcast_in_dim.107), calls=%async_computation.2 | async-start | bytes 16384 | tf_op jit(solution)/shard_map/all_to_all | solution.py:42
  110.8 2.0 %collective-permute-start.14 = (f32[3,16,256]{2,1,0:T(8,128)S(1)}, f32[3,16,256]{2,1,0:T(8,128)S(1)}, u32[]{:S(2)}, u32[]{:S(2)}) collective-permute-start(f32[3,16,256]{2,1,0:T(8,128)S(1)} %get-tuple-element.76), channel_id=1, source_target_pairs={{0,1},{1,0},{2,3},{3,2},{4,5},{5,4},{6,7},{7,6},{8,9},{9,8},{10,11... | collective-permute-start | bytes 147464 | tf_op jit(solution)/shard_map/ppermute | solution.py:33
  112.8 4.5 %collective-permute-start.15 = (f32[3,16,256]{2,1,0:T(8,128)S(1)}, f32[3,16,256]{2,1,0:T(8,128)S(1)}, u32[]{:S(2)}, u32[]{:S(2)}) collective-permute-start(f32[3,16,256]{2,1,0:T(8,128)S(1)} %get-tuple-element.77), channel_id=1, source_target_pairs={{1,2},{2,1},{3,4},{4,3},{5,6},{6,5},{9,10},{10,9},{11,12},{12,11},... | collective-permute-start | bytes 147464 | tf_op jit(solution)/shard_map/ppermute | solution.py:32
  118.0 6.2 %collective-permute-start.12 = (f32[3,8,256]{2,1,0:T(8,128)S(1)}, f32[3,8,256]{2,1,0:T(8,128)S(1)}, u32[]{:S(2)}, u32[]{:S(2)}) collective-permute-start(f32[3,8,256]{2,1,0:T(8,128)S(1)} %get-tuple-element.11), channel_id=1, source_target_pairs={{0,8},{8,0},{16,24},{24,16},{32,40},{40,32},{48,56},{56,48},{64,72... | collective-permute-start | bytes 73736 | tf_op jit(solution)/shard_map/ppermute | solution.py:33
  125.1 4.8 %all-to-all-start.3 = ((f32[32,1,128]{2,1,0:T(1,128)}), f32[32,1,128]{2,1,0:T(1,128)S(1)}, u32[]{:S(2)}, u32[]{:S(2)}) async-start(f32[32,1,128]{2,1,0:T(1,128)} %broadcast_in_dim.108), calls=%async_computation.3 | async-start | bytes 32768 | tf_op jit(solution)/shard_map/all_to_all | solution.py:42
  130.0 8.6 %all-to-all-done.3 = f32[32,1,128]{2,1,0:T(1,128)S(1)} async-done(((f32[32,1,128]{2,1,0:T(1,128)}), f32[32,1,128]{2,1,0:T(1,128)S(1)}, u32[]{:S(2)}, u32[]{:S(2)}) %all-to-all-start.3) | async-done | bytes 16416 | tf_op jit(solution)/shard_map/all_to_all | solution.py:42
  139.3 1.8 %pad_maximum_fusion.46 = f32[2]{0:T(128)} fusion(f32[1]{0:T(128)} %get-tuple-element.94, f32[1]{0:T(128)} %get-tuple-element.92), kind=kLoop, calls=%fused_computation.347 | loop fusion | flops 2 | bytes 16 | tf_op jit(solution)/shard_map/stack | solution.py:181
  (161 shorter events, 27.1 us)
Async XLA Ops:
  1.7 8.3 %collective-permute-start.1 = (f32[9,8,256]{2,0,1:T(8,128)S(1)}, f32[9,8,256]{2,0,1:T(8,128)S(1)}, u32[]{:S(2)}, u32[]{:S(2)}) collective-permute-start(f32[9,8,256]{2,0,1:T(8,128)S(1)} %get-tuple-element.67), channel_id=1, source_target_pairs={{8,16},{16,8},{24,32},{32,24},{40,48},{48,40},{56,64},{64,56},{72,... | collective-permute-start | bytes 221192 | tf_op jit(solution)/shard_map/ppermute | solution.py:32
  2.5 10.5 %collective-permute-start = (f32[9,8,256]{2,0,1:T(8,128)S(1)}, f32[9,8,256]{2,0,1:T(8,128)S(1)}, u32[]{:S(2)}, u32[]{:S(2)}) collective-permute-start(f32[9,8,256]{2,0,1:T(8,128)S(1)} %get-tuple-element.68), channel_id=1, source_target_pairs={{0,8},{8,0},{16,24},{24,16},{32,40},{40,32},{48,56},{56,48},{64,72... | collective-permute-start | bytes 221192 | tf_op jit(solution)/shard_map/ppermute | solution.py:33
  9.9 16.2 %copy-start.10 = (f32[16,8,256]{2,1,0:T(8,128)}, f32[16,8,256]{2,1,0:T(8,128)S(1)}, u32[]{:S(2)}) copy-start(f32[16,8,256]{2,1,0:T(8,128)S(1)} %broadcast_multiply_fusion.3) | copy-start | bytes 393220
  13.5 10.6 %collective-permute-start.3 = (f32[9,16,256]{2,1,0:T(8,128)S(1)}, f32[9,16,256]{2,1,0:T(8,128)S(1)}, u32[]{:S(2)}, u32[]{:S(2)}) collective-permute-start(f32[9,16,256]{2,1,0:T(8,128)S(1)} %get-tuple-element.63), channel_id=1, source_target_pairs={{1,2},{2,1},{3,4},{4,3},{5,6},{6,5},{9,10},{10,9},{11,12},{12,11},... | collective-permute-start | bytes 442376 | tf_op jit(solution)/shard_map/ppermute | solution.py:32
  19.7 4.4 %collective-permute-start.2 = (f32[9,16,256]{2,1,0:T(8,128)S(1)}, f32[9,16,256]{2,1,0:T(8,128)S(1)}, u32[]{:S(2)}, u32[]{:S(2)}) collective-permute-start(f32[9,16,256]{2,1,0:T(8,128)S(1)} %get-tuple-element.64), channel_id=1, source_target_pairs={{0,1},{1,0},{2,3},{3,2},{4,5},{5,4},{6,7},{7,6},{8,9},{9,8},{10,11... | collective-permute-start | bytes 442376 | tf_op jit(solution)/shard_map/ppermute | solution.py:33
  32.6 24.8 %all-to-all-start = ((f32[16,1,128]{2,1,0:T(1,128)}), f32[16,1,128]{2,1,0:T(1,128)S(1)}, u32[]{:S(2)}, u32[]{:S(2)}) async-start(f32[16,1,128]{2,1,0:T(1,128)} %broadcast_in_dim.95), calls=%async_computation | async-start | bytes 16384 | tf_op jit(solution)/shard_map/all_to_all | solution.py:42
  42.4 27.8 %collective-permute-start.5 = (f32[3,8,256]{2,1,0:T(8,128)S(1)}, f32[3,8,256]{2,1,0:T(8,128)}, u32[]{:S(2)}, u32[]{:S(2)}) collective-permute-start(f32[3,8,256]{2,1,0:T(8,128)S(1)} %select_bitcast_fusion.21), channel_id=1, source_target_pairs={{8,16},{16,8},{24,32},{32,24},{40,48},{48,40},{56,64},{64,56},{72,... | collective-permute-start | bytes 73736 | tf_op jit(solution)/shard_map/ppermute | solution.py:32
  43.7 26.5 %collective-permute-start.4 = (f32[3,8,256]{2,1,0:T(8,128)S(1)}, f32[3,8,256]{2,1,0:T(8,128)}, u32[]{:S(2)}, u32[]{:S(2)}) collective-permute-start(f32[3,8,256]{2,1,0:T(8,128)S(1)} %get-tuple-element.24), channel_id=1, source_target_pairs={{0,8},{8,0},{16,24},{24,16},{32,40},{40,32},{48,56},{56,48},{64,72... | collective-permute-start | bytes 73736 | tf_op jit(solution)/shard_map/ppermute | solution.py:33
  50.3 29.8 %collective-permute-start.6 = (f32[3,16,256]{2,1,0:T(8,128)}, f32[3,16,256]{2,1,0:T(8,128)}, u32[]{:S(2)}, u32[]{:S(2)}) collective-permute-start(f32[3,16,256]{2,1,0:T(8,128)} %get-tuple-element.84), channel_id=1, source_target_pairs={{0,1},{1,0},{2,3},{3,2},{4,5},{5,4},{6,7},{7,6},{8,9},{9,8},{10,11... | collective-permute-start | bytes 147464 | tf_op jit(solution)/shard_map/ppermute | solution.py:33
  52.8 27.2 %collective-permute-start.7 = (f32[3,16,256]{2,1,0:T(8,128)}, f32[3,16,256]{2,1,0:T(8,128)}, u32[]{:S(2)}, u32[]{:S(2)}) collective-permute-start(f32[3,16,256]{2,1,0:T(8,128)} %get-tuple-element.85), channel_id=1, source_target_pairs={{1,2},{2,1},{3,4},{4,3},{5,6},{6,5},{9,10},{10,9},{11,12},{12,11},... | collective-permute-start | bytes 147464 | tf_op jit(solution)/shard_map/ppermute | solution.py:32
  58.1 20.7 %all-to-all-start.1 = ((f32[32,1,128]{2,1,0:T(1,128)}), f32[32,1,128]{2,1,0:T(1,128)S(1)}, u32[]{:S(2)}, u32[]{:S(2)}) async-start(f32[32,1,128]{2,1,0:T(1,128)} %broadcast_in_dim.96), calls=%async_computation.1 | async-start | bytes 32768 | tf_op jit(solution)/shard_map/all_to_all | solution.py:42
  83.0 10.1 %collective-permute-start.8 = (f32[3,8,256]{2,1,0:T(8,128)S(1)}, f32[3,8,256]{2,1,0:T(8,128)S(1)}, u32[]{:S(2)}, u32[]{:S(2)}) collective-permute-start(f32[3,8,256]{2,1,0:T(8,128)S(1)} %get-tuple-element.50), channel_id=1, source_target_pairs={{0,8},{8,0},{16,24},{24,16},{32,40},{40,32},{48,56},{56,48},{64,72... | collective-permute-start | bytes 73736 | tf_op jit(solution)/shard_map/ppermute | solution.py:33
  85.3 7.8 %collective-permute-start.9 = (f32[3,8,256]{2,1,0:T(8,128)S(1)}, f32[3,8,256]{2,1,0:T(8,128)S(1)}, u32[]{:S(2)}, u32[]{:S(2)}) collective-permute-start(f32[3,8,256]{2,1,0:T(8,128)S(1)} %get-tuple-element.51), channel_id=1, source_target_pairs={{8,16},{16,8},{24,32},{32,24},{40,48},{48,40},{56,64},{64,56},{72,... | collective-permute-start | bytes 73736 | tf_op jit(solution)/shard_map/ppermute | solution.py:32
  86.0 7.1 %collective-permute-start.10 = (f32[3,16,256]{2,1,0:T(8,128)S(1)}, f32[3,16,256]{2,1,0:T(8,128)S(1)}, u32[]{:S(2)}, u32[]{:S(2)}) collective-permute-start(f32[3,16,256]{2,1,0:T(8,128)S(1)} %get-tuple-element.80), channel_id=1, source_target_pairs={{0,1},{1,0},{2,3},{3,2},{4,5},{5,4},{6,7},{7,6},{8,9},{9,8},{10,11... | collective-permute-start | bytes 147464 | tf_op jit(solution)/shard_map/ppermute | solution.py:33
  87.9 6.9 %collective-permute-start.11 = (f32[3,16,256]{2,1,0:T(8,128)S(1)}, f32[3,16,256]{2,1,0:T(8,128)S(1)}, u32[]{:S(2)}, u32[]{:S(2)}) collective-permute-start(f32[3,16,256]{2,1,0:T(8,128)S(1)} %get-tuple-element.81), channel_id=1, source_target_pairs={{1,2},{2,1},{3,4},{4,3},{5,6},{6,5},{9,10},{10,9},{11,12},{12,11},... | collective-permute-start | bytes 147464 | tf_op jit(solution)/shard_map/ppermute | solution.py:32
  98.4 12.3 %copy-start.20 = (f32[16,8,256]{2,1,0:T(8,128)}, f32[16,8,256]{2,1,0:T(8,128)S(1)}, u32[]{:S(2)}) copy-start(f32[16,8,256]{2,1,0:T(8,128)S(1)} %get-tuple-element.8) | copy-start | bytes 393220
  99.2 11.5 %copy-start = (f32[6,16,8,256]{3,2,1,0:T(8,128)}, f32[6,16,8,256]{3,2,1,0:T(8,128)S(1)}, u32[]{:S(2)}) copy-start(f32[6,16,8,256]{3,2,1,0:T(8,128)S(1)} %broadcast_multiply_fusion) | copy-start | bytes 2359300
  101.1 23.3 %all-to-all-start.2 = ((f32[16,1,128]{2,1,0:T(1,128)}), f32[16,1,128]{2,1,0:T(1,128)S(1)}, u32[]{:S(2)}, u32[]{:S(2)}) async-start(f32[16,1,128]{2,1,0:T(1,128)} %broadcast_in_dim.107), calls=%async_computation.2 | async-start | bytes 16384 | tf_op jit(solution)/shard_map/all_to_all | solution.py:42
  110.8 31.0 %collective-permute-start.14 = (f32[3,16,256]{2,1,0:T(8,128)S(1)}, f32[3,16,256]{2,1,0:T(8,128)S(1)}, u32[]{:S(2)}, u32[]{:S(2)}) collective-permute-start(f32[3,16,256]{2,1,0:T(8,128)S(1)} %get-tuple-element.76), channel_id=1, source_target_pairs={{0,1},{1,0},{2,3},{3,2},{4,5},{5,4},{6,7},{7,6},{8,9},{9,8},{10,11... | collective-permute-start | bytes 147464 | tf_op jit(solution)/shard_map/ppermute | solution.py:33
  112.8 29.0 %collective-permute-start.15 = (f32[3,16,256]{2,1,0:T(8,128)S(1)}, f32[3,16,256]{2,1,0:T(8,128)S(1)}, u32[]{:S(2)}, u32[]{:S(2)}) collective-permute-start(f32[3,16,256]{2,1,0:T(8,128)S(1)} %get-tuple-element.77), channel_id=1, source_target_pairs={{1,2},{2,1},{3,4},{4,3},{5,6},{6,5},{9,10},{10,9},{11,12},{12,11},... | collective-permute-start | bytes 147464 | tf_op jit(solution)/shard_map/ppermute | solution.py:32
  117.3 12.6 %collective-permute-start.13 = (f32[3,8,256]{2,1,0:T(8,128)S(1)}, f32[3,8,256]{2,1,0:T(8,128)S(1)}, u32[]{:S(2)}, u32[]{:S(2)}) collective-permute-start(f32[3,8,256]{2,1,0:T(8,128)S(1)} %select_bitcast_fusion.13), channel_id=1, source_target_pairs={{8,16},{16,8},{24,32},{32,24},{40,48},{48,40},{56,64},{64,56},{72,... | collective-permute-start | bytes 73736 | tf_op jit(solution)/shard_map/ppermute | solution.py:32
  118.0 11.9 %collective-permute-start.12 = (f32[3,8,256]{2,1,0:T(8,128)S(1)}, f32[3,8,256]{2,1,0:T(8,128)S(1)}, u32[]{:S(2)}, u32[]{:S(2)}) collective-permute-start(f32[3,8,256]{2,1,0:T(8,128)S(1)} %get-tuple-element.11), channel_id=1, source_target_pairs={{0,8},{8,0},{16,24},{24,16},{32,40},{40,32},{48,56},{56,48},{64,72... | collective-permute-start | bytes 73736 | tf_op jit(solution)/shard_map/ppermute | solution.py:33
  124.5 17.5 %copy-start.4 = (f32[3,16,8,256]{3,2,1,0:T(8,128)S(1)}, f32[3,16,8,256]{3,2,1,0:T(8,128)}, u32[]{:S(2)}) copy-start(f32[3,16,8,256]{3,2,1,0:T(8,128)} %get-tuple-element.23) | copy-start | bytes 1179652
  125.1 13.5 %all-to-all-start.3 = ((f32[32,1,128]{2,1,0:T(1,128)}), f32[32,1,128]{2,1,0:T(1,128)S(1)}, u32[]{:S(2)}, u32[]{:S(2)}) async-start(f32[32,1,128]{2,1,0:T(1,128)} %broadcast_in_dim.108), calls=%async_computation.3 | async-start | bytes 32768 | tf_op jit(solution)/shard_map/all_to_all | solution.py:42
  (21 other events, 61.3 us)

commit v2 on v1

v2 whole, which is shorter than its diff:
```python
import math

import jax
import jax.numpy as jnp
from jax import lax
from jax.experimental import pallas as pl
from jax.experimental.pallas import tpu as pltpu
from jax.sharding import Mesh
from jax.sharding import PartitionSpec as P

GX = ("gx_0", "gx_1", "gx_2")
GZ = ("gz_0", "gz_1")
YCORE = ("gx_2", "gz_0", "gz_1")
XZ = ("gx_0", "gx_1")

WEIGHT_TOTAL = sum(math.exp(-(k * k) / 18.0) for k in range(-6, 7))
WEIGHTS = [math.exp(-(k * k) / 18.0) / WEIGHT_TOTAL for k in range(-6, 7)]
SHEAR = 20.0
F32 = jnp.float32
LX, LZ, NY = 16, 8, 256
ROWS = LX * LZ
CHUNK = 16
XX, ZZ, YY, XZ_, XY, ZY = range(6)
ALONG_X = (XX, XZ_, XY)
ALONG_Z = (XZ_, ZZ, ZY)
ALONG_Y = (XY, ZY, YY)
VMEM = pl.BlockSpec(memory_space=pltpu.VMEM)
SMEM = pl.BlockSpec(memory_space=pltpu.SMEM)


def call(kernel, outs, operands, flops, scratch=(), out_specs=None):
    size = sum(math.prod(a.shape) * 4 for a in operands)
    size += sum(math.prod(s) * 4 for s in outs)
    return pl.pallas_call(
        kernel,
        out_shape=[jax.ShapeDtypeStruct(s, F32) for s in outs],
        in_specs=[VMEM] * len(operands),
        out_specs=out_specs or [VMEM] * len(outs),
        scratch_shapes=list(scratch),
        compiler_params=pltpu.CompilerParams(vmem_limit_bytes=14 * 1024 * 1024),
        cost_estimate=pl.CostEstimate(flops=flops, bytes_accessed=size, transcendentals=0),
    )(*operands)


def pairs(count, first):
    out = []
    for i in range(first, count - 1, 2):
        out += [(i, i + 1), (i + 1, i)]
    return out


def exchange(axis, far, near):
    count = lax.axis_size(axis)
    return (
        lax.ppermute(far, axis, pairs(count, 1)),
        lax.ppermute(near, axis, pairs(count, 0)),
    )


def spread(row, axes):
    return lax.all_to_all(row, axes, 0, 0, tiled=True)


def even_x():
    return lax.axis_index("gx_2") == 0


def even_z():
    return lax.axis_index("gz_1") == 0


def facing(even, first, last):
    return jnp.where(even, first, last), jnp.where(even, last, first)


def sides(even, far, near):
    return jnp.where(even, far, near), jnp.where(even, near, far)


def iotas():
    row = lax.broadcasted_iota(jnp.int32, (CHUNK, NY), 0) % LZ
    col = lax.broadcasted_iota(jnp.int32, (CHUNK, NY), 1)
    return row == 0, row == LZ - 1, col == 0, col == NY - 1


def below(ref, f, start, low):
    if start == 0:
        return jnp.concatenate([low, ref[f, 0 : CHUNK - LZ]], axis=0)
    return ref[f, start - LZ : start - LZ + CHUNK]


def above(ref, f, start, high):
    if start == ROWS - CHUNK:
        return jnp.concatenate([ref[f, start + LZ : ROWS], high], axis=0)
    return ref[f, start + LZ : start + LZ + CHUNK]


def diff_x(ref, f, start, low, high):
    return (above(ref, f, start, high) - below(ref, f, start, low)) * 0.5


def diff_z(value, low, high, masks):
    up = jnp.where(masks[1], high, pltpu.roll(value, CHUNK - 1, 0))
    down = jnp.where(masks[0], low, pltpu.roll(value, 1, 0))
    return (up - down) * 0.5


def diff_y(value, masks):
    up = jnp.where(masks[3], 0.0, pltpu.roll(value, NY - 1, 1))
    down = jnp.where(masks[2], 0.0, pltpu.roll(value, 1, 1))
    return (up - down) * 0.5


def spread_rows(face, f, low, high):
    for h in range(2):
        lanes = slice(h * 128, (h + 1) * 128)
        face[0, f, h, pl.ds(0, LX, stride=LZ), :] = low[:, lanes]
        face[1, f, h, pl.ds(LZ - 1, LX, stride=LZ), :] = high[:, lanes]


def face_rows(face, side, f, here):
    return jnp.concatenate([face[side, f, h, here] for h in range(2)], axis=1)


def keep(slots, f, value):
    for h in range(2):
        slots[f, h] = value[:, h * 128 : (h + 1) * 128]


def layer(slots, f, z):
    return jnp.concatenate([slots[f, h, pl.ds(z, LX, stride=LZ), :] for h in range(2)], axis=1)


def send_x(ref, fields, far, near):
    even = even_x()
    for i, f in enumerate(fields):
        a, b = facing(even, ref[f, 0:LZ], ref[f, ROWS - LZ : ROWS])
        far[i * LZ : (i + 1) * LZ] = a
        near[i * LZ : (i + 1) * LZ] = b


def send_z(ref, fields, far, near, slots):
    even = even_z()
    for i, f in enumerate(fields):
        keep(slots, i, ref[f])
        a, b = facing(even, layer(slots, i, 0), layer(slots, i, LZ - 1))
        far[i * LX : (i + 1) * LX] = a
        near[i * LX : (i + 1) * LX] = b


def store_row(out, top_yield, top_eta):
    a = jnp.max(top_yield, axis=(0, 1), keepdims=True)
    b = jnp.max(top_eta, axis=(0, 1), keepdims=True)
    lane = lax.broadcasted_iota(jnp.int32, (1, 128), 1)
    row = jnp.where(lane == 0, a, b)
    out[...] = jnp.broadcast_to(row[None], out.shape)


def relay_row(ref, out):
    out[...] = jnp.broadcast_to(jnp.max(ref[...], axis=0, keepdims=True), out.shape)


def row_values(ref):
    row = jnp.max(ref[...], axis=0)
    lane = lax.broadcasted_iota(jnp.int32, (1, 128), 1)
    top = jnp.max(jnp.where(lane == 0, row, -jnp.inf), axis=(0, 1), keepdims=True)
    eta = jnp.max(jnp.where(lane == 1, row, -jnp.inf), axis=(0, 1), keepdims=True)
    return top, eta


def return_map(dxv, dzv, dyv, old, eta, pres, cohesion):
    div = dxv[0] + dzv[1] + dyv[2]
    pres = pres - 0.25 * div
    third = div / 3.0
    strain = [
        dxv[0] - third,
        dzv[1] - third,
        dyv[2] - third,
        0.5 * (dxv[1] + dzv[0]),
        0.5 * (dxv[2] + dyv[0]),
        0.5 * (dzv[2] + dyv[1]),
    ]
    trial = [2.0 * eta * (e + o / (2.0 * SHEAR)) for e, o in zip(strain, old)]
    tau_ii = jnp.sqrt(
        0.5 * (trial[0] * trial[0] + trial[1] * trial[1] + trial[2] * trial[2])
        + trial[3] * trial[3]
        + trial[4] * trial[4]
        + trial[5] * trial[5]
    )
    yield_f = tau_ii - 0.5 * jnp.maximum(pres, 0.0) - 0.8660254 * cohesion
    dlam = jnp.maximum(yield_f, 0.0) / (eta + 0.5)
    shrink = 1.0 - eta * dlam / jnp.maximum(tau_ii, 0.5)
    return pres, [t * shrink for t in trial], eta * shrink, yield_f, dlam


def smooth_x_kernel(v, plastic, x_far, x_near, along, z_far, z_near, slots):
    even = even_x()
    low, high = sides(even, x_far[3 * LZ :], x_near[3 * LZ :])
    padded = jnp.concatenate([low, plastic[...], high], axis=0)
    total = WEIGHTS[0] * padded[0:ROWS]
    for k in range(1, 13):
        total = total + WEIGHTS[k] * padded[k * LZ : k * LZ + ROWS]
    along[...] = total
    keep(slots, 3, total)
    even = even_z()
    for i in range(9):
        if i < 3:
            keep(slots, i, v[i])
            a, b = facing(even, layer(slots, i, 0), layer(slots, i, LZ - 1))
        else:
            a, b = facing(even, layer(slots, 3, i - 3), layer(slots, 3, i - 1))
        z_far[i * LX : (i + 1) * LX] = a
        z_near[i * LX : (i + 1) * LX] = b


def gauss(gap, inside):
    g = gap.astype(F32)
    return jnp.where(inside & (jnp.abs(gap) <= 6), jnp.exp(g * g * (-1.0 / 18.0)) / WEIGHT_TOTAL, 0.0)


def dot(a, b):
    return jnp.dot(a, b, precision=lax.Precision.HIGHEST, preferred_element_type=F32)


def first_kernel(
    v, pressure, old, along, plastic, viscosity, seed, x_far, x_near, z_far, z_near,
    held, pres, total, eta_out, cohesion_out, row_out, sx_far, sx_near, sz_far, sz_near,
    face, slots,
):
    low, high = sides(even_z(), z_far[...], z_near[...])
    r = lax.broadcasted_iota(jnp.int32, (ROWS, ROWS), 0)
    c = lax.broadcasted_iota(jnp.int32, (ROWS, ROWS), 1)
    own = gauss(c % LZ - r % LZ, c // LZ == r // LZ)
    r = lax.broadcasted_iota(jnp.int32, (ROWS, 6 * LX), 0)
    c = lax.broadcasted_iota(jnp.int32, (ROWS, 6 * LX), 1)
    same = c % LX == r // LZ
    from_low = gauss(c // LX - 6 - r % LZ, same)
    from_high = gauss(c // LX + LZ - r % LZ, same)
    along_z = dot(own, along[...]) + dot(from_low, low[3 * LX :]) + dot(from_high, high[3 * LX :])
    r = lax.broadcasted_iota(jnp.int32, (NY, NY), 0)
    c = lax.broadcasted_iota(jnp.int32, (NY, NY), 1)
    smoothed = dot(along_z, gauss(r - c, r >= 0))
    cohesion_out[...] = (1.0 - 0.6 * seed[...].astype(F32)) / (1.0 + 2.0 * smoothed)
    for f in range(3):
        spread_rows(face, f, low[f * LX : (f + 1) * LX], high[f * LX : (f + 1) * LX])
    x_low, x_high = sides(even_x(), x_far[0 : 3 * LZ], x_near[0 : 3 * LZ])
    masks = iotas()
    top_yield = jnp.full((CHUNK, NY), -jnp.inf, F32)
    top_eta = jnp.full((CHUNK, NY), -jnp.inf, F32)
    for start in range(0, ROWS, CHUNK):
        here = slice(start, start + CHUNK)
        eta = 1.0 / (1.0 / viscosity[here] + 1.0 / SHEAR)
        dxv, dzv, dyv = [], [], []
        for f in range(3):
            value = v[f, here]
            slab = slice(f * LZ, (f + 1) * LZ)
            dxv.append(diff_x(v, f, start, x_low[slab], x_high[slab]))
            dzv.append(diff_z(value, face_rows(face, 0, f, here), face_rows(face, 1, f, here), masks))
            dyv.append(diff_y(value, masks))
        p, tau, eta_shrink, yield_f, dlam = return_map(
            dxv, dzv, dyv, [old[i, here] for i in range(6)], eta, pressure[here], cohesion_out[here]
        )
        for i in range(6):
            held[i, here] = tau[i] - p if i < 3 else tau[i]
        pres[here] = p
        total[here] = plastic[here] + dlam
        eta_out[here] = eta
        top_yield = jnp.maximum(top_yield, yield_f)
        top_eta = jnp.maximum(top_eta, eta_shrink)
    store_row(row_out, top_yield, top_eta)
    send_x(held, ALONG_X, sx_far, sx_near)
    send_z(held, ALONG_Z, sz_far, sz_near, slots)


def residual(held, x_far, x_near, z_far, z_near, out, face):
    x_low, x_high = sides(even_x(), x_far[...], x_near[...])
    z_low, z_high = sides(even_z(), z_far[...], z_near[...])
    for f in range(3):
        rows = slice(f * LX, (f + 1) * LX)
        spread_rows(face, f, z_low[rows], z_high[rows])
    masks = iotas()
    for start in range(0, ROWS, CHUNK):
        here = slice(start, start + CHUNK)
        for f in range(3):
            slab = slice(f * LZ, (f + 1) * LZ)
            out[f, here] = (
                diff_x(held, ALONG_X[f], start, x_low[slab], x_high[slab])
                + diff_z(held[ALONG_Z[f], here], face_rows(face, 0, f, here), face_rows(face, 1, f, here), masks)
                + diff_y(held[ALONG_Y[f], here], masks)
            )


def residual_kernel(
    held, sx_far, sx_near, sz_far, sz_near, row,
    out, row_out, rx_far, rx_near, rz_far, rz_near, face, slots,
):
    relay_row(row, row_out)
    residual(held, sx_far, sx_near, sz_far, sz_near, out, face)
    send_x(out, range(3), rx_far, rx_near)
    send_z(out, range(3), rz_far, rz_near, slots)


def last_residual_kernel(held, sx_far, sx_near, sz_far, sz_near, out, face):
    residual(held, sx_far, sx_near, sz_far, sz_near, out, face)


def relay_kernel(row, row_out):
    relay_row(row, row_out)


def second_kernel(
    v, res, x_far, x_near, z_far, z_near, rx_far, rx_near, rz_far, rz_near, row,
    old, pressure, plastic, eta_in, cohesion,
    stress, pres, total, v_out, held, row_out, top_out, sx_far, sx_near, sz_far, sz_near,
    face, slots,
):
    top, peak = row_values(row)
    top_out[...] = jnp.broadcast_to(top, top_out.shape)
    step = 0.125 / peak
    for f in range(3):
        v_out[f] = v[f] + step * res[f]
    x_low, x_high = sides(
        even_x(),
        x_far[0 : 3 * LZ] + step * rx_far[...],
        x_near[0 : 3 * LZ] + step * rx_near[...],
    )
    z_low, z_high = sides(
        even_z(),
        z_far[0 : 3 * LX] + step * rz_far[...],
        z_near[0 : 3 * LX] + step * rz_near[...],
    )
    for f in range(3):
        rows = slice(f * LX, (f + 1) * LX)
        spread_rows(face, f, z_low[rows], z_high[rows])
    masks = iotas()
    top_yield = jnp.full((CHUNK, NY), -jnp.inf, F32)
    top_eta = jnp.full((CHUNK, NY), -jnp.inf, F32)
    for start in range(0, ROWS, CHUNK):
        here = slice(start, start + CHUNK)
        dxv, dzv, dyv = [], [], []
        for f in range(3):
            value = v_out[f, here]
            slab = slice(f * LZ, (f + 1) * LZ)
            dxv.append(diff_x(v_out, f, start, x_low[slab], x_high[slab]))
            dzv.append(diff_z(value, face_rows(face, 0, f, here), face_rows(face, 1, f, here), masks))
            dyv.append(diff_y(value, masks))
        p, tau, eta_shrink, yield_f, dlam = return_map(
            dxv, dzv, dyv, [old[i, here] for i in range(6)], eta_in[here], pressure[here], cohesion[here]
        )
        for i in range(6):
            stress[i, here] = tau[i]
            held[i, here] = tau[i] - p if i < 3 else tau[i]
        pres[here] = p
        total[here] = plastic[here] + dlam
        top_yield = jnp.maximum(top_yield, yield_f)
        top_eta = jnp.maximum(top_eta, eta_shrink)
    store_row(row_out, top_yield, top_eta)
    send_x(held, ALONG_X, sx_far, sx_near)
    send_z(held, ALONG_Z, sz_far, sz_near, slots)


def final_kernel(v, res, row, first_top, v_out, peaks):
    top, peak = row_values(row)
    step = 0.125 / peak
    for f in range(3):
        v_out[f] = v[f] + step * res[f]
    peaks[0] = jnp.max(first_top[...])
    peaks[1] = jnp.max(top)


def per_device(velocity, pressure, stress_old, plastic, viscosity, weak_seed):
    shapes = [a.shape for a in (velocity, pressure, stress_old, plastic)]
    one = (ROWS, NY)
    v = velocity.reshape((3,) + one)
    old = stress_old.reshape((6,) + one)
    pressure, plastic, viscosity, weak_seed = (
        a.reshape(one) for a in (pressure, plastic, viscosity, weak_seed)
    )
    three, six = (3,) + one, (6,) + one
    face = pltpu.VMEM((2, 3, 2, ROWS, 128), F32)
    slots = pltpu.VMEM((4, 2, ROWS, 128), F32)
    level_1, level_2 = lax.axis_size(YCORE), lax.axis_size(XZ)
    row_1, row_2 = (level_1, 1, 128), (level_2, 1, 128)
    x_3, z_3, x_9, z_9 = (3 * LZ, NY), (3 * LX, NY), (9 * LZ, NY), (9 * LX, NY)

    first = jnp.concatenate([v[:, :LZ].reshape(x_3), plastic[: 6 * LZ]])
    last = jnp.concatenate([v[:, ROWS - LZ :].reshape(x_3), plastic[ROWS - 6 * LZ :]])
    x_msgs = exchange(GX, *facing(even_x(), first, last))
    along, *z_msgs = call(smooth_x_kernel, [one, z_9, z_9], [v, plastic, *x_msgs], 10**6, [slots])
    z_msgs = exchange(GZ, *z_msgs)
    held, pres, total, eta, cohesion, row, *sent = call(
        first_kernel,
        [six, one, one, one, one, row_1, x_3, x_3, z_3, z_3],
        [v, pressure, old, along, plastic, viscosity, weak_seed, *x_msgs, *z_msgs],
        10**7,
        [face, slots],
    )
    row = spread(row, YCORE)
    got = exchange(GX, *sent[:2]) + exchange(GZ, *sent[2:])
    res, row, *sent = call(
        residual_kernel, [three, row_2, x_3, x_3, z_3, z_3], [held, *got, row], 10**6, [face, slots]
    )
    row = spread(row, XZ)
    got = exchange(GX, *sent[:2]) + exchange(GZ, *sent[2:])
    stress, pres, total, v, held, row, first_top, *sent = call(
        second_kernel,
        [six, one, one, three, six, row_1, (1, 128), x_3, x_3, z_3, z_3],
        [v, res, *x_msgs, *z_msgs, *got, row, old, pres, total, eta, cohesion],
        10**7,
        [face, slots],
    )
    row = spread(row, YCORE)
    got = exchange(GX, *sent[:2]) + exchange(GZ, *sent[2:])
    (row,) = call(relay_kernel, [row_2], [row], 10**4)
    row = spread(row, XZ)
    (res,) = call(last_residual_kernel, [three], [held, *got], 10**6, [face])
    v, peaks = call(final_kernel, [three, (2,)], [v, res, row, first_top], 10**5, (), [VMEM, SMEM])
    outs = [a.reshape(s) for a, s in zip((v, pres, stress, total), shapes)]
    return (*outs, peaks)


def solution(mesh):
    split = Mesh(mesh.devices.reshape(4, 8, 2, 4, 2), ("gx_0", "gx_1", "gx_2", "gz_0", "gz_1"))
    return jax.shard_map(
        per_device,
        mesh=split,
        in_specs=(
            P(None, GX, GZ, None),
            P(GX, GZ, None),
            P(None, GX, GZ, None),
            P(GX, GZ, None),
            P(GX, GZ, None),
            P(GX, GZ, None),
        ),
        out_specs=(
            P(None, GX, GZ, None),
            P(GX, GZ, None),
            P(None, GX, GZ, None),
            P(GX, GZ, None),
            P(),
        ),
        check_vma=False,
    )
```

time: 144 us -> 129 us (0.90)
  the two profiles are of different devices: /device:TPU:1 before, /device:TPU:6 now
where the time goes in v2:
time: 129 us; the launch traced here: 128 us
  starting transfers between devices  74.4 us (58%)
  blocking collectives  24.5 us (19%)
  local copies, waits for them, and re-layouts  11.1 us (9%)
  waiting for transfers between devices  10.9 us (8%)
  Pallas kernels  6.17 us (5%)
    ppermute x8, starting transfers between devices, exchange(): lax.ppermute(near, axis, pairs(count, 0))  31 us
    ppermute x8, starting transfers between devices, exchange(): lax.ppermute(far, axis, pairs(count, 1))  30.7 us
    all_to_all x2, blocking collectives, spread(): return lax.all_to_all(row, axes, 0, 0, tiled=True)  24.5 us
    all_to_all x2, starting transfers between devices, spread(): return lax.all_to_all(row, axes, 0, 0, tiled=True)  12.7 us
    unnamed x36, local copies, waits for them, and re-layouts  9.41 us
    pallas_call x7, Pallas kernels, call(): pl.pallas_call(kernel, out_shape=[jax.ShapeDtypeStruct(s, F32) for s in o...  6.17 us
    ppermute x8, waiting for transfers between devices, exchange(): lax.ppermute(far, axis, pairs(count, 1))  6.11 us
    ppermute x8, waiting for transfers between devices, exchange(): lax.ppermute(near, axis, pairs(count, 0))  4.78 us
  transfers between devices with their start and end apart: 18, of which 6 were waited for; matrix products, arithmetic and copies ran while one was open for 0% of the time, Pallas kernels for 1%

profile of v2, /device:TPU:6, one launch (start us, length us, event | category | flops | bytes accessed | tf_op | source)
XLA Modules:
  0.0 127.9 jit_solution(1695198343465436275)
XLA Ops:
  2.4 3.5 %collective-permute-start.1 = (f32[72,256]{1,0:T(8,128)S(1)}, f32[72,256]{1,0:T(8,128)S(1)}, u32[]{:S(2)}, u32[]{:S(2)}) collective-permute-start(f32[72,256]{1,0:T(8,128)S(1)} %get-tuple-element.71), channel_id=1, source_target_pairs={{0,8},{8,0},{16,24},{24,16},{32,40},{40,32},{48,56},{56,48},{64,72... | collective-permute-start | bytes 221192 | tf_op jit(solution)/shard_map/ppermute | solution.py:56
  5.8 11.1 %collective-permute-start = (f32[72,256]{1,0:T(8,128)S(1)}, f32[72,256]{1,0:T(8,128)S(1)}, u32[]{:S(2)}, u32[]{:S(2)}) collective-permute-start(f32[72,256]{1,0:T(8,128)S(1)} %get-tuple-element.72), channel_id=1, source_target_pairs={{8,16},{16,8},{24,32},{32,24},{40,48},{48,40},{56,64},{64,56},{72,... | collective-permute-start | bytes 221192 | tf_op jit(solution)/shard_map/ppermute | solution.py:55
  17.0 2.3 %collective-permute-done.x_far = f32[72,256]{1,0:T(8,128)S(1)} collective-permute-done((f32[72,256]{1,0:T(8,128)S(1)}, f32[72,256]{1,0:T(8,128)S(1)}, u32[]{:S(2)}, u32[]{:S(2)}) %collective-permute-start) | collective-permute-done | bytes 73760 | tf_op jit(solution)/shard_map/ppermute | solution.py:55
  21.1 7.0 %collective-permute-start.3 = (f32[144,256]{1,0:T(8,128)S(1)}, f32[144,256]{1,0:T(8,128)S(1)}, u32[]{:S(2)}, u32[]{:S(2)}) collective-permute-start(f32[144,256]{1,0:T(8,128)S(1)} %get-tuple-element.39), channel_id=1, source_target_pairs={{0,1},{1,0},{2,3},{3,2},{4,5},{5,4},{6,7},{7,6},{8,9},{9,8},{10,11... | collective-permute-start | bytes 442376 | tf_op jit(solution)/shard_map/ppermute | solution.py:56
  28.1 1.0 collective-permute-done.3.z_near
  31.8 1.4 %shard_map.102 = (f32[6,128,256]{2,1,0:T(8,128)S(1)}, f32[128,256]{1,0:T(8,128)S(1)}, f32[128,256]{1,0:T(8,128)S(1)}, f32[128,256]{1,0:T(8,128)S(1)}, f32[128,25...) custom-call(f32[3,128,256]{2,1,0:T(8,128)S(1)} %bitcast.20, ...), custom_call_target="tpu_custom_call" | custom-call | flops 10000000 | bytes 3743744 | tf_op jit(solution)/shard_map/pallas_call | solution.py:34
  33.9 5.9 %collective-permute-start.7 = (f32[48,256]{1,0:T(8,128)S(1)}, f32[48,256]{1,0:T(8,128)S(1)}, u32[]{:S(2)}, u32[]{:S(2)}) collective-permute-start(f32[48,256]{1,0:T(8,128)S(1)} %get-tuple-element.44), channel_id=1, source_target_pairs={{0,1},{1,0},{2,3},{3,2},{4,5},{5,4},{6,7},{7,6},{8,9},{9,8},{10,11... | collective-permute-start | bytes 147464 | tf_op jit(solution)/shard_map/ppermute | solution.py:56
  39.8 7.1 %collective-permute-start.4 = (f32[24,256]{1,0:T(8,128)S(1)}, f32[24,256]{1,0:T(8,128)S(1)}, u32[]{:S(2)}, u32[]{:S(2)}) collective-permute-start(f32[24,256]{1,0:T(8,128)S(1)} %get-tuple-element.41), channel_id=1, source_target_pairs={{8,16},{16,8},{24,32},{32,24},{40,48},{48,40},{56,64},{64,56},{72,... | collective-permute-start | bytes 73736 | tf_op jit(solution)/shard_map/ppermute | solution.py:55
  46.9 1.9 %collective-permute-start.5 = (f32[24,256]{1,0:T(8,128)S(1)}, f32[24,256]{1,0:T(8,128)S(1)}, u32[]{:S(2)}, u32[]{:S(2)}) collective-permute-start(f32[24,256]{1,0:T(8,128)S(1)} %get-tuple-element.42), channel_id=1, source_target_pairs={{0,8},{8,0},{16,24},{24,16},{32,40},{40,32},{48,56},{56,48},{64,72... | collective-permute-start | bytes 73736 | tf_op jit(solution)/shard_map/ppermute | solution.py:56
  48.9 13.6 %all_to_all.20.row = f32[16,1,128]{2,1,0:T(1,128)S(1)} all-to-all(f32[16,1,128]{2,1,0:T(1,128)S(1)} %get-tuple-element.45), channel_id=1, replica_groups=mesh['gx_0'=4,'gx_1'=8,'gx_2'=2,'gz_0'=4,'gz_1'=2] {'gx_2','gz_0','gz_1'}, dimensions={0} | all-to-all | bytes 16384 | tf_op jit(solution)/shard_map/all_to_all | solution.py:61
  64.1 3.8 %collective-permute-start.11 = (f32[48,256]{1,0:T(8,128)S(1)}, f32[48,256]{1,0:T(8,128)S(1)}, u32[]{:S(2)}, u32[]{:S(2)}) collective-permute-start(f32[48,256]{1,0:T(8,128)S(1)} %get-tuple-element.50), channel_id=1, source_target_pairs={{0,1},{1,0},{2,3},{3,2},{4,5},{5,4},{6,7},{7,6},{8,9},{9,8},{10,11... | collective-permute-start | bytes 147464 | tf_op jit(solution)/shard_map/ppermute | solution.py:56
  67.9 4.7 %all-to-all-start.1 = ((f32[32,1,128]{2,1,0:T(1,128)}), f32[32,1,128]{2,1,0:T(1,128)S(1)}, u32[]{:S(2)}, u32[]{:S(2)}) async-start(f32[32,1,128]{2,1,0:T(1,128)} %get-tuple-element.51), calls=%async_computation.1 | async-start | bytes 32768 | tf_op jit(solution)/shard_map/all_to_all | solution.py:61
  72.7 4.9 %collective-permute-start.8 = (f32[24,256]{1,0:T(8,128)S(1)}, f32[24,256]{1,0:T(8,128)S(1)}, u32[]{:S(2)}, u32[]{:S(2)}) collective-permute-start(f32[24,256]{1,0:T(8,128)S(1)} %get-tuple-element.47), channel_id=1, source_target_pairs={{8,16},{16,8},{24,32},{32,24},{40,48},{48,40},{56,64},{64,56},{72,... | collective-permute-start | bytes 73736 | tf_op jit(solution)/shard_map/ppermute | solution.py:55
  77.6 1.9 %collective-permute-start.9 = (f32[24,256]{1,0:T(8,128)S(1)}, f32[24,256]{1,0:T(8,128)S(1)}, u32[]{:S(2)}, u32[]{:S(2)}) collective-permute-start(f32[24,256]{1,0:T(8,128)S(1)} %get-tuple-element.48), channel_id=1, source_target_pairs={{0,8},{8,0},{16,24},{24,16},{32,40},{40,32},{48,56},{56,48},{64,72... | collective-permute-start | bytes 73736 | tf_op jit(solution)/shard_map/ppermute | solution.py:56
  79.5 1.9 %collective-permute-done.8.rx_far = f32[24,256]{1,0:T(8,128)S(1)} collective-permute-done((f32[24,256]{1,0:T(8,128)S(1)}, f32[24,256]{1,0:T(8,128)S(1)}, u32[]{:S(2)}, u32[]{:S(2)}) %collective-permute-start.8) | collective-permute-done | bytes 24608 | tf_op jit(solution)/shard_map/ppermute | solution.py:55
  81.4 1.9 %collective-permute-done.9.rx_near = f32[24,256]{1,0:T(8,128)S(1)} collective-permute-done((f32[24,256]{1,0:T(8,128)S(1)}, f32[24,256]{1,0:T(8,128)S(1)}, u32[]{:S(2)}, u32[]{:S(2)}) %collective-permute-start.9) | collective-permute-done | bytes 24608 | tf_op jit(solution)/shard_map/ppermute | solution.py:56
  87.9 1.9 %shard_map.104 = (f32[6,128,256]{2,1,0:T(8,128)}, f32[128,256]{1,0:T(8,128)}, f32[128,256]{1,0:T(8,128)}, f32[3,128,256]{2,1,0:T(8,128)S(1)}, f32[6,128,256]{2,1...) custom-call(f32[3,128,256]{2,1,0:T(8,128)S(1)} %bitcast.21, ...), custom_call_target="tpu_custom_call" | custom-call | flops 10000000 | bytes 5087744 | tf_op jit(solution)/shard_map/pallas_call | solution.py:34
  91.6 5.0 %collective-permute-start.15 = (f32[48,256]{1,0:T(8,128)}, f32[48,256]{1,0:T(8,128)S(1)}, u32[]{:S(2)}, u32[]{:S(2)}) collective-permute-start(f32[48,256]{1,0:T(8,128)} %get-tuple-element.61), channel_id=1, source_target_pairs={{0,1},{1,0},{2,3},{3,2},{4,5},{5,4},{6,7},{7,6},{8,9},{9,8},{10,11... | collective-permute-start | bytes 147464 | tf_op jit(solution)/shard_map/ppermute | solution.py:56
  96.6 10.8 %all_to_all.21.row = f32[16,1,128]{2,1,0:T(1,128)S(1)} all-to-all(f32[16,1,128]{2,1,0:T(1,128)S(1)} %get-tuple-element.62), channel_id=1, replica_groups=mesh['gx_0'=4,'gx_1'=8,'gx_2'=2,'gz_0'=4,'gz_1'=2] {'gx_2','gz_0','gz_1'}, dimensions={0} | all-to-all | bytes 16384 | tf_op jit(solution)/shard_map/all_to_all | solution.py:61
  108.0 8.0 %all-to-all-start.3 = ((f32[32,1,128]{2,1,0:T(1,128)}), f32[32,1,128]{2,1,0:T(1,128)S(1)}, u32[]{:S(2)}, u32[]{:S(2)}) async-start(f32[32,1,128]{2,1,0:T(1,128)} %shard_map.106), calls=%async_computation.3 | async-start | bytes 32768 | tf_op jit(solution)/shard_map/all_to_all | solution.py:61
  116.0 4.9 %collective-permute-start.12 = (f32[24,256]{1,0:T(8,128)S(1)}, f32[24,256]{1,0:T(8,128)S(1)}, u32[]{:S(2)}, u32[]{:S(2)}) collective-permute-start(f32[24,256]{1,0:T(8,128)S(1)} %copy-done.17), channel_id=1, source_target_pairs={{8,16},{16,8},{24,32},{32,24},{40,48},{48,40},{56,64},{64,56},{72,... | collective-permute-start | bytes 73736 | tf_op jit(solution)/shard_map/ppermute | solution.py:55
  120.9 1.9 %collective-permute-start.13 = (f32[24,256]{1,0:T(8,128)S(1)}, f32[24,256]{1,0:T(8,128)S(1)}, u32[]{:S(2)}, u32[]{:S(2)}) collective-permute-start(f32[24,256]{1,0:T(8,128)S(1)} %copy-done.15), channel_id=1, source_target_pairs={{0,8},{8,0},{16,24},{24,16},{32,40},{40,32},{48,56},{56,48},{64,72... | collective-permute-start | bytes 73736 | tf_op jit(solution)/shard_map/ppermute | solution.py:56
  122.9 1.9 %collective-permute-done.12.sx_far = f32[24,256]{1,0:T(8,128)S(1)} collective-permute-done((f32[24,256]{1,0:T(8,128)S(1)}, f32[24,256]{1,0:T(8,128)S(1)}, u32[]{:S(2)}, u32[]{:S(2)}) %collective-permute-start.12) | collective-permute-done | bytes 24608 | tf_op jit(solution)/shard_map/ppermute | solution.py:55
  124.8 1.9 %collective-permute-done.13.sx_near = f32[24,256]{1,0:T(8,128)S(1)} collective-permute-done((f32[24,256]{1,0:T(8,128)S(1)}, f32[24,256]{1,0:T(8,128)S(1)}, u32[]{:S(2)}, u32[]{:S(2)}) %collective-permute-start.13) | collective-permute-done | bytes 24608 | tf_op jit(solution)/shard_map/ppermute | solution.py:56
  (60 shorter events, 16.7 us)
Async XLA Ops:
  0.6 18.6 %copy-start = (f32[3,16,8,256]{3,2,1,0:T(8,128)S(1)}, f32[3,16,8,256]{3,2,1,0:T(8,128)}, u32[]{:S(2)}) copy-start(f32[3,16,8,256]{3,2,1,0:T(8,128)} %param.6) | copy-start | bytes 1179652
  0.6 28.4 %copy-start.1 = (f32[6,16,8,256]{3,2,1,0:T(8,128)S(1)}, f32[6,16,8,256]{3,2,1,0:T(8,128)}, u32[]{:S(2)}) copy-start(f32[6,16,8,256]{3,2,1,0:T(8,128)} %param.8) | copy-start | bytes 2359300
  2.4 14.6 %collective-permute-start.1 = (f32[72,256]{1,0:T(8,128)S(1)}, f32[72,256]{1,0:T(8,128)S(1)}, u32[]{:S(2)}, u32[]{:S(2)}) collective-permute-start(f32[72,256]{1,0:T(8,128)S(1)} %get-tuple-element.71), channel_id=1, source_target_pairs={{0,8},{8,0},{16,24},{24,16},{32,40},{40,32},{48,56},{56,48},{64,72... | collective-permute-start | bytes 221192 | tf_op jit(solution)/shard_map/ppermute | solution.py:56
  5.8 13.4 %collective-permute-start = (f32[72,256]{1,0:T(8,128)S(1)}, f32[72,256]{1,0:T(8,128)S(1)}, u32[]{:S(2)}, u32[]{:S(2)}) collective-permute-start(f32[72,256]{1,0:T(8,128)S(1)} %get-tuple-element.72), channel_id=1, source_target_pairs={{8,16},{16,8},{24,32},{32,24},{40,48},{48,40},{56,64},{64,56},{72,... | collective-permute-start | bytes 221192 | tf_op jit(solution)/shard_map/ppermute | solution.py:55
  20.4 7.7 %collective-permute-start.2 = (f32[144,256]{1,0:T(8,128)S(1)}, f32[144,256]{1,0:T(8,128)S(1)}, u32[]{:S(2)}, u32[]{:S(2)}) collective-permute-start(f32[144,256]{1,0:T(8,128)S(1)} %get-tuple-element.38), channel_id=1, source_target_pairs={{1,2},{2,1},{3,4},{4,3},{5,6},{6,5},{9,10},{10,9},{11,12},{12,11},... | collective-permute-start | bytes 442376 | tf_op jit(solution)/shard_map/ppermute | solution.py:55
  21.1 8.0 %collective-permute-start.3 = (f32[144,256]{1,0:T(8,128)S(1)}, f32[144,256]{1,0:T(8,128)S(1)}, u32[]{:S(2)}, u32[]{:S(2)}) collective-permute-start(f32[144,256]{1,0:T(8,128)S(1)} %get-tuple-element.39), channel_id=1, source_target_pairs={{0,1},{1,0},{2,3},{3,2},{4,5},{5,4},{6,7},{7,6},{8,9},{9,8},{10,11... | collective-permute-start | bytes 442376 | tf_op jit(solution)/shard_map/ppermute | solution.py:56
  33.2 30.2 %copy-start.6 = (f32[128,256]{1,0:T(8,128)}, f32[128,256]{1,0:T(8,128)S(1)}, u32[]{:S(2)}) copy-start(f32[128,256]{1,0:T(8,128)S(1)} %get-tuple-element.54.eta_in) | copy-start | bytes 393220
  33.2 30.2 %copy-start.8 = (f32[128,256]{1,0:T(8,128)}, f32[128,256]{1,0:T(8,128)S(1)}, u32[]{:S(2)}) copy-start(f32[128,256]{1,0:T(8,128)S(1)} %get-tuple-element.55.cohesion) | copy-start | bytes 393220
  33.2 29.3 %collective-permute-start.6 = (f32[48,256]{1,0:T(8,128)S(1)}, f32[48,256]{1,0:T(8,128)S(1)}, u32[]{:S(2)}, u32[]{:S(2)}) collective-permute-start(f32[48,256]{1,0:T(8,128)S(1)} %get-tuple-element.43), channel_id=1, source_target_pairs={{1,2},{2,1},{3,4},{4,3},{5,6},{6,5},{9,10},{10,9},{11,12},{12,11},... | collective-permute-start | bytes 147464 | tf_op jit(solution)/shard_map/ppermute | solution.py:55
  33.9 28.7 %collective-permute-start.7 = (f32[48,256]{1,0:T(8,128)S(1)}, f32[48,256]{1,0:T(8,128)S(1)}, u32[]{:S(2)}, u32[]{:S(2)}) collective-permute-start(f32[48,256]{1,0:T(8,128)S(1)} %get-tuple-element.44), channel_id=1, source_target_pairs={{0,1},{1,0},{2,3},{3,2},{4,5},{5,4},{6,7},{7,6},{8,9},{9,8},{10,11... | collective-permute-start | bytes 147464 | tf_op jit(solution)/shard_map/ppermute | solution.py:56
  39.8 22.7 %collective-permute-start.4 = (f32[24,256]{1,0:T(8,128)S(1)}, f32[24,256]{1,0:T(8,128)S(1)}, u32[]{:S(2)}, u32[]{:S(2)}) collective-permute-start(f32[24,256]{1,0:T(8,128)S(1)} %get-tuple-element.41), channel_id=1, source_target_pairs={{8,16},{16,8},{24,32},{32,24},{40,48},{48,40},{56,64},{64,56},{72,... | collective-permute-start | bytes 73736 | tf_op jit(solution)/shard_map/ppermute | solution.py:55
  46.9 15.6 %collective-permute-start.5 = (f32[24,256]{1,0:T(8,128)S(1)}, f32[24,256]{1,0:T(8,128)S(1)}, u32[]{:S(2)}, u32[]{:S(2)}) collective-permute-start(f32[24,256]{1,0:T(8,128)S(1)} %get-tuple-element.42), channel_id=1, source_target_pairs={{0,8},{8,0},{16,24},{24,16},{32,40},{40,32},{48,56},{56,48},{64,72... | collective-permute-start | bytes 73736 | tf_op jit(solution)/shard_map/ppermute | solution.py:56
  63.4 20.5 %collective-permute-start.10 = (f32[48,256]{1,0:T(8,128)S(1)}, f32[48,256]{1,0:T(8,128)S(1)}, u32[]{:S(2)}, u32[]{:S(2)}) collective-permute-start(f32[48,256]{1,0:T(8,128)S(1)} %get-tuple-element.49), channel_id=1, source_target_pairs={{1,2},{2,1},{3,4},{4,3},{5,6},{6,5},{9,10},{10,9},{11,12},{12,11},... | collective-permute-start | bytes 147464 | tf_op jit(solution)/shard_map/ppermute | solution.py:55
  64.1 19.8 %collective-permute-start.11 = (f32[48,256]{1,0:T(8,128)S(1)}, f32[48,256]{1,0:T(8,128)S(1)}, u32[]{:S(2)}, u32[]{:S(2)}) collective-permute-start(f32[48,256]{1,0:T(8,128)S(1)} %get-tuple-element.50), channel_id=1, source_target_pairs={{0,1},{1,0},{2,3},{3,2},{4,5},{5,4},{6,7},{7,6},{8,9},{9,8},{10,11... | collective-permute-start | bytes 147464 | tf_op jit(solution)/shard_map/ppermute | solution.py:56
  67.9 16.0 %all-to-all-start.1 = ((f32[32,1,128]{2,1,0:T(1,128)}), f32[32,1,128]{2,1,0:T(1,128)S(1)}, u32[]{:S(2)}, u32[]{:S(2)}) async-start(f32[32,1,128]{2,1,0:T(1,128)} %get-tuple-element.51), calls=%async_computation.1 | async-start | bytes 32768 | tf_op jit(solution)/shard_map/all_to_all | solution.py:61
  72.7 8.7 %collective-permute-start.8 = (f32[24,256]{1,0:T(8,128)S(1)}, f32[24,256]{1,0:T(8,128)S(1)}, u32[]{:S(2)}, u32[]{:S(2)}) collective-permute-start(f32[24,256]{1,0:T(8,128)S(1)} %get-tuple-element.47), channel_id=1, source_target_pairs={{8,16},{16,8},{24,32},{32,24},{40,48},{48,40},{56,64},{64,56},{72,... | collective-permute-start | bytes 73736 | tf_op jit(solution)/shard_map/ppermute | solution.py:55
  77.6 5.7 %collective-permute-start.9 = (f32[24,256]{1,0:T(8,128)S(1)}, f32[24,256]{1,0:T(8,128)S(1)}, u32[]{:S(2)}, u32[]{:S(2)}) collective-permute-start(f32[24,256]{1,0:T(8,128)S(1)} %get-tuple-element.48), channel_id=1, source_target_pairs={{0,8},{8,0},{16,24},{24,16},{32,40},{40,32},{48,56},{56,48},{64,72... | collective-permute-start | bytes 73736 | tf_op jit(solution)/shard_map/ppermute | solution.py:56
  90.9 35.7 %collective-permute-start.14 = (f32[48,256]{1,0:T(8,128)}, f32[48,256]{1,0:T(8,128)S(1)}, u32[]{:S(2)}, u32[]{:S(2)}) collective-permute-start(f32[48,256]{1,0:T(8,128)} %get-tuple-element.60), channel_id=1, source_target_pairs={{1,2},{2,1},{3,4},{4,3},{5,6},{6,5},{9,10},{10,9},{11,12},{12,11},... | collective-permute-start | bytes 147464 | tf_op jit(solution)/shard_map/ppermute | solution.py:55
  91.6 35.1 %collective-permute-start.15 = (f32[48,256]{1,0:T(8,128)}, f32[48,256]{1,0:T(8,128)S(1)}, u32[]{:S(2)}, u32[]{:S(2)}) collective-permute-start(f32[48,256]{1,0:T(8,128)} %get-tuple-element.61), channel_id=1, source_target_pairs={{0,1},{1,0},{2,3},{3,2},{4,5},{5,4},{6,7},{7,6},{8,9},{9,8},{10,11... | collective-permute-start | bytes 147464 | tf_op jit(solution)/shard_map/ppermute | solution.py:56
  107.4 8.6 %copy-start.17 = (f32[24,256]{1,0:T(8,128)S(1)}, f32[24,256]{1,0:T(8,128)}, u32[]{:S(2)}) copy-start(f32[24,256]{1,0:T(8,128)} %copy-done.16) | copy-start | bytes 73732
  107.4 13.5 %copy-start.15 = (f32[24,256]{1,0:T(8,128)S(1)}, f32[24,256]{1,0:T(8,128)}, u32[]{:S(2)}) copy-start(f32[24,256]{1,0:T(8,128)} %copy-done.14) | copy-start | bytes 73732
  108.0 19.0 %all-to-all-start.3 = ((f32[32,1,128]{2,1,0:T(1,128)}), f32[32,1,128]{2,1,0:T(1,128)S(1)}, u32[]{:S(2)}, u32[]{:S(2)}) async-start(f32[32,1,128]{2,1,0:T(1,128)} %shard_map.106), calls=%async_computation.3 | async-start | bytes 32768 | tf_op jit(solution)/shard_map/all_to_all | solution.py:61
  116.0 8.7 %collective-permute-start.12 = (f32[24,256]{1,0:T(8,128)S(1)}, f32[24,256]{1,0:T(8,128)S(1)}, u32[]{:S(2)}, u32[]{:S(2)}) collective-permute-start(f32[24,256]{1,0:T(8,128)S(1)} %copy-done.17), channel_id=1, source_target_pairs={{8,16},{16,8},{24,32},{32,24},{40,48},{48,40},{56,64},{64,56},{72,... | collective-permute-start | bytes 73736 | tf_op jit(solution)/shard_map/ppermute | solution.py:55
  120.9 5.7 %collective-permute-start.13 = (f32[24,256]{1,0:T(8,128)S(1)}, f32[24,256]{1,0:T(8,128)S(1)}, u32[]{:S(2)}, u32[]{:S(2)}) collective-permute-start(f32[24,256]{1,0:T(8,128)S(1)} %copy-done.15), channel_id=1, source_target_pairs={{0,8},{8,0},{16,24},{24,16},{32,40},{40,32},{48,56},{56,48},{64,72... | collective-permute-start | bytes 73736 | tf_op jit(solution)/shard_map/ppermute | solution.py:56
  (12 other events, 9.4 us)

commit v3 on v2

--- a/solution.py
+++ b/solution.py
@@ -26,18 +26,19 @@
 ALONG_Y = (XY, ZY, YY)
 VMEM = pl.BlockSpec(memory_space=pltpu.VMEM)
 SMEM = pl.BlockSpec(memory_space=pltpu.SMEM)
-
-
-def call(kernel, outs, operands, flops, scratch=(), out_specs=None):
+HBM = pl.BlockSpec(memory_space=pltpu.HBM)
+
+
+def call(kernel, outs, operands, flops, scratch=(), out_specs=None, in_specs=None, limit=14):
     size = sum(math.prod(a.shape) * 4 for a in operands)
     size += sum(math.prod(s) * 4 for s in outs)
     return pl.pallas_call(
         kernel,
         out_shape=[jax.ShapeDtypeStruct(s, F32) for s in outs],
-        in_specs=[VMEM] * len(operands),
+        in_specs=in_specs or [VMEM] * len(operands),
         out_specs=out_specs or [VMEM] * len(outs),
         scratch_shapes=list(scratch),
-        compiler_params=pltpu.CompilerParams(vmem_limit_bytes=14 * 1024 * 1024),
+        compiler_params=pltpu.CompilerParams(vmem_limit_bytes=limit * 1024 * 1024),
         cost_estimate=pl.CostEstimate(flops=flops, bytes_accessed=size, transcendentals=0),
     )(*operands)
 
@@ -131,41 +132,91 @@
     return jnp.concatenate([slots[f, h, pl.ds(z, LX, stride=LZ), :] for h in range(2)], axis=1)
 
 
-def send_x(ref, fields, far, near):
-    even = even_x()
+def place(axes):
+    index, count = 0, 1
+    for axis in axes:
+        size = lax.axis_size(axis)
+        index, count = index * size + lax.axis_index(axis), count * size
+    return index > 0, index < count - 1
+
+
+def x_faces(ref, fields, out):
     for i, f in enumerate(fields):
-        a, b = facing(even, ref[f, 0:LZ], ref[f, ROWS - LZ : ROWS])
-        far[i * LZ : (i + 1) * LZ] = a
-        near[i * LZ : (i + 1) * LZ] = b
-
-
-def send_z(ref, fields, far, near, slots):
-    even = even_z()
+        out[0, i * LZ : (i + 1) * LZ] = ref[f, 0:LZ]
+        out[1, i * LZ : (i + 1) * LZ] = ref[f, ROWS - LZ : ROWS]
+
+
+def z_faces(ref, fields, out, slots):
     for i, f in enumerate(fields):
         keep(slots, i, ref[f])
-        a, b = facing(even, layer(slots, i, 0), layer(slots, i, LZ - 1))
-        far[i * LX : (i + 1) * LX] = a
-        near[i * LX : (i + 1) * LX] = b
-
-
-def store_row(out, top_yield, top_eta):
+        out[0, i * LX : (i + 1) * LX] = layer(slots, i, 0)
+        out[1, i * LX : (i + 1) * LX] = layer(slots, i, LZ - 1)
+
+
+def faces_kernel(v, plastic, x_far, x_near, sem):
+    even = even_x()
+    for i, (out, low) in enumerate(((x_far, even), (x_near, jnp.logical_not(even)))):
+        top = pl.multiple_of(jnp.where(low, 0, ROWS - LZ), LZ)
+        deep = pl.multiple_of(jnp.where(low, 0, ROWS - 6 * LZ), LZ)
+        copies = [
+            pltpu.make_async_copy(
+                v.at[f, pl.ds(top, LZ)], out.at[pl.ds(f * LZ, LZ)], sem.at[4 * i + f]
+            )
+            for f in range(3)
+        ]
+        copies.append(
+            pltpu.make_async_copy(
+                plastic.at[pl.ds(deep, 6 * LZ)], out.at[pl.ds(3 * LZ, 6 * LZ)], sem.at[4 * i + 3]
+            )
+        )
+        for copy in copies:
+            copy.start()
+    for i, out in enumerate((x_far, x_near)):
+        for f in range(3):
+            rows = pl.ds(f * LZ, LZ)
+            pltpu.make_async_copy(v.at[f, pl.ds(0, LZ)], out.at[rows], sem.at[4 * i + f]).wait()
+        rows = pl.ds(3 * LZ, 6 * LZ)
+        pltpu.make_async_copy(plastic.at[pl.ds(0, 6 * LZ)], out.at[rows], sem.at[4 * i + 3]).wait()
+
+
+def load_kernel(
+    v_in, plastic_in, pressure_in, old_in, viscosity_in, seed_in,
+    v, plastic, pressure, old, eta, weak, viscosity, seed, sem,
+):
+    ins = (viscosity_in, seed_in, v_in, plastic_in, pressure_in, old_in)
+    outs = (viscosity, seed, v, plastic, pressure, old)
+    copies = [pltpu.make_async_copy(a, b, sem.at[i]) for i, (a, b) in enumerate(zip(ins, outs))]
+    for copy in copies:
+        copy.start()
+    copies[0].wait()
+    eta[...] = 1.0 / (1.0 / viscosity[...] + 1.0 / SHEAR)
+    copies[1].wait()
+    weak[...] = 1.0 - 0.6 * seed[...].astype(F32)
+    for copy in copies[2:]:
+        copy.wait()
+
+
+def store_row(out, top_yield, top_eta, earlier=None):
     a = jnp.max(top_yield, axis=(0, 1), keepdims=True)
     b = jnp.max(top_eta, axis=(0, 1), keepdims=True)
     lane = lax.broadcasted_iota(jnp.int32, (1, 128), 1)
     row = jnp.where(lane == 0, a, b)
+    if earlier is not None:
+        row = jnp.where(lane == 2, earlier, row)
     out[...] = jnp.broadcast_to(row[None], out.shape)
 
 
 def relay_row(ref, out):
-    out[...] = jnp.broadcast_to(jnp.max(ref[...], axis=0, keepdims=True), out.shape)
-
-
-def row_values(ref):
-    row = jnp.max(ref[...], axis=0)
+    row = jnp.max(ref[...], axis=0)[0:1]
+    out[...] = jnp.broadcast_to(row[None], out.shape)
+
+
+def row_values(ref, lanes):
+    row = jnp.max(ref[...], axis=0)[0:1]
     lane = lax.broadcasted_iota(jnp.int32, (1, 128), 1)
-    top = jnp.max(jnp.where(lane == 0, row, -jnp.inf), axis=(0, 1), keepdims=True)
-    eta = jnp.max(jnp.where(lane == 1, row, -jnp.inf), axis=(0, 1), keepdims=True)
-    return top, eta
+    return [
+        jnp.max(jnp.where(lane == i, row, -jnp.inf), axis=(0, 1), keepdims=True) for i in lanes
+    ]
 
 
 def return_map(dxv, dzv, dyv, old, eta, pres, cohesion):
@@ -223,9 +274,9 @@
 
 
 def first_kernel(
-    v, pressure, old, along, plastic, viscosity, seed, x_far, x_near, z_far, z_near,
-    held, pres, total, eta_out, cohesion_out, row_out, sx_far, sx_near, sz_far, sz_near,
-    face, slots,
+    v, pressure, old, along, plastic, eta_in, weak, x_far, x_near, z_far, z_near,
+    part, pres, total, cohesion_out, vx_out, vz_out, gx, fz, row_out, sz_far, sz_near,
+    face, slots, held,
 ):
     low, high = sides(even_z(), z_far[...], z_near[...])
     r = lax.broadcasted_iota(jnp.int32, (ROWS, ROWS), 0)
@@ -240,16 +291,18 @@
     r = lax.broadcasted_iota(jnp.int32, (NY, NY), 0)
     c = lax.broadcasted_iota(jnp.int32, (NY, NY), 1)
     smoothed = dot(along_z, gauss(r - c, r >= 0))
-    cohesion_out[...] = (1.0 - 0.6 * seed[...].astype(F32)) / (1.0 + 2.0 * smoothed)
+    cohesion_out[...] = weak[...] / (1.0 + 2.0 * smoothed)
     for f in range(3):
         spread_rows(face, f, low[f * LX : (f + 1) * LX], high[f * LX : (f + 1) * LX])
     x_low, x_high = sides(even_x(), x_far[0 : 3 * LZ], x_near[0 : 3 * LZ])
+    vx_out[0], vx_out[1] = x_low, x_high
+    vz_out[0], vz_out[1] = low[0 : 3 * LX], high[0 : 3 * LX]
     masks = iotas()
     top_yield = jnp.full((CHUNK, NY), -jnp.inf, F32)
     top_eta = jnp.full((CHUNK, NY), -jnp.inf, F32)
     for start in range(0, ROWS, CHUNK):
         here = slice(start, start + CHUNK)
-        eta = 1.0 / (1.0 / viscosity[here] + 1.0 / SHEAR)
+        eta = eta_in[here]
         dxv, dzv, dyv = [], [], []
         for f in range(3):
             value = v[f, here]
@@ -264,12 +317,34 @@
             held[i, here] = tau[i] - p if i < 3 else tau[i]
         pres[here] = p
         total[here] = plastic[here] + dlam
-        eta_out[here] = eta
         top_yield = jnp.maximum(top_yield, yield_f)
         top_eta = jnp.maximum(top_eta, eta_shrink)
     store_row(row_out, top_yield, top_eta)
-    send_x(held, ALONG_X, sx_far, sx_near)
-    send_z(held, ALONG_Z, sz_far, sz_near, slots)
+    nothing = jnp.zeros((LZ, NY), F32)
+    for start in range(0, ROWS, CHUNK):
+        here = slice(start, start + CHUNK)
+        for f in range(3):
+            part[f, here] = (
+                diff_x(held, ALONG_X[f], start, nothing, nothing)
+                + diff_z(held[ALONG_Z[f], here], 0.0, 0.0, masks)
+                + diff_y(held[ALONG_Y[f], here], masks)
+            )
+    x_faces(held, ALONG_X, gx)
+    z_faces(held, ALONG_Z, fz, slots)
+    even = even_z()
+    a, b = facing(even, fz[0], fz[1])
+    sz_far[0 : 3 * LX], sz_near[0 : 3 * LX] = a, b
+    for i in range(3):
+        keep(slots, 3 + i, part[i])
+        a, b = facing(even, layer(slots, 3 + i, 0), layer(slots, 3 + i, LZ - 1))
+        sz_far[(3 + i) * LX : (4 + i) * LX] = a
+        sz_near[(3 + i) * LX : (4 + i) * LX] = b
+    corners = []
+    for z in (0, LZ - 1):
+        ends = [held[f, x * LZ + z : x * LZ + z + 1] for f in (XX, XY) for x in (0, LX - 1)]
+        corners.append(jnp.concatenate(ends + ends, axis=0))
+    a, b = facing(even, *corners)
+    sz_far[6 * LX :], sz_near[6 * LX :] = a, b
 
 
 def residual(held, x_far, x_near, z_far, z_near, out, face):
@@ -290,45 +365,83 @@
             )
 
 
-def residual_kernel(
-    held, sx_far, sx_near, sz_far, sz_near, row,
-    out, row_out, rx_far, rx_near, rz_far, rz_near, face, slots,
-):
+def x_pack_kernel(part, gx, sz_far, sz_near, row, row_out, sx_far, sx_near):
     relay_row(row, row_out)
-    residual(held, sx_far, sx_near, sz_far, sz_near, out, face)
-    send_x(out, range(3), rx_far, rx_near)
-    send_z(out, range(3), rz_far, rz_near, slots)
+    low, high = sides(even_z(), sz_far[...], sz_near[...])
+    z = lax.broadcasted_iota(jnp.int32, (LZ, NY), 0)
+    messages = []
+    for e, x in enumerate((0, LX - 1)):
+        pieces = [gx[e]]
+        for f in range(3):
+            below_z, above_z = (h[f * LX + x : f * LX + x + 1] for h in (low, high))
+            pieces.append(
+                part[f, x * LZ : (x + 1) * LZ]
+                - jnp.where(z == 0, below_z * 0.5, 0.0)
+                + jnp.where(z == LZ - 1, above_z * 0.5, 0.0)
+            )
+        ends = []
+        for h in (low, high):
+            ends += [h[6 * LX + e : 6 * LX + e + 1], h[x : x + 1], h[6 * LX + 2 + e : 6 * LX + 3 + e]]
+        pieces.append(jnp.concatenate(ends + ends[:2], axis=0))
+        messages.append(jnp.concatenate(pieces, axis=0))
+    sx_far[...], sx_near[...] = facing(even_x(), *messages)
+
+
+def residual_kernel(part, gx, fz, sx_far, sx_near, sz_far, sz_near, out, rx, rz, face):
+    x_low, x_high = sides(even_x(), sx_far[...], sx_near[...])
+    z_low, z_high = sides(even_z(), sz_far[...], sz_near[...])
+    masks = iotas()
+    for f in range(3):
+        rows = slice(f * LX, (f + 1) * LX)
+        spread_rows(face, f, z_low[rows], z_high[rows])
+        slab = slice(f * LZ, (f + 1) * LZ)
+        for start in range(0, ROWS, CHUNK):
+            here = slice(start, start + CHUNK)
+            out[f, here] = (
+                part[f, here]
+                - jnp.where(masks[0], face_rows(face, 0, f, here) * 0.5, 0.0)
+                + jnp.where(masks[1], face_rows(face, 1, f, here) * 0.5, 0.0)
+            )
+        out[f, 0:LZ] = out[f, 0:LZ] - x_low[slab] * 0.5
+        out[f, ROWS - LZ : ROWS] = out[f, ROWS - LZ : ROWS] + x_high[slab] * 0.5
+    has_low, has_high = place(GX)
+    rx[0] = jnp.where(has_low, x_low[3 * LZ : 6 * LZ] + gx[0] * 0.5, 0.0)
+    rx[1] = jnp.where(has_high, x_high[3 * LZ : 6 * LZ] - gx[1] * 0.5, 0.0)
+    x = lax.broadcasted_iota(jnp.int32, (LX, NY), 0)
+    for side, (has, slab, sign) in enumerate(zip(place(GZ), (z_low, z_high), (0.5, -0.5))):
+        for f in range(3):
+            rows = slice(f * LX, (f + 1) * LX)
+            end = 6 * LZ + 3 * side + f
+            value = (
+                slab[(3 + f) * LX : (4 + f) * LX]
+                + fz[side, rows] * sign
+                - jnp.where(x == 0, x_low[end : end + 1] * 0.5, 0.0)
+                + jnp.where(x == LX - 1, x_high[end : end + 1] * 0.5, 0.0)
+            )
+            rz[side, rows] = jnp.where(has, value, 0.0)
 
 
 def last_residual_kernel(held, sx_far, sx_near, sz_far, sz_near, out, face):
     residual(held, sx_far, sx_near, sz_far, sz_near, out, face)
 
 
-def relay_kernel(row, row_out):
+def relay_kernel(gx, sz_far, sz_near, row, row_out, sx_far, sx_near):
     relay_row(row, row_out)
+    sx_far[...], sx_near[...] = facing(even_x(), gx[0], gx[1])
 
 
 def second_kernel(
-    v, res, x_far, x_near, z_far, z_near, rx_far, rx_near, rz_far, rz_near, row,
+    v, res, vx, vz, rx, rz, row,
     old, pressure, plastic, eta_in, cohesion,
-    stress, pres, total, v_out, held, row_out, top_out, sx_far, sx_near, sz_far, sz_near,
-    face, slots,
+    stress, pres, total, v_out, held, row_out, gx, sz_far, sz_near,
+    face, slots, fz,
 ):
-    top, peak = row_values(row)
-    top_out[...] = jnp.broadcast_to(top, top_out.shape)
+    top, peak = row_values(row, (0, 1))
     step = 0.125 / peak
     for f in range(3):
         v_out[f] = v[f] + step * res[f]
-    x_low, x_high = sides(
-        even_x(),
-        x_far[0 : 3 * LZ] + step * rx_far[...],
-        x_near[0 : 3 * LZ] + step * rx_near[...],
-    )
-    z_low, z_high = sides(
-        even_z(),
-        z_far[0 : 3 * LX] + step * rz_far[...],
-        z_near[0 : 3 * LX] + step * rz_near[...],
-    )
+    x_low, x_high = vx[0] + step * rx[0], vx[1] + step * rx[1]
+    z_low, z_high = vz[0] + step * rz[0], vz[1] + step * rz[1]
     for f in range(3):
         rows = slice(f * LX, (f + 1) * LX)
         spread_rows(face, f, z_low[rows], z_high[rows])
@@ -354,17 +467,18 @@
         total[here] = plastic[here] + dlam
         top_yield = jnp.maximum(top_yield, yield_f)
         top_eta = jnp.maximum(top_eta, eta_shrink)
-    store_row(row_out, top_yield, top_eta)
-    send_x(held, ALONG_X, sx_far, sx_near)
-    send_z(held, ALONG_Z, sz_far, sz_near, slots)
-
-
-def final_kernel(v, res, row, first_top, v_out, peaks):
-    top, peak = row_values(row)
+    store_row(row_out, top_yield, top_eta, top)
+    x_faces(held, ALONG_X, gx)
+    z_faces(held, ALONG_Z, fz, slots)
+    sz_far[...], sz_near[...] = facing(even_z(), fz[0], fz[1])
+
+
+def final_kernel(v, res, row, v_out, peaks):
+    top, peak, first_top = row_values(row, (0, 1, 2))
     step = 0.125 / peak
     for f in range(3):
         v_out[f] = v[f] + step * res[f]
-    peaks[0] = jnp.max(first_top[...])
+    peaks[0] = jnp.max(first_top)
     peaks[1] = jnp.max(top)
 
 
@@ -372,49 +486,63 @@
     shapes = [a.shape for a in (velocity, pressure, stress_old, plastic)]
     one = (ROWS, NY)
     v = velocity.reshape((3,) + one)
-    old = stress_old.reshape((6,) + one)
+    old = again = stress_old.reshape((6,) + one)
     pressure, plastic, viscosity, weak_seed = (
         a.reshape(one) for a in (pressure, plastic, viscosity, weak_seed)
     )
     three, six = (3,) + one, (6,) + one
     face = pltpu.VMEM((2, 3, 2, ROWS, 128), F32)
-    slots = pltpu.VMEM((4, 2, ROWS, 128), F32)
+    slots = pltpu.VMEM((6, 2, ROWS, 128), F32)
     level_1, level_2 = lax.axis_size(YCORE), lax.axis_size(XZ)
-    row_1, row_2 = (level_1, 1, 128), (level_2, 1, 128)
+    row_1, row_2 = (level_1, 8, 128), (level_2, 2, 128)
     x_3, z_3, x_9, z_9 = (3 * LZ, NY), (3 * LX, NY), (9 * LZ, NY), (9 * LX, NY)
 
-    first = jnp.concatenate([v[:, :LZ].reshape(x_3), plastic[: 6 * LZ]])
-    last = jnp.concatenate([v[:, ROWS - LZ :].reshape(x_3), plastic[ROWS - 6 * LZ :]])
-    x_msgs = exchange(GX, *facing(even_x(), first, last))
+    dma = pltpu.SemaphoreType.DMA
+    x_msgs = call(faces_kernel, [x_9, x_9], [v, plastic], 0, [dma((8,))], None, [HBM, HBM], 60)
+    x_msgs = exchange(GX, *x_msgs)
+    v, plastic, pressure, old, eta, weak = call(
+        load_kernel,
+        [three, one, one, six, one, one],
+        [v, plastic, pressure, old, viscosity, weak_seed],
+        10**5,
+        [pltpu.VMEM(one, F32), pltpu.VMEM(one, jnp.int32), dma((6,))],
+        None,
+        [HBM] * 6,
+    )
     along, *z_msgs = call(smooth_x_kernel, [one, z_9, z_9], [v, plastic, *x_msgs], 10**6, [slots])
     z_msgs = exchange(GZ, *z_msgs)
-    held, pres, total, eta, cohesion, row, *sent = call(
+    x_two, z_two, x_full, z_full = (2,) + x_3, (2,) + z_3, (7 * LZ, NY), (6 * LX + 8, NY)
+    part, pres, total, cohesion, vx, vz, gx, fz, row, *sent = call(
         first_kernel,
-        [six, one, one, one, one, row_1, x_3, x_3, z_3, z_3],
-        [v, pressure, old, along, plastic, viscosity, weak_seed, *x_msgs, *z_msgs],
+        [three, one, one, one, x_two, z_two, x_two, z_two, row_1, z_full, z_full],
+        [v, pressure, old, along, plastic, eta, weak, *x_msgs, *z_msgs],
         10**7,
-        [face, slots],
+        [face, slots, pltpu.VMEM(six, F32)],
     )
     row = spread(row, YCORE)
-    got = exchange(GX, *sent[:2]) + exchange(GZ, *sent[2:])
-    res, row, *sent = call(
-        residual_kernel, [three, row_2, x_3, x_3, z_3, z_3], [held, *got, row], 10**6, [face, slots]
+    z_got = exchange(GZ, *sent)
+    row, *sent = call(
+        x_pack_kernel, [row_2, x_full, x_full], [part, gx, *z_got, row], 10**5
     )
     row = spread(row, XZ)
-    got = exchange(GX, *sent[:2]) + exchange(GZ, *sent[2:])
-    stress, pres, total, v, held, row, first_top, *sent = call(
+    x_got = exchange(GX, *sent)
+    res, rx, rz = call(
+        residual_kernel, [three, x_two, z_two], [part, gx, fz, *x_got, *z_got], 10**6, [face]
+    )
+    stress, pres, total, v, held, row, gx, *sent = call(
         second_kernel,
-        [six, one, one, three, six, row_1, (1, 128), x_3, x_3, z_3, z_3],
-        [v, res, *x_msgs, *z_msgs, *got, row, old, pres, total, eta, cohesion],
+        [six, one, one, three, six, row_1, x_two, z_3, z_3],
+        [v, res, vx, vz, rx, rz, row, again, pres, total, eta, cohesion],
         10**7,
-        [face, slots],
+        [face, slots, pltpu.VMEM(z_two, F32)],
     )
     row = spread(row, YCORE)
-    got = exchange(GX, *sent[:2]) + exchange(GZ, *sent[2:])
-    (row,) = call(relay_kernel, [row_2], [row], 10**4)
+    z_got = exchange(GZ, *sent)
+    row, *sent = call(relay_kernel, [row_2, x_3, x_3], [gx, *z_got, row], 10**4)
     row = spread(row, XZ)
-    (res,) = call(last_residual_kernel, [three], [held, *got], 10**6, [face])
-    v, peaks = call(final_kernel, [three, (2,)], [v, res, row, first_top], 10**5, (), [VMEM, SMEM])
+    x_got = exchange(GX, *sent)
+    (res,) = call(last_residual_kernel, [three], [held, *x_got, *z_got], 10**6, [face])
+    v, peaks = call(final_kernel, [three, (2,)], [v, res, row], 10**5, (), [VMEM, SMEM])
     outs = [a.reshape(s) for a, s in zip((v, pres, stress, total), shapes)]
     return (*outs, peaks)
 

time: 129 us -> 111 us (0.86)
  the two profiles are of different devices: /device:TPU:6 before, /device:TPU:22 now
where the time goes in v3:
time: 111 us; the launch traced here: 110 us
  starting transfers between devices  79.9 us (72%)
  waiting for transfers between devices  10.7 us (10%)
  Pallas kernels  9.55 us (9%)
  local copies, waits for them, and re-layouts  8.55 us (8%)
    all_to_all x4, starting transfers between devices, spread(): return lax.all_to_all(row, axes, 0, 0, tiled=True)  29.8 us
    ppermute x6, starting transfers between devices, exchange(): lax.ppermute(far, axis, pairs(count, 1))  28.5 us
    ppermute x6, starting transfers between devices, exchange(): lax.ppermute(near, axis, pairs(count, 0))  21.6 us
    pallas_call x10, Pallas kernels, call(): pl.pallas_call(kernel, out_shape=[jax.ShapeDtypeStruct(s, F32) for s in o...  9.55 us
    unnamed x32, local copies, waits for them, and re-layouts  8.55 us
    ppermute x6, waiting for transfers between devices, exchange(): lax.ppermute(near, axis, pairs(count, 0))  6.43 us
    ppermute x6, waiting for transfers between devices, exchange(): lax.ppermute(far, axis, pairs(count, 1))  4.27 us
  transfers between devices with their start and end apart: 16, of which 8 were waited for; matrix products, arithmetic and copies ran while one was open for 0% of the time, Pallas kernels for 1%

profile of v3, /device:TPU:22, one launch (start us, length us, event | category | flops | bytes accessed | tf_op | source)
XLA Modules:
  0.0 109.7 jit_solution(7963372241996232698)
XLA Ops:
  0.7 1.7 %shard_map.102 = (f32[72,256]{1,0:T(8,128)}, f32[72,256]{1,0:T(8,128)}) custom-call(f32[3,128,256]{2,1,0:T(8,128)} %bitcast.12, f32[128,256]{1,0:T(8,128)} %bitcast.14), custom_call_target="tpu_custom_call" | custom-call | bytes 671744 | tf_op jit(solution)/shard_map/pallas_call | solution.py:35
  2.4 12.2 %collective-permute-start = (f32[72,256]{1,0:T(8,128)}, f32[72,256]{1,0:T(8,128)S(1)}, u32[]{:S(2)}, u32[]{:S(2)}) collective-permute-start(f32[72,256]{1,0:T(8,128)} %get-tuple-element.51), channel_id=1, source_target_pairs={{8,16},{16,8},{24,32},{32,24},{40,48},{48,40},{56,64},{64,56},{72,... | collective-permute-start | bytes 221192 | tf_op jit(solution)/shard_map/ppermute | solution.py:56
  14.6 1.9 %collective-permute-start.1 = (f32[72,256]{1,0:T(8,128)}, f32[72,256]{1,0:T(8,128)S(1)}, u32[]{:S(2)}, u32[]{:S(2)}) collective-permute-start(f32[72,256]{1,0:T(8,128)} %get-tuple-element.52), channel_id=1, source_target_pairs={{0,8},{8,0},{16,24},{24,16},{32,40},{40,32},{48,56},{56,48},{64,72... | collective-permute-start | bytes 221192 | tf_op jit(solution)/shard_map/ppermute | solution.py:57
  16.6 1.1 %copy-done = f32[6,16,8,256]{3,2,1,0:T(8,128)S(1)} copy-done((f32[6,16,8,256]{3,2,1,0:T(8,128)S(1)}, f32[6,16,8,256]{3,2,1,0:T(8,128)}, u32[]{:S(2)}) %copy-start) | copy-done | bytes 786456
  21.6 1.9 %collective-permute-start.2 = (f32[144,256]{1,0:T(8,128)S(1)}, f32[144,256]{1,0:T(8,128)S(1)}, u32[]{:S(2)}, u32[]{:S(2)}) collective-permute-start(f32[144,256]{1,0:T(8,128)S(1)} %get-tuple-element.56), channel_id=1, source_target_pairs={{1,2},{2,1},{3,4},{4,3},{5,6},{6,5},{9,10},{10,9},{11,12},{12,11},... | collective-permute-start | bytes 442376 | tf_op jit(solution)/shard_map/ppermute | solution.py:56
  23.6 4.9 %collective-permute-start.3 = (f32[144,256]{1,0:T(8,128)S(1)}, f32[144,256]{1,0:T(8,128)S(1)}, u32[]{:S(2)}, u32[]{:S(2)}) collective-permute-start(f32[144,256]{1,0:T(8,128)S(1)} %get-tuple-element.57), channel_id=1, source_target_pairs={{0,1},{1,0},{2,3},{3,2},{4,5},{5,4},{6,7},{7,6},{8,9},{9,8},{10,11... | collective-permute-start | bytes 442376 | tf_op jit(solution)/shard_map/ppermute | solution.py:57
  29.5 2.2 %shard_map.104 = (f32[3,128,256]{2,1,0:T(8,128)S(1)}, f32[128,256]{1,0:T(8,128)S(1)}, f32[128,256]{1,0:T(8,128)S(1)}, f32[128,256]{1,0:T(8,128)S(1)}, f32[2,24,2...) custom-call(f32[3,128,256]{2,1,0:T(8,128)S(1)} %get-tuple-element.47, ...), custom_call_target="tpu_custom_call" | custom-call | flops 10000000 | bytes 3637248 | tf_op jit(solution)/shard_map/pallas_call | solution.py:35
  32.3 8.9 %all-to-all-start = ((f32[16,8,128]{2,1,0:T(8,128)}), f32[16,8,128]{2,1,0:T(8,128)S(1)}, u32[]{:S(2)}, u32[]{:S(2)}) async-start(f32[16,8,128]{2,1,0:T(8,128)} %get-tuple-element.63), calls=%async_computation | async-start | bytes 131072 | tf_op jit(solution)/shard_map/all_to_all | solution.py:62
  41.2 2.0 %collective-permute-start.4 = (f32[104,256]{1,0:T(8,128)S(1)}, f32[104,256]{1,0:T(8,128)S(1)}, u32[]{:S(2)}, u32[]{:S(2)}) collective-permute-start(f32[104,256]{1,0:T(8,128)S(1)} %get-tuple-element.61), channel_id=1, source_target_pairs={{1,2},{2,1},{3,4},{4,3},{5,6},{6,5},{9,10},{10,9},{11,12},{12,11},... | collective-permute-start | bytes 319496 | tf_op jit(solution)/shard_map/ppermute | solution.py:56
  43.2 5.5 %collective-permute-start.5 = (f32[104,256]{1,0:T(8,128)S(1)}, f32[104,256]{1,0:T(8,128)S(1)}, u32[]{:S(2)}, u32[]{:S(2)}) collective-permute-start(f32[104,256]{1,0:T(8,128)S(1)} %get-tuple-element.62), channel_id=1, source_target_pairs={{0,1},{1,0},{2,3},{3,2},{4,5},{5,4},{6,7},{7,6},{8,9},{9,8},{10,11... | collective-permute-start | bytes 319496 | tf_op jit(solution)/shard_map/ppermute | solution.py:57
  50.3 6.0 %all-to-all-start.1 = ((f32[32,2,128]{2,1,0:T(2,128)}), f32[32,2,128]{2,1,0:T(2,128)S(1)}, u32[]{:S(2)}, u32[]{:S(2)}) async-start(f32[32,2,128]{2,1,0:T(2,128)} %get-tuple-element.71), calls=%async_computation.1 | async-start | bytes 65536 | tf_op jit(solution)/shard_map/all_to_all | solution.py:62
  56.3 5.5 %collective-permute-start.6 = (f32[56,256]{1,0:T(8,128)S(1)}, f32[56,256]{1,0:T(8,128)S(1)}, u32[]{:S(2)}, u32[]{:S(2)}) collective-permute-start(f32[56,256]{1,0:T(8,128)S(1)} %get-tuple-element.64), channel_id=1, source_target_pairs={{8,16},{16,8},{24,32},{32,24},{40,48},{48,40},{56,64},{64,56},{72,... | collective-permute-start | bytes 172040 | tf_op jit(solution)/shard_map/ppermute | solution.py:56
  61.8 1.9 %collective-permute-start.7 = (f32[56,256]{1,0:T(8,128)S(1)}, f32[56,256]{1,0:T(8,128)S(1)}, u32[]{:S(2)}, u32[]{:S(2)}) collective-permute-start(f32[56,256]{1,0:T(8,128)S(1)} %get-tuple-element.65), channel_id=1, source_target_pairs={{0,8},{8,0},{16,24},{24,16},{32,40},{40,32},{48,56},{56,48},{64,72... | collective-permute-start | bytes 172040 | tf_op jit(solution)/shard_map/ppermute | solution.py:57
  63.7 1.7 %collective-permute-done.6.sx_far = f32[56,256]{1,0:T(8,128)S(1)} collective-permute-done((f32[56,256]{1,0:T(8,128)S(1)}, f32[56,256]{1,0:T(8,128)S(1)}, u32[]{:S(2)}, u32[]{:S(2)}) %collective-permute-start.6) | collective-permute-done | bytes 57376 | tf_op jit(solution)/shard_map/ppermute | solution.py:56
  65.4 2.4 %collective-permute-done.7.sx_near = f32[56,256]{1,0:T(8,128)S(1)} collective-permute-done((f32[56,256]{1,0:T(8,128)S(1)}, f32[56,256]{1,0:T(8,128)S(1)}, u32[]{:S(2)}, u32[]{:S(2)}) %collective-permute-start.7) | collective-permute-done | bytes 57376 | tf_op jit(solution)/shard_map/ppermute | solution.py:57
  70.2 1.8 %shard_map.107 = (f32[6,128,256]{2,1,0:T(8,128)}, f32[128,256]{1,0:T(8,128)}, f32[128,256]{1,0:T(8,128)}, f32[3,128,256]{2,1,0:T(8,128)S(1)}, f32[6,128,256]{2,1...) custom-call(f32[3,128,256]{2,1,0:T(8,128)S(1)} %get-tuple-element.47, ...), custom_call_target="tpu_custom_call" | custom-call | flops 10000000 | bytes 4866048 | tf_op jit(solution)/shard_map/pallas_call | solution.py:35
  73.9 6.6 %all-to-all-start.2 = ((f32[16,8,128]{2,1,0:T(8,128)}), f32[16,8,128]{2,1,0:T(8,128)S(1)}, u32[]{:S(2)}, u32[]{:S(2)}) async-start(f32[16,8,128]{2,1,0:T(8,128)} %copy-done.7), calls=%async_computation.2 | async-start | bytes 131072 | tf_op jit(solution)/shard_map/all_to_all | solution.py:62
  80.5 2.0 %collective-permute-start.8 = (f32[48,256]{1,0:T(8,128)S(1)}, f32[48,256]{1,0:T(8,128)S(1)}, u32[]{:S(2)}, u32[]{:S(2)}) collective-permute-start(f32[48,256]{1,0:T(8,128)S(1)} %copy-done.15), channel_id=1, source_target_pairs={{1,2},{2,1},{3,4},{4,3},{5,6},{6,5},{9,10},{10,9},{11,12},{12,11},... | collective-permute-start | bytes 147464 | tf_op jit(solution)/shard_map/ppermute | solution.py:56
  82.5 5.5 %collective-permute-start.9 = (f32[48,256]{1,0:T(8,128)S(1)}, f32[48,256]{1,0:T(8,128)S(1)}, u32[]{:S(2)}, u32[]{:S(2)}) collective-permute-start(f32[48,256]{1,0:T(8,128)S(1)} %copy-done.13), channel_id=1, source_target_pairs={{0,1},{1,0},{2,3},{3,2},{4,5},{5,4},{6,7},{7,6},{8,9},{9,8},{10,11... | collective-permute-start | bytes 147464 | tf_op jit(solution)/shard_map/ppermute | solution.py:57
  89.5 8.3 %all-to-all-start.3 = ((f32[32,2,128]{2,1,0:T(2,128)}), f32[32,2,128]{2,1,0:T(2,128)S(1)}, u32[]{:S(2)}, u32[]{:S(2)}) async-start(f32[32,2,128]{2,1,0:T(2,128)} %get-tuple-element.83), calls=%async_computation.3 | async-start | bytes 65536 | tf_op jit(solution)/shard_map/all_to_all | solution.py:62
  97.8 4.9 %collective-permute-start.10 = (f32[24,256]{1,0:T(8,128)S(1)}, f32[24,256]{1,0:T(8,128)S(1)}, u32[]{:S(2)}, u32[]{:S(2)}) collective-permute-start(f32[24,256]{1,0:T(8,128)S(1)} %get-tuple-element.81), channel_id=1, source_target_pairs={{8,16},{16,8},{24,32},{32,24},{40,48},{48,40},{56,64},{64,56},{72,... | collective-permute-start | bytes 73736 | tf_op jit(solution)/shard_map/ppermute | solution.py:56
  102.7 1.9 %collective-permute-start.11 = (f32[24,256]{1,0:T(8,128)S(1)}, f32[24,256]{1,0:T(8,128)S(1)}, u32[]{:S(2)}, u32[]{:S(2)}) collective-permute-start(f32[24,256]{1,0:T(8,128)S(1)} %get-tuple-element.82), channel_id=1, source_target_pairs={{0,8},{8,0},{16,24},{24,16},{32,40},{40,32},{48,56},{56,48},{64,72... | collective-permute-start | bytes 73736 | tf_op jit(solution)/shard_map/ppermute | solution.py:57
  104.6 1.9 %collective-permute-done.10.sx_far = f32[24,256]{1,0:T(8,128)S(1)} collective-permute-done((f32[24,256]{1,0:T(8,128)S(1)}, f32[24,256]{1,0:T(8,128)S(1)}, u32[]{:S(2)}, u32[]{:S(2)}) %collective-permute-start.10) | collective-permute-done | bytes 24608 | tf_op jit(solution)/shard_map/ppermute | solution.py:56
  106.5 1.9 %collective-permute-done.11.sx_near = f32[24,256]{1,0:T(8,128)S(1)} collective-permute-done((f32[24,256]{1,0:T(8,128)S(1)}, f32[24,256]{1,0:T(8,128)S(1)}, u32[]{:S(2)}, u32[]{:S(2)}) %collective-permute-start.11) | collective-permute-done | bytes 24608 | tf_op jit(solution)/shard_map/ppermute | solution.py:57
  (50 shorter events, 14.0 us)
Async XLA Ops:
  0.6 15.9 %copy-start.2 = (f32[3,16,8,256]{3,2,1,0:T(8,128)S(1)}, f32[3,16,8,256]{3,2,1,0:T(8,128)}, u32[]{:S(2)}) copy-start(f32[3,16,8,256]{3,2,1,0:T(8,128)} %param.6) | copy-start | bytes 1179652
  0.6 15.9 %copy-start.3 = (f32[16,8,256]{2,1,0:T(8,128)S(1)}, f32[16,8,256]{2,1,0:T(8,128)}, u32[]{:S(2)}) copy-start(f32[16,8,256]{2,1,0:T(8,128)} %param.9) | copy-start | bytes 393220
  2.4 19.0 %collective-permute-start = (f32[72,256]{1,0:T(8,128)}, f32[72,256]{1,0:T(8,128)S(1)}, u32[]{:S(2)}, u32[]{:S(2)}) collective-permute-start(f32[72,256]{1,0:T(8,128)} %get-tuple-element.51), channel_id=1, source_target_pairs={{8,16},{16,8},{24,32},{32,24},{40,48},{48,40},{56,64},{64,56},{72,... | collective-permute-start | bytes 221192 | tf_op jit(solution)/shard_map/ppermute | solution.py:56
  14.6 6.8 %collective-permute-start.1 = (f32[72,256]{1,0:T(8,128)}, f32[72,256]{1,0:T(8,128)S(1)}, u32[]{:S(2)}, u32[]{:S(2)}) collective-permute-start(f32[72,256]{1,0:T(8,128)} %get-tuple-element.52), channel_id=1, source_target_pairs={{0,8},{8,0},{16,24},{24,16},{32,40},{40,32},{48,56},{56,48},{64,72... | collective-permute-start | bytes 221192 | tf_op jit(solution)/shard_map/ppermute | solution.py:57
  16.5 1.1 %copy-start = (f32[6,16,8,256]{3,2,1,0:T(8,128)S(1)}, f32[6,16,8,256]{3,2,1,0:T(8,128)}, u32[]{:S(2)}) copy-start(f32[6,16,8,256]{3,2,1,0:T(8,128)} %param.8) | copy-start | bytes 2359300
  17.7 0.9 copy-start.4
  18.6 0.9 copy-start.5
  21.6 7.5 %collective-permute-start.2 = (f32[144,256]{1,0:T(8,128)S(1)}, f32[144,256]{1,0:T(8,128)S(1)}, u32[]{:S(2)}, u32[]{:S(2)}) collective-permute-start(f32[144,256]{1,0:T(8,128)S(1)} %get-tuple-element.56), channel_id=1, source_target_pairs={{1,2},{2,1},{3,4},{4,3},{5,6},{6,5},{9,10},{10,9},{11,12},{12,11},... | collective-permute-start | bytes 442376 | tf_op jit(solution)/shard_map/ppermute | solution.py:56
  23.6 5.9 %collective-permute-start.3 = (f32[144,256]{1,0:T(8,128)S(1)}, f32[144,256]{1,0:T(8,128)S(1)}, u32[]{:S(2)}, u32[]{:S(2)}) collective-permute-start(f32[144,256]{1,0:T(8,128)S(1)} %get-tuple-element.57), channel_id=1, source_target_pairs={{0,1},{1,0},{2,3},{3,2},{4,5},{5,4},{6,7},{7,6},{8,9},{9,8},{10,11... | collective-permute-start | bytes 442376 | tf_op jit(solution)/shard_map/ppermute | solution.py:57
  32.3 17.4 %all-to-all-start = ((f32[16,8,128]{2,1,0:T(8,128)}), f32[16,8,128]{2,1,0:T(8,128)S(1)}, u32[]{:S(2)}, u32[]{:S(2)}) async-start(f32[16,8,128]{2,1,0:T(8,128)} %get-tuple-element.63), calls=%async_computation | async-start | bytes 131072 | tf_op jit(solution)/shard_map/all_to_all | solution.py:62
  41.2 7.5 %collective-permute-start.4 = (f32[104,256]{1,0:T(8,128)S(1)}, f32[104,256]{1,0:T(8,128)S(1)}, u32[]{:S(2)}, u32[]{:S(2)}) collective-permute-start(f32[104,256]{1,0:T(8,128)S(1)} %get-tuple-element.61), channel_id=1, source_target_pairs={{1,2},{2,1},{3,4},{4,3},{5,6},{6,5},{9,10},{10,9},{11,12},{12,11},... | collective-permute-start | bytes 319496 | tf_op jit(solution)/shard_map/ppermute | solution.py:56
  43.2 6.4 %collective-permute-start.5 = (f32[104,256]{1,0:T(8,128)S(1)}, f32[104,256]{1,0:T(8,128)S(1)}, u32[]{:S(2)}, u32[]{:S(2)}) collective-permute-start(f32[104,256]{1,0:T(8,128)S(1)} %get-tuple-element.62), channel_id=1, source_target_pairs={{0,1},{1,0},{2,3},{3,2},{4,5},{5,4},{6,7},{7,6},{8,9},{9,8},{10,11... | collective-permute-start | bytes 319496 | tf_op jit(solution)/shard_map/ppermute | solution.py:57
  49.6 19.0 %copy-start.1 = (f32[6,16,8,256]{3,2,1,0:T(8,128)S(1)}, f32[6,16,8,256]{3,2,1,0:T(8,128)}, u32[]{:S(2)}) copy-start(f32[6,16,8,256]{3,2,1,0:T(8,128)} %param.8) | copy-start | bytes 2359300
  50.3 18.4 %all-to-all-start.1 = ((f32[32,2,128]{2,1,0:T(2,128)}), f32[32,2,128]{2,1,0:T(2,128)S(1)}, u32[]{:S(2)}, u32[]{:S(2)}) async-start(f32[32,2,128]{2,1,0:T(2,128)} %get-tuple-element.71), calls=%async_computation.1 | async-start | bytes 65536 | tf_op jit(solution)/shard_map/all_to_all | solution.py:62
  56.3 9.2 %collective-permute-start.6 = (f32[56,256]{1,0:T(8,128)S(1)}, f32[56,256]{1,0:T(8,128)S(1)}, u32[]{:S(2)}, u32[]{:S(2)}) collective-permute-start(f32[56,256]{1,0:T(8,128)S(1)} %get-tuple-element.64), channel_id=1, source_target_pairs={{8,16},{16,8},{24,32},{32,24},{40,48},{48,40},{56,64},{64,56},{72,... | collective-permute-start | bytes 172040 | tf_op jit(solution)/shard_map/ppermute | solution.py:56
  61.8 6.1 %collective-permute-start.7 = (f32[56,256]{1,0:T(8,128)S(1)}, f32[56,256]{1,0:T(8,128)S(1)}, u32[]{:S(2)}, u32[]{:S(2)}) collective-permute-start(f32[56,256]{1,0:T(8,128)S(1)} %get-tuple-element.65), channel_id=1, source_target_pairs={{0,8},{8,0},{16,24},{24,16},{32,40},{40,32},{48,56},{56,48},{64,72... | collective-permute-start | bytes 172040 | tf_op jit(solution)/shard_map/ppermute | solution.py:57
  73.9 6.6 %copy-start.15 = (f32[48,256]{1,0:T(8,128)S(1)}, f32[48,256]{1,0:T(8,128)}, u32[]{:S(2)}) copy-start(f32[48,256]{1,0:T(8,128)} %copy-done.14) | copy-start | bytes 147460
  73.9 8.6 %copy-start.13 = (f32[48,256]{1,0:T(8,128)S(1)}, f32[48,256]{1,0:T(8,128)}, u32[]{:S(2)}) copy-start(f32[48,256]{1,0:T(8,128)} %copy-done.12) | copy-start | bytes 147460
  73.9 15.0 %all-to-all-start.2 = ((f32[16,8,128]{2,1,0:T(8,128)}), f32[16,8,128]{2,1,0:T(8,128)S(1)}, u32[]{:S(2)}, u32[]{:S(2)}) async-start(f32[16,8,128]{2,1,0:T(8,128)} %copy-done.7), calls=%async_computation.2 | async-start | bytes 131072 | tf_op jit(solution)/shard_map/all_to_all | solution.py:62
  80.5 7.5 %collective-permute-start.8 = (f32[48,256]{1,0:T(8,128)S(1)}, f32[48,256]{1,0:T(8,128)S(1)}, u32[]{:S(2)}, u32[]{:S(2)}) collective-permute-start(f32[48,256]{1,0:T(8,128)S(1)} %copy-done.15), channel_id=1, source_target_pairs={{1,2},{2,1},{3,4},{4,3},{5,6},{6,5},{9,10},{10,9},{11,12},{12,11},... | collective-permute-start | bytes 147464 | tf_op jit(solution)/shard_map/ppermute | solution.py:56
  82.5 6.3 %collective-permute-start.9 = (f32[48,256]{1,0:T(8,128)S(1)}, f32[48,256]{1,0:T(8,128)S(1)}, u32[]{:S(2)}, u32[]{:S(2)}) collective-permute-start(f32[48,256]{1,0:T(8,128)S(1)} %copy-done.13), channel_id=1, source_target_pairs={{0,1},{1,0},{2,3},{3,2},{4,5},{5,4},{6,7},{7,6},{8,9},{9,8},{10,11... | collective-permute-start | bytes 147464 | tf_op jit(solution)/shard_map/ppermute | solution.py:57
  89.5 19.2 %all-to-all-start.3 = ((f32[32,2,128]{2,1,0:T(2,128)}), f32[32,2,128]{2,1,0:T(2,128)S(1)}, u32[]{:S(2)}, u32[]{:S(2)}) async-start(f32[32,2,128]{2,1,0:T(2,128)} %get-tuple-element.83), calls=%async_computation.3 | async-start | bytes 65536 | tf_op jit(solution)/shard_map/all_to_all | solution.py:62
  97.8 8.7 %collective-permute-start.10 = (f32[24,256]{1,0:T(8,128)S(1)}, f32[24,256]{1,0:T(8,128)S(1)}, u32[]{:S(2)}, u32[]{:S(2)}) collective-permute-start(f32[24,256]{1,0:T(8,128)S(1)} %get-tuple-element.81), channel_id=1, source_target_pairs={{8,16},{16,8},{24,32},{32,24},{40,48},{48,40},{56,64},{64,56},{72,... | collective-permute-start | bytes 73736 | tf_op jit(solution)/shard_map/ppermute | solution.py:56
  102.7 5.7 %collective-permute-start.11 = (f32[24,256]{1,0:T(8,128)S(1)}, f32[24,256]{1,0:T(8,128)S(1)}, u32[]{:S(2)}, u32[]{:S(2)}) collective-permute-start(f32[24,256]{1,0:T(8,128)S(1)} %get-tuple-element.82), channel_id=1, source_target_pairs={{0,8},{8,0},{16,24},{24,16},{32,40},{40,32},{48,56},{56,48},{64,72... | collective-permute-start | bytes 73736 | tf_op jit(solution)/shard_map/ppermute | solution.py:57
  (8 other events, 5.6 us)

commit v4 on v3

--- a/solution.py
+++ b/solution.py
@@ -179,21 +179,9 @@
         pltpu.make_async_copy(plastic.at[pl.ds(0, 6 * LZ)], out.at[rows], sem.at[4 * i + 3]).wait()
 
 
-def load_kernel(
-    v_in, plastic_in, pressure_in, old_in, viscosity_in, seed_in,
-    v, plastic, pressure, old, eta, weak, viscosity, seed, sem,
-):
-    ins = (viscosity_in, seed_in, v_in, plastic_in, pressure_in, old_in)
-    outs = (viscosity, seed, v, plastic, pressure, old)
-    copies = [pltpu.make_async_copy(a, b, sem.at[i]) for i, (a, b) in enumerate(zip(ins, outs))]
-    for copy in copies:
-        copy.start()
-    copies[0].wait()
+def eta_kernel(viscosity, seed, eta, weak):
     eta[...] = 1.0 / (1.0 / viscosity[...] + 1.0 / SHEAR)
-    copies[1].wait()
     weak[...] = 1.0 - 0.6 * seed[...].astype(F32)
-    for copy in copies[2:]:
-        copy.wait()
 
 
 def store_row(out, top_yield, top_eta, earlier=None):
@@ -244,13 +232,58 @@
     return pres, [t * shrink for t in trial], eta * shrink, yield_f, dlam
 
 
-def smooth_x_kernel(v, plastic, x_far, x_near, along, z_far, z_near, slots):
-    even = even_x()
-    low, high = sides(even, x_far[3 * LZ :], x_near[3 * LZ :])
-    padded = jnp.concatenate([low, plastic[...], high], axis=0)
-    total = WEIGHTS[0] * padded[0:ROWS]
-    for k in range(1, 13):
-        total = total + WEIGHTS[k] * padded[k * LZ : k * LZ + ROWS]
+def partial_residual(held, part, masks):
+    nothing = jnp.zeros((LZ, NY), F32)
+    for start in range(0, ROWS, CHUNK):
+        here = slice(start, start + CHUNK)
+        for f in range(3):
+            part[f, here] = (
+                diff_x(held, ALONG_X[f], start, nothing, nothing)
+                + diff_z(held[ALONG_Z[f], here], 0.0, 0.0, masks)
+                + diff_y(held[ALONG_Y[f], here], masks)
+            )
+
+
+def whole_residual(part, x_low, x_high, z_low, z_high, face, masks):
+    for f in range(3):
+        rows = slice(f * LX, (f + 1) * LX)
+        spread_rows(face, f, z_low[rows], z_high[rows])
+        slab = slice(f * LZ, (f + 1) * LZ)
+        for start in range(0, ROWS, CHUNK):
+            here = slice(start, start + CHUNK)
+            value = (
+                part[f, here]
+                - jnp.where(masks[0], face_rows(face, 0, f, here) * 0.5, 0.0)
+                + jnp.where(masks[1], face_rows(face, 1, f, here) * 0.5, 0.0)
+            )
+            if start == 0:
+                value = jnp.concatenate([value[:LZ] - x_low[slab] * 0.5, value[LZ:]], axis=0)
+            if start == ROWS - CHUNK:
+                value = jnp.concatenate([value[:LZ], value[LZ:] + x_high[slab] * 0.5], axis=0)
+            yield f, here, value
+
+
+def own_x_kernel(plastic, along):
+    for x in range(LX):
+        total = None
+        for k in range(max(-6, -x), min(6, LX - 1 - x) + 1):
+            term = WEIGHTS[k + 6] * plastic[(x + k) * LZ : (x + k + 1) * LZ]
+            total = term if total is None else total + term
+        along[x * LZ : (x + 1) * LZ] = total
+
+
+def smooth_x_kernel(v, own, x_far, x_near, along, z_far, z_near, slots):
+    low, high = sides(even_x(), x_far[3 * LZ :], x_near[3 * LZ :])
+    layers = []
+    for x in range(LX):
+        total = own[x * LZ : (x + 1) * LZ]
+        for j in range(6):
+            if x + 6 - j <= 6:
+                total = total + WEIGHTS[j - x] * low[j * LZ : (j + 1) * LZ]
+            if LX + j - x <= 6:
+                total = total + WEIGHTS[LX + j - x + 6] * high[j * LZ : (j + 1) * LZ]
+        layers.append(total)
+    total = jnp.concatenate(layers, axis=0)
     along[...] = total
     keep(slots, 3, total)
     even = even_z()
@@ -320,15 +353,7 @@
         top_yield = jnp.maximum(top_yield, yield_f)
         top_eta = jnp.maximum(top_eta, eta_shrink)
     store_row(row_out, top_yield, top_eta)
-    nothing = jnp.zeros((LZ, NY), F32)
-    for start in range(0, ROWS, CHUNK):
-        here = slice(start, start + CHUNK)
-        for f in range(3):
-            part[f, here] = (
-                diff_x(held, ALONG_X[f], start, nothing, nothing)
-                + diff_z(held[ALONG_Z[f], here], 0.0, 0.0, masks)
-                + diff_y(held[ALONG_Y[f], here], masks)
-            )
+    partial_residual(held, part, masks)
     x_faces(held, ALONG_X, gx)
     z_faces(held, ALONG_Z, fz, slots)
     even = even_z()
@@ -345,24 +370,6 @@
         corners.append(jnp.concatenate(ends + ends, axis=0))
     a, b = facing(even, *corners)
     sz_far[6 * LX :], sz_near[6 * LX :] = a, b
-
-
-def residual(held, x_far, x_near, z_far, z_near, out, face):
-    x_low, x_high = sides(even_x(), x_far[...], x_near[...])
-    z_low, z_high = sides(even_z(), z_far[...], z_near[...])
-    for f in range(3):
-        rows = slice(f * LX, (f + 1) * LX)
-        spread_rows(face, f, z_low[rows], z_high[rows])
-    masks = iotas()
-    for start in range(0, ROWS, CHUNK):
-        here = slice(start, start + CHUNK)
-        for f in range(3):
-            slab = slice(f * LZ, (f + 1) * LZ)
-            out[f, here] = (
-                diff_x(held, ALONG_X[f], start, x_low[slab], x_high[slab])
-                + diff_z(held[ALONG_Z[f], here], face_rows(face, 0, f, here), face_rows(face, 1, f, here), masks)
-                + diff_y(held[ALONG_Y[f], here], masks)
-            )
 
 
 def x_pack_kernel(part, gx, sz_far, sz_near, row, row_out, sx_far, sx_near):
@@ -390,20 +397,8 @@
 def residual_kernel(part, gx, fz, sx_far, sx_near, sz_far, sz_near, out, rx, rz, face):
     x_low, x_high = sides(even_x(), sx_far[...], sx_near[...])
     z_low, z_high = sides(even_z(), sz_far[...], sz_near[...])
-    masks = iotas()
-    for f in range(3):
-        rows = slice(f * LX, (f + 1) * LX)
-        spread_rows(face, f, z_low[rows], z_high[rows])
-        slab = slice(f * LZ, (f + 1) * LZ)
-        for start in range(0, ROWS, CHUNK):
-            here = slice(start, start + CHUNK)
-            out[f, here] = (
-                part[f, here]
-                - jnp.where(masks[0], face_rows(face, 0, f, here) * 0.5, 0.0)
-                + jnp.where(masks[1], face_rows(face, 1, f, here) * 0.5, 0.0)
-            )
-        out[f, 0:LZ] = out[f, 0:LZ] - x_low[slab] * 0.5
-        out[f, ROWS - LZ : ROWS] = out[f, ROWS - LZ : ROWS] + x_high[slab] * 0.5
+    for f, here, value in whole_residual(part, x_low, x_high, z_low, z_high, face, iotas()):
+        out[f, here] = value
     has_low, has_high = place(GX)
     rx[0] = jnp.where(has_low, x_low[3 * LZ : 6 * LZ] + gx[0] * 0.5, 0.0)
     rx[1] = jnp.where(has_high, x_high[3 * LZ : 6 * LZ] - gx[1] * 0.5, 0.0)
@@ -421,10 +416,6 @@
             rz[side, rows] = jnp.where(has, value, 0.0)
 
 
-def last_residual_kernel(held, sx_far, sx_near, sz_far, sz_near, out, face):
-    residual(held, sx_far, sx_near, sz_far, sz_near, out, face)
-
-
 def relay_kernel(gx, sz_far, sz_near, row, row_out, sx_far, sx_near):
     relay_row(row, row_out)
     sx_far[...], sx_near[...] = facing(even_x(), gx[0], gx[1])
@@ -433,8 +424,8 @@
 def second_kernel(
     v, res, vx, vz, rx, rz, row,
     old, pressure, plastic, eta_in, cohesion,
-    stress, pres, total, v_out, held, row_out, gx, sz_far, sz_near,
-    face, slots, fz,
+    stress, pres, total, v_out, part, row_out, gx, sz_far, sz_near,
+    face, slots, fz, held,
 ):
     top, peak = row_values(row, (0, 1))
     step = 0.125 / peak
@@ -468,16 +459,18 @@
         top_yield = jnp.maximum(top_yield, yield_f)
         top_eta = jnp.maximum(top_eta, eta_shrink)
     store_row(row_out, top_yield, top_eta, top)
+    partial_residual(held, part, masks)
     x_faces(held, ALONG_X, gx)
     z_faces(held, ALONG_Z, fz, slots)
     sz_far[...], sz_near[...] = facing(even_z(), fz[0], fz[1])
 
 
-def final_kernel(v, res, row, v_out, peaks):
+def final_kernel(v, part, sx_far, sx_near, sz_far, sz_near, row, v_out, peaks, face):
     top, peak, first_top = row_values(row, (0, 1, 2))
     step = 0.125 / peak
-    for f in range(3):
-        v_out[f] = v[f] + step * res[f]
+    slabs = sides(even_x(), sx_far[...], sx_near[...]) + sides(even_z(), sz_far[...], sz_near[...])
+    for f, here, value in whole_residual(part, *slabs, face, iotas()):
+        v_out[f, here] = v[f, here] + step * value
     peaks[0] = jnp.max(first_top)
     peaks[1] = jnp.max(top)
 
@@ -486,7 +479,7 @@
     shapes = [a.shape for a in (velocity, pressure, stress_old, plastic)]
     one = (ROWS, NY)
     v = velocity.reshape((3,) + one)
-    old = again = stress_old.reshape((6,) + one)
+    old = stress_old.reshape((6,) + one)
     pressure, plastic, viscosity, weak_seed = (
         a.reshape(one) for a in (pressure, plastic, viscosity, weak_seed)
     )
@@ -498,18 +491,11 @@
     x_3, z_3, x_9, z_9 = (3 * LZ, NY), (3 * LX, NY), (9 * LZ, NY), (9 * LX, NY)
 
     dma = pltpu.SemaphoreType.DMA
-    x_msgs = call(faces_kernel, [x_9, x_9], [v, plastic], 0, [dma((8,))], None, [HBM, HBM], 60)
+    x_msgs = call(faces_kernel, [x_9, x_9], [v, plastic], 0, [dma((8,))], [HBM, HBM], [HBM, HBM], 60)
     x_msgs = exchange(GX, *x_msgs)
-    v, plastic, pressure, old, eta, weak = call(
-        load_kernel,
-        [three, one, one, six, one, one],
-        [v, plastic, pressure, old, viscosity, weak_seed],
-        10**5,
-        [pltpu.VMEM(one, F32), pltpu.VMEM(one, jnp.int32), dma((6,))],
-        None,
-        [HBM] * 6,
-    )
-    along, *z_msgs = call(smooth_x_kernel, [one, z_9, z_9], [v, plastic, *x_msgs], 10**6, [slots])
+    eta, weak = call(eta_kernel, [one, one], [viscosity, weak_seed], 10**5)
+    (along,) = call(own_x_kernel, [one], [plastic], 10**6)
+    along, *z_msgs = call(smooth_x_kernel, [one, z_9, z_9], [v, along, *x_msgs], 10**6, [slots])
     z_msgs = exchange(GZ, *z_msgs)
     x_two, z_two, x_full, z_full = (2,) + x_3, (2,) + z_3, (7 * LZ, NY), (6 * LX + 8, NY)
     part, pres, total, cohesion, vx, vz, gx, fz, row, *sent = call(
@@ -529,20 +515,26 @@
     res, rx, rz = call(
         residual_kernel, [three, x_two, z_two], [part, gx, fz, *x_got, *z_got], 10**6, [face]
     )
-    stress, pres, total, v, held, row, gx, *sent = call(
+    stress, pres, total, v, part, row, gx, *sent = call(
         second_kernel,
-        [six, one, one, three, six, row_1, x_two, z_3, z_3],
-        [v, res, vx, vz, rx, rz, row, again, pres, total, eta, cohesion],
+        [six, one, one, three, three, row_1, x_two, z_3, z_3],
+        [v, res, vx, vz, rx, rz, row, old, pres, total, eta, cohesion],
         10**7,
-        [face, slots, pltpu.VMEM(z_two, F32)],
+        [face, slots, pltpu.VMEM(z_two, F32), pltpu.VMEM(six, F32)],
     )
     row = spread(row, YCORE)
     z_got = exchange(GZ, *sent)
     row, *sent = call(relay_kernel, [row_2, x_3, x_3], [gx, *z_got, row], 10**4)
     row = spread(row, XZ)
     x_got = exchange(GX, *sent)
-    (res,) = call(last_residual_kernel, [three], [held, *x_got, *z_got], 10**6, [face])
-    v, peaks = call(final_kernel, [three, (2,)], [v, res, row], 10**5, (), [VMEM, SMEM])
+    v, peaks = call(
+        final_kernel,
+        [three, (2,)],
+        [v, part, *x_got, *z_got, row],
+        10**6,
+        [face],
+        [VMEM, SMEM],
+    )
     outs = [a.reshape(s) for a, s in zip((v, pres, stress, total), shapes)]
     return (*outs, peaks)
 

time: 111 us -> 108 us (0.973)
  local copies, waits for them, and re-layouts: 8.55 us -> 0.93 us
  waiting for transfers between devices: 10.7 us -> 14.1 us
  Pallas kernels: 9.55 us -> 12.4 us
    unnamed x32 -> x14, local copies, waits for them, and re-layouts: 8.55 us -> 0.93 us
    ppermute x6, waiting for transfers between devices: 6.43 us -> 9.92 us  [exchange(): lax.ppermute(near, axis, pairs(count, 0))]
    pallas_call x10, Pallas kernels: 9.55 us -> 12.4 us  [call(): pl.pallas_call(kernel, out_shape=[jax.ShapeDtypeStruct(s, F32) for s in o...]
  transfers between devices with their start and end apart: 16 -> 16, of which waited for: 8 -> 9; matrix products, arithmetic and copies ran while one was open for 0% -> 0% of each run, Pallas kernels for 1% -> 0%
where the time goes in v4:
time: 108 us; the launch traced here: 107 us
  starting transfers between devices  78.9 us (73%)
  waiting for transfers between devices  14.1 us (13%)
  Pallas kernels  12.4 us (11%)
    all_to_all x4, starting transfers between devices, spread(): return lax.all_to_all(row, axes, 0, 0, tiled=True)  28.8 us
    ppermute x6, starting transfers between devices, exchange(): lax.ppermute(far, axis, pairs(count, 1))  28.5 us
    ppermute x6, starting transfers between devices, exchange(): lax.ppermute(near, axis, pairs(count, 0))  21.6 us
    pallas_call x10, Pallas kernels, call(): pl.pallas_call(kernel, out_shape=[jax.ShapeDtypeStruct(s, F32) for s in o...  12.4 us
    ppermute x6, waiting for transfers between devices, exchange(): lax.ppermute(near, axis, pairs(count, 0))  9.92 us
    ppermute x6, waiting for transfers between devices, exchange(): lax.ppermute(far, axis, pairs(count, 1))  4.18 us
  transfers between devices with their start and end apart: 16, of which 9 were waited for; matrix products, arithmetic and copies ran while one was open for 0% of the time, Pallas kernels for 0%

profile of v4, /device:TPU:22, one launch (start us, length us, event | category | flops | bytes accessed | tf_op | source)
XLA Modules:
  0.0 107.3 jit_solution(5284727502655385418)
XLA Ops:
  0.7 5.7 %shard_map.102 = (f32[72,256]{1,0:T(8,128)}, f32[72,256]{1,0:T(8,128)}) custom-call(f32[3,128,256]{2,1,0:T(8,128)} %bitcast.10, f32[128,256]{1,0:T(8,128)} %bitcast.16), custom_call_target="tpu_custom_call" | custom-call | bytes 671744 | tf_op jit(solution)/shard_map/pallas_call | solution.py:35
  6.4 12.2 %collective-permute-start = (f32[72,256]{1,0:T(8,128)}, f32[72,256]{1,0:T(8,128)S(1)}, u32[]{:S(2)}, u32[]{:S(2)}) collective-permute-start(f32[72,256]{1,0:T(8,128)} %get-tuple-element.43), channel_id=1, source_target_pairs={{8,16},{16,8},{24,32},{32,24},{40,48},{48,40},{56,64},{64,56},{72,... | collective-permute-start | bytes 221192 | tf_op jit(solution)/shard_map/ppermute | solution.py:56
  18.6 1.9 %collective-permute-start.1 = (f32[72,256]{1,0:T(8,128)}, f32[72,256]{1,0:T(8,128)S(1)}, u32[]{:S(2)}, u32[]{:S(2)}) collective-permute-start(f32[72,256]{1,0:T(8,128)} %get-tuple-element.44), channel_id=1, source_target_pairs={{0,8},{8,0},{16,24},{24,16},{32,40},{40,32},{48,56},{56,48},{64,72... | collective-permute-start | bytes 221192 | tf_op jit(solution)/shard_map/ppermute | solution.py:57
  21.5 3.5 %collective-permute-done.1.x_near = f32[72,256]{1,0:T(8,128)S(1)} collective-permute-done((f32[72,256]{1,0:T(8,128)}, f32[72,256]{1,0:T(8,128)S(1)}, u32[]{:S(2)}, u32[]{:S(2)}) %collective-permute-start.1) | collective-permute-done | bytes 73760 | tf_op jit(solution)/shard_map/ppermute | solution.py:57
  25.1 1.9 %collective-permute-start.2 = (f32[144,256]{1,0:T(8,128)S(1)}, f32[144,256]{1,0:T(8,128)S(1)}, u32[]{:S(2)}, u32[]{:S(2)}) collective-permute-start(f32[144,256]{1,0:T(8,128)S(1)} %get-tuple-element.48), channel_id=1, source_target_pairs={{1,2},{2,1},{3,4},{4,3},{5,6},{6,5},{9,10},{10,9},{11,12},{12,11},... | collective-permute-start | bytes 442376 | tf_op jit(solution)/shard_map/ppermute | solution.py:56
  27.1 4.9 %collective-permute-start.3 = (f32[144,256]{1,0:T(8,128)S(1)}, f32[144,256]{1,0:T(8,128)S(1)}, u32[]{:S(2)}, u32[]{:S(2)}) collective-permute-start(f32[144,256]{1,0:T(8,128)S(1)} %get-tuple-element.49), channel_id=1, source_target_pairs={{0,1},{1,0},{2,3},{3,2},{4,5},{5,4},{6,7},{7,6},{8,9},{9,8},{10,11... | collective-permute-start | bytes 442376 | tf_op jit(solution)/shard_map/ppermute | solution.py:57
  33.0 2.2 %shard_map.105 = (f32[3,128,256]{2,1,0:T(8,128)S(1)}, f32[128,256]{1,0:T(8,128)S(1)}, f32[128,256]{1,0:T(8,128)S(1)}, f32[128,256]{1,0:T(8,128)S(1)}, f32[2,24,2...) custom-call(f32[3,128,256]{2,1,0:T(8,128)S(1)} %bitcast.12, ...), custom_call_target="tpu_custom_call" | custom-call | flops 10000000 | bytes 3637248 | tf_op jit(solution)/shard_map/pallas_call | solution.py:35
  35.2 7.4 %all-to-all-start = ((f32[16,8,128]{2,1,0:T(8,128)}), f32[16,8,128]{2,1,0:T(8,128)S(1)}, u32[]{:S(2)}, u32[]{:S(2)}) async-start(f32[16,8,128]{2,1,0:T(8,128)} %get-tuple-element.55), calls=%async_computation | async-start | bytes 131072 | tf_op jit(solution)/shard_map/all_to_all | solution.py:62
  42.6 2.0 %collective-permute-start.4 = (f32[104,256]{1,0:T(8,128)S(1)}, f32[104,256]{1,0:T(8,128)S(1)}, u32[]{:S(2)}, u32[]{:S(2)}) collective-permute-start(f32[104,256]{1,0:T(8,128)S(1)} %get-tuple-element.53), channel_id=1, source_target_pairs={{1,2},{2,1},{3,4},{4,3},{5,6},{6,5},{9,10},{10,9},{11,12},{12,11},... | collective-permute-start | bytes 319496 | tf_op jit(solution)/shard_map/ppermute | solution.py:56
  44.6 5.5 %collective-permute-start.5 = (f32[104,256]{1,0:T(8,128)S(1)}, f32[104,256]{1,0:T(8,128)S(1)}, u32[]{:S(2)}, u32[]{:S(2)}) collective-permute-start(f32[104,256]{1,0:T(8,128)S(1)} %get-tuple-element.54), channel_id=1, source_target_pairs={{0,1},{1,0},{2,3},{3,2},{4,5},{5,4},{6,7},{7,6},{8,9},{9,8},{10,11... | collective-permute-start | bytes 319496 | tf_op jit(solution)/shard_map/ppermute | solution.py:57
  51.7 6.6 %all-to-all-start.1 = ((f32[32,2,128]{2,1,0:T(2,128)}), f32[32,2,128]{2,1,0:T(2,128)S(1)}, u32[]{:S(2)}, u32[]{:S(2)}) async-start(f32[32,2,128]{2,1,0:T(2,128)} %get-tuple-element.63), calls=%async_computation.1 | async-start | bytes 65536 | tf_op jit(solution)/shard_map/all_to_all | solution.py:62
  58.3 5.5 %collective-permute-start.6 = (f32[56,256]{1,0:T(8,128)S(1)}, f32[56,256]{1,0:T(8,128)S(1)}, u32[]{:S(2)}, u32[]{:S(2)}) collective-permute-start(f32[56,256]{1,0:T(8,128)S(1)} %get-tuple-element.56), channel_id=1, source_target_pairs={{8,16},{16,8},{24,32},{32,24},{40,48},{48,40},{56,64},{64,56},{72,... | collective-permute-start | bytes 172040 | tf_op jit(solution)/shard_map/ppermute | solution.py:56
  63.8 1.9 %collective-permute-start.7 = (f32[56,256]{1,0:T(8,128)S(1)}, f32[56,256]{1,0:T(8,128)S(1)}, u32[]{:S(2)}, u32[]{:S(2)}) collective-permute-start(f32[56,256]{1,0:T(8,128)S(1)} %get-tuple-element.57), channel_id=1, source_target_pairs={{0,8},{8,0},{16,24},{24,16},{32,40},{40,32},{48,56},{56,48},{64,72... | collective-permute-start | bytes 172040 | tf_op jit(solution)/shard_map/ppermute | solution.py:57
  65.7 1.7 %collective-permute-done.6.sx_far = f32[56,256]{1,0:T(8,128)S(1)} collective-permute-done((f32[56,256]{1,0:T(8,128)S(1)}, f32[56,256]{1,0:T(8,128)S(1)}, u32[]{:S(2)}, u32[]{:S(2)}) %collective-permute-start.6) | collective-permute-done | bytes 57376 | tf_op jit(solution)/shard_map/ppermute | solution.py:56
  67.4 2.4 %collective-permute-done.7.sx_near = f32[56,256]{1,0:T(8,128)S(1)} collective-permute-done((f32[56,256]{1,0:T(8,128)S(1)}, f32[56,256]{1,0:T(8,128)S(1)}, u32[]{:S(2)}, u32[]{:S(2)}) %collective-permute-start.7) | collective-permute-done | bytes 57376 | tf_op jit(solution)/shard_map/ppermute | solution.py:57
  70.0 2.0 %shard_map.108 = (f32[6,128,256]{2,1,0:T(8,128)}, f32[128,256]{1,0:T(8,128)}, f32[128,256]{1,0:T(8,128)}, f32[3,128,256]{2,1,0:T(8,128)S(1)}, f32[3,128,256]{2,1...) custom-call(f32[3,128,256]{2,1,0:T(8,128)S(1)} %bitcast.13, ...), custom_call_target="tpu_custom_call" | custom-call | flops 10000000 | bytes 4472832 | tf_op jit(solution)/shard_map/pallas_call | solution.py:35
  72.0 6.4 %all-to-all-start.2 = ((f32[16,8,128]{2,1,0:T(8,128)}), f32[16,8,128]{2,1,0:T(8,128)S(1)}, u32[]{:S(2)}, u32[]{:S(2)}) async-start(f32[16,8,128]{2,1,0:T(8,128)} %get-tuple-element.72), calls=%async_computation.2 | async-start | bytes 131072 | tf_op jit(solution)/shard_map/all_to_all | solution.py:62
  78.4 2.0 %collective-permute-start.8 = (f32[48,256]{1,0:T(8,128)S(1)}, f32[48,256]{1,0:T(8,128)S(1)}, u32[]{:S(2)}, u32[]{:S(2)}) collective-permute-start(f32[48,256]{1,0:T(8,128)S(1)} %get-tuple-element.70), channel_id=1, source_target_pairs={{1,2},{2,1},{3,4},{4,3},{5,6},{6,5},{9,10},{10,9},{11,12},{12,11},... | collective-permute-start | bytes 147464 | tf_op jit(solution)/shard_map/ppermute | solution.py:56
  80.5 5.5 %collective-permute-start.9 = (f32[48,256]{1,0:T(8,128)S(1)}, f32[48,256]{1,0:T(8,128)S(1)}, u32[]{:S(2)}, u32[]{:S(2)}) collective-permute-start(f32[48,256]{1,0:T(8,128)S(1)} %get-tuple-element.71), channel_id=1, source_target_pairs={{0,1},{1,0},{2,3},{3,2},{4,5},{5,4},{6,7},{7,6},{8,9},{9,8},{10,11... | collective-permute-start | bytes 147464 | tf_op jit(solution)/shard_map/ppermute | solution.py:57
  87.4 8.3 %all-to-all-start.3 = ((f32[32,2,128]{2,1,0:T(2,128)}), f32[32,2,128]{2,1,0:T(2,128)S(1)}, u32[]{:S(2)}, u32[]{:S(2)}) async-start(f32[32,2,128]{2,1,0:T(2,128)} %get-tuple-element.75), calls=%async_computation.3 | async-start | bytes 65536 | tf_op jit(solution)/shard_map/all_to_all | solution.py:62
  95.8 4.9 %collective-permute-start.10 = (f32[24,256]{1,0:T(8,128)S(1)}, f32[24,256]{1,0:T(8,128)S(1)}, u32[]{:S(2)}, u32[]{:S(2)}) collective-permute-start(f32[24,256]{1,0:T(8,128)S(1)} %get-tuple-element.73), channel_id=1, source_target_pairs={{8,16},{16,8},{24,32},{32,24},{40,48},{48,40},{56,64},{64,56},{72,... | collective-permute-start | bytes 73736 | tf_op jit(solution)/shard_map/ppermute | solution.py:56
  100.6 1.9 %collective-permute-start.11 = (f32[24,256]{1,0:T(8,128)S(1)}, f32[24,256]{1,0:T(8,128)S(1)}, u32[]{:S(2)}, u32[]{:S(2)}) collective-permute-start(f32[24,256]{1,0:T(8,128)S(1)} %get-tuple-element.74), channel_id=1, source_target_pairs={{0,8},{8,0},{16,24},{24,16},{32,40},{40,32},{48,56},{56,48},{64,72... | collective-permute-start | bytes 73736 | tf_op jit(solution)/shard_map/ppermute | solution.py:57
  102.6 1.9 %collective-permute-done.10.sx_far = f32[24,256]{1,0:T(8,128)S(1)} collective-permute-done((f32[24,256]{1,0:T(8,128)S(1)}, f32[24,256]{1,0:T(8,128)S(1)}, u32[]{:S(2)}, u32[]{:S(2)}) %collective-permute-start.10) | collective-permute-done | bytes 24608 | tf_op jit(solution)/shard_map/ppermute | solution.py:56
  104.5 1.9 %collective-permute-done.11.sx_near = f32[24,256]{1,0:T(8,128)S(1)} collective-permute-done((f32[24,256]{1,0:T(8,128)S(1)}, f32[24,256]{1,0:T(8,128)S(1)}, u32[]{:S(2)}, u32[]{:S(2)}) %collective-permute-start.11) | collective-permute-done | bytes 24608 | tf_op jit(solution)/shard_map/ppermute | solution.py:57
  (32 shorter events, 6.2 us)
Async XLA Ops:
  0.6 24.4 %copy-start = (f32[3,16,8,256]{3,2,1,0:T(8,128)S(1)}, f32[3,16,8,256]{3,2,1,0:T(8,128)}, u32[]{:S(2)}) copy-start(f32[3,16,8,256]{3,2,1,0:T(8,128)} %param.6) | copy-start | bytes 1179652
  0.6 32.3 %copy-start.1 = (f32[6,16,8,256]{3,2,1,0:T(8,128)S(1)}, f32[6,16,8,256]{3,2,1,0:T(8,128)}, u32[]{:S(2)}) copy-start(f32[6,16,8,256]{3,2,1,0:T(8,128)} %param.8) | copy-start | bytes 2359300
  6.4 15.2 %collective-permute-start = (f32[72,256]{1,0:T(8,128)}, f32[72,256]{1,0:T(8,128)S(1)}, u32[]{:S(2)}, u32[]{:S(2)}) collective-permute-start(f32[72,256]{1,0:T(8,128)} %get-tuple-element.43), channel_id=1, source_target_pairs={{8,16},{16,8},{24,32},{32,24},{40,48},{48,40},{56,64},{64,56},{72,... | collective-permute-start | bytes 221192 | tf_op jit(solution)/shard_map/ppermute | solution.py:56
  18.6 6.5 %collective-permute-start.1 = (f32[72,256]{1,0:T(8,128)}, f32[72,256]{1,0:T(8,128)S(1)}, u32[]{:S(2)}, u32[]{:S(2)}) collective-permute-start(f32[72,256]{1,0:T(8,128)} %get-tuple-element.44), channel_id=1, source_target_pairs={{0,8},{8,0},{16,24},{24,16},{32,40},{40,32},{48,56},{56,48},{64,72... | collective-permute-start | bytes 221192 | tf_op jit(solution)/shard_map/ppermute | solution.py:57
  20.5 0.9 copy-start.2
  21.5 10.5 %copy-start.5 = (f32[16,8,256]{2,1,0:T(8,128)S(1)}, f32[16,8,256]{2,1,0:T(8,128)}, u32[]{:S(2)}) copy-start(f32[16,8,256]{2,1,0:T(8,128)} %param.10) | copy-start | bytes 393220
  21.5 10.5 %copy-start.6 = (s32[16,8,256]{2,1,0:T(8,128)S(1)}, s32[16,8,256]{2,1,0:T(8,128)}, u32[]{:S(2)}) copy-start(s32[16,8,256]{2,1,0:T(8,128)} %param.11) | copy-start | bytes 393220
  25.1 7.5 %collective-permute-start.2 = (f32[144,256]{1,0:T(8,128)S(1)}, f32[144,256]{1,0:T(8,128)S(1)}, u32[]{:S(2)}, u32[]{:S(2)}) collective-permute-start(f32[144,256]{1,0:T(8,128)S(1)} %get-tuple-element.48), channel_id=1, source_target_pairs={{1,2},{2,1},{3,4},{4,3},{5,6},{6,5},{9,10},{10,9},{11,12},{12,11},... | collective-permute-start | bytes 442376 | tf_op jit(solution)/shard_map/ppermute | solution.py:56
  27.1 5.9 %collective-permute-start.3 = (f32[144,256]{1,0:T(8,128)S(1)}, f32[144,256]{1,0:T(8,128)S(1)}, u32[]{:S(2)}, u32[]{:S(2)}) collective-permute-start(f32[144,256]{1,0:T(8,128)S(1)} %get-tuple-element.49), channel_id=1, source_target_pairs={{0,1},{1,0},{2,3},{3,2},{4,5},{5,4},{6,7},{7,6},{8,9},{9,8},{10,11... | collective-permute-start | bytes 442376 | tf_op jit(solution)/shard_map/ppermute | solution.py:57
  32.0 1.0 copy-start.3
  32.0 1.0 copy-start.4
  35.2 15.9 %all-to-all-start = ((f32[16,8,128]{2,1,0:T(8,128)}), f32[16,8,128]{2,1,0:T(8,128)S(1)}, u32[]{:S(2)}, u32[]{:S(2)}) async-start(f32[16,8,128]{2,1,0:T(8,128)} %get-tuple-element.55), calls=%async_computation | async-start | bytes 131072 | tf_op jit(solution)/shard_map/all_to_all | solution.py:62
  42.6 7.5 %collective-permute-start.4 = (f32[104,256]{1,0:T(8,128)S(1)}, f32[104,256]{1,0:T(8,128)S(1)}, u32[]{:S(2)}, u32[]{:S(2)}) collective-permute-start(f32[104,256]{1,0:T(8,128)S(1)} %get-tuple-element.53), channel_id=1, source_target_pairs={{1,2},{2,1},{3,4},{4,3},{5,6},{6,5},{9,10},{10,9},{11,12},{12,11},... | collective-permute-start | bytes 319496 | tf_op jit(solution)/shard_map/ppermute | solution.py:56
  44.6 6.4 %collective-permute-start.5 = (f32[104,256]{1,0:T(8,128)S(1)}, f32[104,256]{1,0:T(8,128)S(1)}, u32[]{:S(2)}, u32[]{:S(2)}) collective-permute-start(f32[104,256]{1,0:T(8,128)S(1)} %get-tuple-element.54), channel_id=1, source_target_pairs={{0,1},{1,0},{2,3},{3,2},{4,5},{5,4},{6,7},{7,6},{8,9},{9,8},{10,11... | collective-permute-start | bytes 319496 | tf_op jit(solution)/shard_map/ppermute | solution.py:57
  51.7 18.3 %all-to-all-start.1 = ((f32[32,2,128]{2,1,0:T(2,128)}), f32[32,2,128]{2,1,0:T(2,128)S(1)}, u32[]{:S(2)}, u32[]{:S(2)}) async-start(f32[32,2,128]{2,1,0:T(2,128)} %get-tuple-element.63), calls=%async_computation.1 | async-start | bytes 65536 | tf_op jit(solution)/shard_map/all_to_all | solution.py:62
  58.3 9.2 %collective-permute-start.6 = (f32[56,256]{1,0:T(8,128)S(1)}, f32[56,256]{1,0:T(8,128)S(1)}, u32[]{:S(2)}, u32[]{:S(2)}) collective-permute-start(f32[56,256]{1,0:T(8,128)S(1)} %get-tuple-element.56), channel_id=1, source_target_pairs={{8,16},{16,8},{24,32},{32,24},{40,48},{48,40},{56,64},{64,56},{72,... | collective-permute-start | bytes 172040 | tf_op jit(solution)/shard_map/ppermute | solution.py:56
  63.8 6.1 %collective-permute-start.7 = (f32[56,256]{1,0:T(8,128)S(1)}, f32[56,256]{1,0:T(8,128)S(1)}, u32[]{:S(2)}, u32[]{:S(2)}) collective-permute-start(f32[56,256]{1,0:T(8,128)S(1)} %get-tuple-element.57), channel_id=1, source_target_pairs={{0,8},{8,0},{16,24},{24,16},{32,40},{40,32},{48,56},{56,48},{64,72... | collective-permute-start | bytes 172040 | tf_op jit(solution)/shard_map/ppermute | solution.py:57
  72.0 14.8 %all-to-all-start.2 = ((f32[16,8,128]{2,1,0:T(8,128)}), f32[16,8,128]{2,1,0:T(8,128)S(1)}, u32[]{:S(2)}, u32[]{:S(2)}) async-start(f32[16,8,128]{2,1,0:T(8,128)} %get-tuple-element.72), calls=%async_computation.2 | async-start | bytes 131072 | tf_op jit(solution)/shard_map/all_to_all | solution.py:62
  78.4 7.5 %collective-permute-start.8 = (f32[48,256]{1,0:T(8,128)S(1)}, f32[48,256]{1,0:T(8,128)S(1)}, u32[]{:S(2)}, u32[]{:S(2)}) collective-permute-start(f32[48,256]{1,0:T(8,128)S(1)} %get-tuple-element.70), channel_id=1, source_target_pairs={{1,2},{2,1},{3,4},{4,3},{5,6},{6,5},{9,10},{10,9},{11,12},{12,11},... | collective-permute-start | bytes 147464 | tf_op jit(solution)/shard_map/ppermute | solution.py:56
  80.5 6.3 %collective-permute-start.9 = (f32[48,256]{1,0:T(8,128)S(1)}, f32[48,256]{1,0:T(8,128)S(1)}, u32[]{:S(2)}, u32[]{:S(2)}) collective-permute-start(f32[48,256]{1,0:T(8,128)S(1)} %get-tuple-element.71), channel_id=1, source_target_pairs={{0,1},{1,0},{2,3},{3,2},{4,5},{5,4},{6,7},{7,6},{8,9},{9,8},{10,11... | collective-permute-start | bytes 147464 | tf_op jit(solution)/shard_map/ppermute | solution.py:57
  87.4 18.9 %all-to-all-start.3 = ((f32[32,2,128]{2,1,0:T(2,128)}), f32[32,2,128]{2,1,0:T(2,128)S(1)}, u32[]{:S(2)}, u32[]{:S(2)}) async-start(f32[32,2,128]{2,1,0:T(2,128)} %get-tuple-element.75), calls=%async_computation.3 | async-start | bytes 65536 | tf_op jit(solution)/shard_map/all_to_all | solution.py:62
  95.8 8.7 %collective-permute-start.10 = (f32[24,256]{1,0:T(8,128)S(1)}, f32[24,256]{1,0:T(8,128)S(1)}, u32[]{:S(2)}, u32[]{:S(2)}) collective-permute-start(f32[24,256]{1,0:T(8,128)S(1)} %get-tuple-element.73), channel_id=1, source_target_pairs={{8,16},{16,8},{24,32},{32,24},{40,48},{48,40},{56,64},{64,56},{72,... | collective-permute-start | bytes 73736 | tf_op jit(solution)/shard_map/ppermute | solution.py:56
  100.6 5.7 %collective-permute-start.11 = (f32[24,256]{1,0:T(8,128)S(1)}, f32[24,256]{1,0:T(8,128)S(1)}, u32[]{:S(2)}, u32[]{:S(2)}) collective-permute-start(f32[24,256]{1,0:T(8,128)S(1)} %get-tuple-element.74), channel_id=1, source_target_pairs={{0,8},{8,0},{16,24},{24,16},{32,40},{40,32},{48,56},{56,48},{64,72... | collective-permute-start | bytes 73736 | tf_op jit(solution)/shard_map/ppermute | solution.py:57

commit v5 on v4

--- a/solution.py
+++ b/solution.py
@@ -179,11 +179,6 @@
         pltpu.make_async_copy(plastic.at[pl.ds(0, 6 * LZ)], out.at[rows], sem.at[4 * i + 3]).wait()
 
 
-def eta_kernel(viscosity, seed, eta, weak):
-    eta[...] = 1.0 / (1.0 / viscosity[...] + 1.0 / SHEAR)
-    weak[...] = 1.0 - 0.6 * seed[...].astype(F32)
-
-
 def store_row(out, top_yield, top_eta, earlier=None):
     a = jnp.max(top_yield, axis=(0, 1), keepdims=True)
     b = jnp.max(top_eta, axis=(0, 1), keepdims=True)
@@ -302,28 +297,34 @@
     return jnp.where(inside & (jnp.abs(gap) <= 6), jnp.exp(g * g * (-1.0 / 18.0)) / WEIGHT_TOTAL, 0.0)
 
 
+def own_kernel(along, viscosity, seed, eta, weak, own, from_z, along_y):
+    eta[...] = 1.0 / (1.0 / viscosity[...] + 1.0 / SHEAR)
+    weak[...] = 1.0 - 0.6 * seed[...].astype(F32)
+    r = lax.broadcasted_iota(jnp.int32, (ROWS, ROWS), 0)
+    c = lax.broadcasted_iota(jnp.int32, (ROWS, ROWS), 1)
+    own_z = gauss(c % LZ - r % LZ, c // LZ == r // LZ)
+    r = lax.broadcasted_iota(jnp.int32, (ROWS, NY), 0)
+    c = lax.broadcasted_iota(jnp.int32, (ROWS, NY), 1)
+    j = c // LX
+    from_z[...] = gauss(jnp.where(j < 6, j - 6, j - 6 + LZ) - r % LZ, c % LX == r // LZ)
+    r = lax.broadcasted_iota(jnp.int32, (NY, NY), 0)
+    c = lax.broadcasted_iota(jnp.int32, (NY, NY), 1)
+    along_y[...] = gauss(r - c, r >= 0)
+    own[...] = dot(dot(own_z, along[...]), along_y[...])
+
+
 def dot(a, b):
     return jnp.dot(a, b, precision=lax.Precision.HIGHEST, preferred_element_type=F32)
 
 
 def first_kernel(
-    v, pressure, old, along, plastic, eta_in, weak, x_far, x_near, z_far, z_near,
+    v, pressure, old, plastic, eta_in, weak, own, from_z, along_y, x_far, x_near, z_far, z_near,
     part, pres, total, cohesion_out, vx_out, vz_out, gx, fz, row_out, sz_far, sz_near,
     face, slots, held,
 ):
     low, high = sides(even_z(), z_far[...], z_near[...])
-    r = lax.broadcasted_iota(jnp.int32, (ROWS, ROWS), 0)
-    c = lax.broadcasted_iota(jnp.int32, (ROWS, ROWS), 1)
-    own = gauss(c % LZ - r % LZ, c // LZ == r // LZ)
-    r = lax.broadcasted_iota(jnp.int32, (ROWS, 6 * LX), 0)
-    c = lax.broadcasted_iota(jnp.int32, (ROWS, 6 * LX), 1)
-    same = c % LX == r // LZ
-    from_low = gauss(c // LX - 6 - r % LZ, same)
-    from_high = gauss(c // LX + LZ - r % LZ, same)
-    along_z = dot(own, along[...]) + dot(from_low, low[3 * LX :]) + dot(from_high, high[3 * LX :])
-    r = lax.broadcasted_iota(jnp.int32, (NY, NY), 0)
-    c = lax.broadcasted_iota(jnp.int32, (NY, NY), 1)
-    smoothed = dot(along_z, gauss(r - c, r >= 0))
+    beside = jnp.concatenate([low[3 * LX :], high[3 * LX :]], axis=0)
+    smoothed = own[...] + dot(dot(from_z[:, : 12 * LX], beside), along_y[...])
     cohesion_out[...] = weak[...] / (1.0 + 2.0 * smoothed)
     for f in range(3):
         spread_rows(face, f, low[f * LX : (f + 1) * LX], high[f * LX : (f + 1) * LX])
@@ -491,17 +492,19 @@
     x_3, z_3, x_9, z_9 = (3 * LZ, NY), (3 * LX, NY), (9 * LZ, NY), (9 * LX, NY)
 
     dma = pltpu.SemaphoreType.DMA
-    x_msgs = call(faces_kernel, [x_9, x_9], [v, plastic], 0, [dma((8,))], [HBM, HBM], [HBM, HBM], 60)
+    x_msgs = call(faces_kernel, [x_9, x_9], [v, plastic], 0, [dma((8,))], None, [HBM, HBM], 60)
     x_msgs = exchange(GX, *x_msgs)
-    eta, weak = call(eta_kernel, [one, one], [viscosity, weak_seed], 10**5)
     (along,) = call(own_x_kernel, [one], [plastic], 10**6)
     along, *z_msgs = call(smooth_x_kernel, [one, z_9, z_9], [v, along, *x_msgs], 10**6, [slots])
     z_msgs = exchange(GZ, *z_msgs)
+    eta, weak, *tables = call(
+        own_kernel, [one, one, one, one, (NY, NY)], [along, viscosity, weak_seed], 10**7
+    )
     x_two, z_two, x_full, z_full = (2,) + x_3, (2,) + z_3, (7 * LZ, NY), (6 * LX + 8, NY)
     part, pres, total, cohesion, vx, vz, gx, fz, row, *sent = call(
         first_kernel,
         [three, one, one, one, x_two, z_two, x_two, z_two, row_1, z_full, z_full],
-        [v, pressure, old, along, plastic, eta, weak, *x_msgs, *z_msgs],
+        [v, pressure, old, plastic, eta, weak, *tables, *x_msgs, *z_msgs],
         10**7,
         [face, slots, pltpu.VMEM(six, F32)],
     )

time: 108 us -> 104 us (0.963)
  Pallas kernels: 12.4 us -> 8.91 us
    pallas_call x10, Pallas kernels: 12.4 us -> 8.91 us  [call(): pl.pallas_call(kernel, out_shape=[jax.ShapeDtypeStruct(s, F32) for s in o...]
  transfers between devices with their start and end apart: 16 -> 16, of which waited for: 9 -> 8; matrix products, arithmetic and copies ran while one was open for 0% -> 0% of each run, Pallas kernels for 0% -> 1%
where the time goes in v5:
time: 104 us; the launch traced here: 103 us
  starting transfers between devices  78.2 us (75%)
  waiting for transfers between devices  14.1 us (14%)
  Pallas kernels  8.91 us (9%)
    ppermute x6, starting transfers between devices, exchange(): lax.ppermute(far, axis, pairs(count, 1))  28.7 us
    all_to_all x4, starting transfers between devices, spread(): return lax.all_to_all(row, axes, 0, 0, tiled=True)  27.9 us
    ppermute x6, starting transfers between devices, exchange(): lax.ppermute(near, axis, pairs(count, 0))  21.6 us
    ppermute x6, waiting for transfers between devices, exchange(): lax.ppermute(near, axis, pairs(count, 0))  9.98 us
    pallas_call x10, Pallas kernels, call(): pl.pallas_call(kernel, out_shape=[jax.ShapeDtypeStruct(s, F32) for s in o...  8.91 us
    ppermute x6, waiting for transfers between devices, exchange(): lax.ppermute(far, axis, pairs(count, 1))  4.14 us
  transfers between devices with their start and end apart: 16, of which 8 were waited for; matrix products, arithmetic and copies ran while one was open for 0% of the time, Pallas kernels for 1%

profile of v5, /device:TPU:22, one launch (start us, length us, event | category | flops | bytes accessed | tf_op | source)
XLA Modules:
  0.0 103.2 jit_solution(14869526959165394731)
XLA Ops:
  0.7 1.7 %shard_map.102 = (f32[72,256]{1,0:T(8,128)}, f32[72,256]{1,0:T(8,128)}) custom-call(f32[3,128,256]{2,1,0:T(8,128)} %bitcast.10, f32[128,256]{1,0:T(8,128)} %bitcast.16), custom_call_target="tpu_custom_call" | custom-call | bytes 671744 | tf_op jit(solution)/shard_map/pallas_call | solution.py:35
  2.4 12.4 %collective-permute-start = (f32[72,256]{1,0:T(8,128)}, f32[72,256]{1,0:T(8,128)S(1)}, u32[]{:S(2)}, u32[]{:S(2)}) collective-permute-start(f32[72,256]{1,0:T(8,128)} %get-tuple-element.46), channel_id=1, source_target_pairs={{8,16},{16,8},{24,32},{32,24},{40,48},{48,40},{56,64},{64,56},{72,... | collective-permute-start | bytes 221192 | tf_op jit(solution)/shard_map/ppermute | solution.py:56
  14.7 1.9 %collective-permute-start.1 = (f32[72,256]{1,0:T(8,128)}, f32[72,256]{1,0:T(8,128)S(1)}, u32[]{:S(2)}, u32[]{:S(2)}) collective-permute-start(f32[72,256]{1,0:T(8,128)} %get-tuple-element.47), channel_id=1, source_target_pairs={{0,8},{8,0},{16,24},{24,16},{32,40},{40,32},{48,56},{56,48},{64,72... | collective-permute-start | bytes 221192 | tf_op jit(solution)/shard_map/ppermute | solution.py:57
  17.3 3.9 %collective-permute-done.1.x_near = f32[72,256]{1,0:T(8,128)S(1)} collective-permute-done((f32[72,256]{1,0:T(8,128)}, f32[72,256]{1,0:T(8,128)S(1)}, u32[]{:S(2)}, u32[]{:S(2)}) %collective-permute-start.1) | collective-permute-done | bytes 73760 | tf_op jit(solution)/shard_map/ppermute | solution.py:57
  21.3 1.9 %collective-permute-start.2 = (f32[144,256]{1,0:T(8,128)S(1)}, f32[144,256]{1,0:T(8,128)S(1)}, u32[]{:S(2)}, u32[]{:S(2)}) collective-permute-start(f32[144,256]{1,0:T(8,128)S(1)} %get-tuple-element.54), channel_id=1, source_target_pairs={{1,2},{2,1},{3,4},{4,3},{5,6},{6,5},{9,10},{10,9},{11,12},{12,11},... | collective-permute-start | bytes 442376 | tf_op jit(solution)/shard_map/ppermute | solution.py:56
  23.2 4.9 %collective-permute-start.3 = (f32[144,256]{1,0:T(8,128)S(1)}, f32[144,256]{1,0:T(8,128)S(1)}, u32[]{:S(2)}, u32[]{:S(2)}) collective-permute-start(f32[144,256]{1,0:T(8,128)S(1)} %get-tuple-element.55), channel_id=1, source_target_pairs={{0,1},{1,0},{2,3},{3,2},{4,5},{5,4},{6,7},{7,6},{8,9},{9,8},{10,11... | collective-permute-start | bytes 442376 | tf_op jit(solution)/shard_map/ppermute | solution.py:57
  30.0 1.9 %shard_map.105 = (f32[3,128,256]{2,1,0:T(8,128)S(1)}, f32[128,256]{1,0:T(8,128)S(1)}, f32[128,256]{1,0:T(8,128)S(1)}, f32[128,256]{1,0:T(8,128)S(1)}, f32[2,24,2...) custom-call(f32[3,128,256]{2,1,0:T(8,128)S(1)} %bitcast.12, ...), custom_call_target="tpu_custom_call" | custom-call | flops 10000000 | bytes 4030464 | tf_op jit(solution)/shard_map/pallas_call | solution.py:35
  31.9 6.6 %all-to-all-start = ((f32[16,8,128]{2,1,0:T(8,128)}), f32[16,8,128]{2,1,0:T(8,128)S(1)}, u32[]{:S(2)}, u32[]{:S(2)}) async-start(f32[16,8,128]{2,1,0:T(8,128)} %get-tuple-element.61), calls=%async_computation | async-start | bytes 131072 | tf_op jit(solution)/shard_map/all_to_all | solution.py:62
  38.5 2.0 %collective-permute-start.4 = (f32[104,256]{1,0:T(8,128)S(1)}, f32[104,256]{1,0:T(8,128)S(1)}, u32[]{:S(2)}, u32[]{:S(2)}) collective-permute-start(f32[104,256]{1,0:T(8,128)S(1)} %get-tuple-element.59), channel_id=1, source_target_pairs={{1,2},{2,1},{3,4},{4,3},{5,6},{6,5},{9,10},{10,9},{11,12},{12,11},... | collective-permute-start | bytes 319496 | tf_op jit(solution)/shard_map/ppermute | solution.py:56
  40.5 5.5 %collective-permute-start.5 = (f32[104,256]{1,0:T(8,128)S(1)}, f32[104,256]{1,0:T(8,128)S(1)}, u32[]{:S(2)}, u32[]{:S(2)}) collective-permute-start(f32[104,256]{1,0:T(8,128)S(1)} %get-tuple-element.60), channel_id=1, source_target_pairs={{0,1},{1,0},{2,3},{3,2},{4,5},{5,4},{6,7},{7,6},{8,9},{9,8},{10,11... | collective-permute-start | bytes 319496 | tf_op jit(solution)/shard_map/ppermute | solution.py:57
  47.6 6.6 %all-to-all-start.1 = ((f32[32,2,128]{2,1,0:T(2,128)}), f32[32,2,128]{2,1,0:T(2,128)S(1)}, u32[]{:S(2)}, u32[]{:S(2)}) async-start(f32[32,2,128]{2,1,0:T(2,128)} %get-tuple-element.69), calls=%async_computation.1 | async-start | bytes 65536 | tf_op jit(solution)/shard_map/all_to_all | solution.py:62
  54.2 5.5 %collective-permute-start.6 = (f32[56,256]{1,0:T(8,128)S(1)}, f32[56,256]{1,0:T(8,128)S(1)}, u32[]{:S(2)}, u32[]{:S(2)}) collective-permute-start(f32[56,256]{1,0:T(8,128)S(1)} %get-tuple-element.62), channel_id=1, source_target_pairs={{8,16},{16,8},{24,32},{32,24},{40,48},{48,40},{56,64},{64,56},{72,... | collective-permute-start | bytes 172040 | tf_op jit(solution)/shard_map/ppermute | solution.py:56
  59.7 1.9 %collective-permute-start.7 = (f32[56,256]{1,0:T(8,128)S(1)}, f32[56,256]{1,0:T(8,128)S(1)}, u32[]{:S(2)}, u32[]{:S(2)}) collective-permute-start(f32[56,256]{1,0:T(8,128)S(1)} %get-tuple-element.63), channel_id=1, source_target_pairs={{0,8},{8,0},{16,24},{24,16},{32,40},{40,32},{48,56},{56,48},{64,72... | collective-permute-start | bytes 172040 | tf_op jit(solution)/shard_map/ppermute | solution.py:57
  61.6 1.7 %collective-permute-done.6.sx_far = f32[56,256]{1,0:T(8,128)S(1)} collective-permute-done((f32[56,256]{1,0:T(8,128)S(1)}, f32[56,256]{1,0:T(8,128)S(1)}, u32[]{:S(2)}, u32[]{:S(2)}) %collective-permute-start.6) | collective-permute-done | bytes 57376 | tf_op jit(solution)/shard_map/ppermute | solution.py:56
  63.3 2.4 %collective-permute-done.7.sx_near = f32[56,256]{1,0:T(8,128)S(1)} collective-permute-done((f32[56,256]{1,0:T(8,128)S(1)}, f32[56,256]{1,0:T(8,128)S(1)}, u32[]{:S(2)}, u32[]{:S(2)}) %collective-permute-start.7) | collective-permute-done | bytes 57376 | tf_op jit(solution)/shard_map/ppermute | solution.py:57
  65.9 2.0 %shard_map.108 = (f32[6,128,256]{2,1,0:T(8,128)}, f32[128,256]{1,0:T(8,128)}, f32[128,256]{1,0:T(8,128)}, f32[3,128,256]{2,1,0:T(8,128)S(1)}, f32[3,128,256]{2,1...) custom-call(f32[3,128,256]{2,1,0:T(8,128)S(1)} %bitcast.13, ...), custom_call_target="tpu_custom_call" | custom-call | flops 10000000 | bytes 4472832 | tf_op jit(solution)/shard_map/pallas_call | solution.py:35
  67.9 6.4 %all-to-all-start.2 = ((f32[16,8,128]{2,1,0:T(8,128)}), f32[16,8,128]{2,1,0:T(8,128)S(1)}, u32[]{:S(2)}, u32[]{:S(2)}) async-start(f32[16,8,128]{2,1,0:T(8,128)} %get-tuple-element.78), calls=%async_computation.2 | async-start | bytes 131072 | tf_op jit(solution)/shard_map/all_to_all | solution.py:62
  74.3 2.0 %collective-permute-start.8 = (f32[48,256]{1,0:T(8,128)S(1)}, f32[48,256]{1,0:T(8,128)S(1)}, u32[]{:S(2)}, u32[]{:S(2)}) collective-permute-start(f32[48,256]{1,0:T(8,128)S(1)} %get-tuple-element.76), channel_id=1, source_target_pairs={{1,2},{2,1},{3,4},{4,3},{5,6},{6,5},{9,10},{10,9},{11,12},{12,11},... | collective-permute-start | bytes 147464 | tf_op jit(solution)/shard_map/ppermute | solution.py:56
  76.4 5.5 %collective-permute-start.9 = (f32[48,256]{1,0:T(8,128)S(1)}, f32[48,256]{1,0:T(8,128)S(1)}, u32[]{:S(2)}, u32[]{:S(2)}) collective-permute-start(f32[48,256]{1,0:T(8,128)S(1)} %get-tuple-element.77), channel_id=1, source_target_pairs={{0,1},{1,0},{2,3},{3,2},{4,5},{5,4},{6,7},{7,6},{8,9},{9,8},{10,11... | collective-permute-start | bytes 147464 | tf_op jit(solution)/shard_map/ppermute | solution.py:57
  83.3 8.3 %all-to-all-start.3 = ((f32[32,2,128]{2,1,0:T(2,128)}), f32[32,2,128]{2,1,0:T(2,128)S(1)}, u32[]{:S(2)}, u32[]{:S(2)}) async-start(f32[32,2,128]{2,1,0:T(2,128)} %get-tuple-element.81), calls=%async_computation.3 | async-start | bytes 65536 | tf_op jit(solution)/shard_map/all_to_all | solution.py:62
  91.6 4.9 %collective-permute-start.10 = (f32[24,256]{1,0:T(8,128)S(1)}, f32[24,256]{1,0:T(8,128)S(1)}, u32[]{:S(2)}, u32[]{:S(2)}) collective-permute-start(f32[24,256]{1,0:T(8,128)S(1)} %get-tuple-element.79), channel_id=1, source_target_pairs={{8,16},{16,8},{24,32},{32,24},{40,48},{48,40},{56,64},{64,56},{72,... | collective-permute-start | bytes 73736 | tf_op jit(solution)/shard_map/ppermute | solution.py:56
  96.5 1.9 %collective-permute-start.11 = (f32[24,256]{1,0:T(8,128)S(1)}, f32[24,256]{1,0:T(8,128)S(1)}, u32[]{:S(2)}, u32[]{:S(2)}) collective-permute-start(f32[24,256]{1,0:T(8,128)S(1)} %get-tuple-element.80), channel_id=1, source_target_pairs={{0,8},{8,0},{16,24},{24,16},{32,40},{40,32},{48,56},{56,48},{64,72... | collective-permute-start | bytes 73736 | tf_op jit(solution)/shard_map/ppermute | solution.py:57
  98.5 1.9 %collective-permute-done.10.sx_far = f32[24,256]{1,0:T(8,128)S(1)} collective-permute-done((f32[24,256]{1,0:T(8,128)S(1)}, f32[24,256]{1,0:T(8,128)S(1)}, u32[]{:S(2)}, u32[]{:S(2)}) %collective-permute-start.10) | collective-permute-done | bytes 24608 | tf_op jit(solution)/shard_map/ppermute | solution.py:56
  100.4 1.9 %collective-permute-done.11.sx_near = f32[24,256]{1,0:T(8,128)S(1)} collective-permute-done((f32[24,256]{1,0:T(8,128)S(1)}, f32[24,256]{1,0:T(8,128)S(1)}, u32[]{:S(2)}, u32[]{:S(2)}) %collective-permute-start.11) | collective-permute-done | bytes 24608 | tf_op jit(solution)/shard_map/ppermute | solution.py:57
  (30 shorter events, 6.6 us)
Async XLA Ops:
  0.6 16.0 %copy-start.2 = (f32[16,8,256]{2,1,0:T(8,128)S(1)}, f32[16,8,256]{2,1,0:T(8,128)}, u32[]{:S(2)}) copy-start(f32[16,8,256]{2,1,0:T(8,128)} %param.9) | copy-start | bytes 393220
  0.6 20.6 %copy-start = (f32[3,16,8,256]{3,2,1,0:T(8,128)S(1)}, f32[3,16,8,256]{3,2,1,0:T(8,128)}, u32[]{:S(2)}) copy-start(f32[3,16,8,256]{3,2,1,0:T(8,128)} %param.6) | copy-start | bytes 1179652
  2.4 27.5 %copy-start.1 = (f32[6,16,8,256]{3,2,1,0:T(8,128)S(1)}, f32[6,16,8,256]{3,2,1,0:T(8,128)}, u32[]{:S(2)}) copy-start(f32[6,16,8,256]{3,2,1,0:T(8,128)} %param.8) | copy-start | bytes 2359300
  2.4 14.9 %collective-permute-start = (f32[72,256]{1,0:T(8,128)}, f32[72,256]{1,0:T(8,128)S(1)}, u32[]{:S(2)}, u32[]{:S(2)}) collective-permute-start(f32[72,256]{1,0:T(8,128)} %get-tuple-element.46), channel_id=1, source_target_pairs={{8,16},{16,8},{24,32},{32,24},{40,48},{48,40},{56,64},{64,56},{72,... | collective-permute-start | bytes 221192 | tf_op jit(solution)/shard_map/ppermute | solution.py:56
  14.7 6.5 %collective-permute-start.1 = (f32[72,256]{1,0:T(8,128)}, f32[72,256]{1,0:T(8,128)S(1)}, u32[]{:S(2)}, u32[]{:S(2)}) collective-permute-start(f32[72,256]{1,0:T(8,128)} %get-tuple-element.47), channel_id=1, source_target_pairs={{0,8},{8,0},{16,24},{24,16},{32,40},{40,32},{48,56},{56,48},{64,72... | collective-permute-start | bytes 221192 | tf_op jit(solution)/shard_map/ppermute | solution.py:57
  16.8 11.4 %copy-start.3 = (f32[16,8,256]{2,1,0:T(8,128)S(1)}, f32[16,8,256]{2,1,0:T(8,128)}, u32[]{:S(2)}) copy-start(f32[16,8,256]{2,1,0:T(8,128)} %param.10) | copy-start | bytes 393220
  21.3 8.5 %collective-permute-start.2 = (f32[144,256]{1,0:T(8,128)S(1)}, f32[144,256]{1,0:T(8,128)S(1)}, u32[]{:S(2)}, u32[]{:S(2)}) collective-permute-start(f32[144,256]{1,0:T(8,128)S(1)} %get-tuple-element.54), channel_id=1, source_target_pairs={{1,2},{2,1},{3,4},{4,3},{5,6},{6,5},{9,10},{10,9},{11,12},{12,11},... | collective-permute-start | bytes 442376 | tf_op jit(solution)/shard_map/ppermute | solution.py:56
  23.2 6.6 %collective-permute-start.3 = (f32[144,256]{1,0:T(8,128)S(1)}, f32[144,256]{1,0:T(8,128)S(1)}, u32[]{:S(2)}, u32[]{:S(2)}) collective-permute-start(f32[144,256]{1,0:T(8,128)S(1)} %get-tuple-element.55), channel_id=1, source_target_pairs={{0,1},{1,0},{2,3},{3,2},{4,5},{5,4},{6,7},{7,6},{8,9},{9,8},{10,11... | collective-permute-start | bytes 442376 | tf_op jit(solution)/shard_map/ppermute | solution.py:57
  28.2 0.9 copy-start.4
  29.1 0.9 copy-start.5
  31.9 15.0 %all-to-all-start = ((f32[16,8,128]{2,1,0:T(8,128)}), f32[16,8,128]{2,1,0:T(8,128)S(1)}, u32[]{:S(2)}, u32[]{:S(2)}) async-start(f32[16,8,128]{2,1,0:T(8,128)} %get-tuple-element.61), calls=%async_computation | async-start | bytes 131072 | tf_op jit(solution)/shard_map/all_to_all | solution.py:62
  38.5 7.5 %collective-permute-start.4 = (f32[104,256]{1,0:T(8,128)S(1)}, f32[104,256]{1,0:T(8,128)S(1)}, u32[]{:S(2)}, u32[]{:S(2)}) collective-permute-start(f32[104,256]{1,0:T(8,128)S(1)} %get-tuple-element.59), channel_id=1, source_target_pairs={{1,2},{2,1},{3,4},{4,3},{5,6},{6,5},{9,10},{10,9},{11,12},{12,11},... | collective-permute-start | bytes 319496 | tf_op jit(solution)/shard_map/ppermute | solution.py:56
  40.5 6.4 %collective-permute-start.5 = (f32[104,256]{1,0:T(8,128)S(1)}, f32[104,256]{1,0:T(8,128)S(1)}, u32[]{:S(2)}, u32[]{:S(2)}) collective-permute-start(f32[104,256]{1,0:T(8,128)S(1)} %get-tuple-element.60), channel_id=1, source_target_pairs={{0,1},{1,0},{2,3},{3,2},{4,5},{5,4},{6,7},{7,6},{8,9},{9,8},{10,11... | collective-permute-start | bytes 319496 | tf_op jit(solution)/shard_map/ppermute | solution.py:57
  47.6 18.3 %all-to-all-start.1 = ((f32[32,2,128]{2,1,0:T(2,128)}), f32[32,2,128]{2,1,0:T(2,128)S(1)}, u32[]{:S(2)}, u32[]{:S(2)}) async-start(f32[32,2,128]{2,1,0:T(2,128)} %get-tuple-element.69), calls=%async_computation.1 | async-start | bytes 65536 | tf_op jit(solution)/shard_map/all_to_all | solution.py:62
  54.2 9.2 %collective-permute-start.6 = (f32[56,256]{1,0:T(8,128)S(1)}, f32[56,256]{1,0:T(8,128)S(1)}, u32[]{:S(2)}, u32[]{:S(2)}) collective-permute-start(f32[56,256]{1,0:T(8,128)S(1)} %get-tuple-element.62), channel_id=1, source_target_pairs={{8,16},{16,8},{24,32},{32,24},{40,48},{48,40},{56,64},{64,56},{72,... | collective-permute-start | bytes 172040 | tf_op jit(solution)/shard_map/ppermute | solution.py:56
  59.7 6.1 %collective-permute-start.7 = (f32[56,256]{1,0:T(8,128)S(1)}, f32[56,256]{1,0:T(8,128)S(1)}, u32[]{:S(2)}, u32[]{:S(2)}) collective-permute-start(f32[56,256]{1,0:T(8,128)S(1)} %get-tuple-element.63), channel_id=1, source_target_pairs={{0,8},{8,0},{16,24},{24,16},{32,40},{40,32},{48,56},{56,48},{64,72... | collective-permute-start | bytes 172040 | tf_op jit(solution)/shard_map/ppermute | solution.py:57
  67.9 14.8 %all-to-all-start.2 = ((f32[16,8,128]{2,1,0:T(8,128)}), f32[16,8,128]{2,1,0:T(8,128)S(1)}, u32[]{:S(2)}, u32[]{:S(2)}) async-start(f32[16,8,128]{2,1,0:T(8,128)} %get-tuple-element.78), calls=%async_computation.2 | async-start | bytes 131072 | tf_op jit(solution)/shard_map/all_to_all | solution.py:62
  74.3 7.5 %collective-permute-start.8 = (f32[48,256]{1,0:T(8,128)S(1)}, f32[48,256]{1,0:T(8,128)S(1)}, u32[]{:S(2)}, u32[]{:S(2)}) collective-permute-start(f32[48,256]{1,0:T(8,128)S(1)} %get-tuple-element.76), channel_id=1, source_target_pairs={{1,2},{2,1},{3,4},{4,3},{5,6},{6,5},{9,10},{10,9},{11,12},{12,11},... | collective-permute-start | bytes 147464 | tf_op jit(solution)/shard_map/ppermute | solution.py:56
  76.4 6.3 %collective-permute-start.9 = (f32[48,256]{1,0:T(8,128)S(1)}, f32[48,256]{1,0:T(8,128)S(1)}, u32[]{:S(2)}, u32[]{:S(2)}) collective-permute-start(f32[48,256]{1,0:T(8,128)S(1)} %get-tuple-element.77), channel_id=1, source_target_pairs={{0,1},{1,0},{2,3},{3,2},{4,5},{5,4},{6,7},{7,6},{8,9},{9,8},{10,11... | collective-permute-start | bytes 147464 | tf_op jit(solution)/shard_map/ppermute | solution.py:57
  83.3 18.9 %all-to-all-start.3 = ((f32[32,2,128]{2,1,0:T(2,128)}), f32[32,2,128]{2,1,0:T(2,128)S(1)}, u32[]{:S(2)}, u32[]{:S(2)}) async-start(f32[32,2,128]{2,1,0:T(2,128)} %get-tuple-element.81), calls=%async_computation.3 | async-start | bytes 65536 | tf_op jit(solution)/shard_map/all_to_all | solution.py:62
  91.6 8.7 %collective-permute-start.10 = (f32[24,256]{1,0:T(8,128)S(1)}, f32[24,256]{1,0:T(8,128)S(1)}, u32[]{:S(2)}, u32[]{:S(2)}) collective-permute-start(f32[24,256]{1,0:T(8,128)S(1)} %get-tuple-element.79), channel_id=1, source_target_pairs={{8,16},{16,8},{24,32},{32,24},{40,48},{48,40},{56,64},{64,56},{72,... | collective-permute-start | bytes 73736 | tf_op jit(solution)/shard_map/ppermute | solution.py:56
  96.5 5.7 %collective-permute-start.11 = (f32[24,256]{1,0:T(8,128)S(1)}, f32[24,256]{1,0:T(8,128)S(1)}, u32[]{:S(2)}, u32[]{:S(2)}) collective-permute-start(f32[24,256]{1,0:T(8,128)S(1)} %get-tuple-element.80), channel_id=1, source_target_pairs={{0,8},{8,0},{16,24},{24,16},{32,40},{40,32},{48,56},{56,48},{64,72... | collective-permute-start | bytes 73736 | tf_op jit(solution)/shard_map/ppermute | solution.py:57

commit v6 on v5

--- a/solution.py
+++ b/solution.py
@@ -373,8 +373,7 @@
     sz_far[6 * LX :], sz_near[6 * LX :] = a, b
 
 
-def x_pack_kernel(part, gx, sz_far, sz_near, row, row_out, sx_far, sx_near):
-    relay_row(row, row_out)
+def x_pack_kernel(part, gx, sz_far, sz_near, sx_far, sx_near):
     low, high = sides(even_z(), sz_far[...], sz_near[...])
     z = lax.broadcasted_iota(jnp.int32, (LZ, NY), 0)
     messages = []
@@ -417,16 +416,19 @@
             rz[side, rows] = jnp.where(has, value, 0.0)
 
 
-def relay_kernel(gx, sz_far, sz_near, row, row_out, sx_far, sx_near):
+def relay_kernel(near, row, row_out):
     relay_row(row, row_out)
-    sx_far[...], sx_near[...] = facing(even_x(), gx[0], gx[1])
+
+
+def z_pack_kernel(fz, sx_far, sz_far, sz_near):
+    sz_far[...], sz_near[...] = facing(even_z(), fz[0], fz[1])
 
 
 def second_kernel(
     v, res, vx, vz, rx, rz, row,
     old, pressure, plastic, eta_in, cohesion,
-    stress, pres, total, v_out, part, row_out, gx, sz_far, sz_near,
-    face, slots, fz, held,
+    stress, pres, total, v_out, part, row_out, fz, sx_far, sx_near,
+    face, slots, gx, held,
 ):
     top, peak = row_values(row, (0, 1))
     step = 0.125 / peak
@@ -463,13 +465,16 @@
     partial_residual(held, part, masks)
     x_faces(held, ALONG_X, gx)
     z_faces(held, ALONG_Z, fz, slots)
-    sz_far[...], sz_near[...] = facing(even_z(), fz[0], fz[1])
+    sx_far[0 : 3 * LZ], sx_near[...] = facing(even_x(), gx[0], gx[1])
+    sx_far[3 * LZ :] = jnp.zeros((sx_far.shape[0] - 3 * LZ, NY), F32)
 
 
 def final_kernel(v, part, sx_far, sx_near, sz_far, sz_near, row, v_out, peaks, face):
     top, peak, first_top = row_values(row, (0, 1, 2))
     step = 0.125 / peak
-    slabs = sides(even_x(), sx_far[...], sx_near[...]) + sides(even_z(), sz_far[...], sz_near[...])
+    slabs = sides(even_x(), sx_far[0 : 3 * LZ], sx_near[...]) + sides(
+        even_z(), sz_far[...], sz_near[...]
+    )
     for f, here, value in whole_residual(part, *slabs, face, iotas()):
         v_out[f, here] = v[f, here] + step * value
     peaks[0] = jnp.max(first_top)
@@ -510,26 +515,25 @@
     )
     row = spread(row, YCORE)
     z_got = exchange(GZ, *sent)
-    row, *sent = call(
-        x_pack_kernel, [row_2, x_full, x_full], [part, gx, *z_got, row], 10**5
-    )
+    (row,) = call(relay_kernel, [row_2], [z_got[1], row], 10**4)
     row = spread(row, XZ)
+    sent = call(x_pack_kernel, [x_full, x_full], [part, gx, *z_got], 10**5)
     x_got = exchange(GX, *sent)
     res, rx, rz = call(
         residual_kernel, [three, x_two, z_two], [part, gx, fz, *x_got, *z_got], 10**6, [face]
     )
-    stress, pres, total, v, part, row, gx, *sent = call(
+    stress, pres, total, v, part, row, fz, *sent = call(
         second_kernel,
-        [six, one, one, three, three, row_1, x_two, z_3, z_3],
+        [six, one, one, three, three, row_2, z_two, (72, NY), x_3],
         [v, res, vx, vz, rx, rz, row, old, pres, total, eta, cohesion],
         10**7,
-        [face, slots, pltpu.VMEM(z_two, F32), pltpu.VMEM(six, F32)],
-    )
-    row = spread(row, YCORE)
-    z_got = exchange(GZ, *sent)
-    row, *sent = call(relay_kernel, [row_2, x_3, x_3], [gx, *z_got, row], 10**4)
+        [face, slots, pltpu.VMEM(x_two, F32), pltpu.VMEM(six, F32)],
+    )
     row = spread(row, XZ)
     x_got = exchange(GX, *sent)
+    (row,) = call(relay_kernel, [row_1], [x_got[1], row], 10**4)
+    row = spread(row, YCORE)
+    z_got = exchange(GZ, *call(z_pack_kernel, [z_3, z_3], [fz, x_got[0]], 10**4))
     v, peaks = call(
         final_kernel,
         [three, (2,)],

time: 104 us -> 99.8 us (0.960)
  the two profiles are of different devices: /device:TPU:22 before, /device:TPU:1 now
where the time goes in v6:
time: 99.8 us; the launch traced here: 99.1 us
  starting transfers between devices  75.6 us (76%)
  waiting for transfers between devices  12.7 us (13%)
  Pallas kernels  8.96 us (9%)
    all_to_all x4, starting transfers between devices, spread(): return lax.all_to_all(row, axes, 0, 0, tiled=True)  36.9 us
    ppermute x6, starting transfers between devices, exchange(): lax.ppermute(near, axis, pairs(count, 0))  21.7 us
    ppermute x6, starting transfers between devices, exchange(): lax.ppermute(far, axis, pairs(count, 1))  17 us
    pallas_call x12, Pallas kernels, call(): pl.pallas_call(kernel, out_shape=[jax.ShapeDtypeStruct(s, F32) for s in o...  8.96 us
    all_to_all x4, waiting for transfers between devices, spread(): return lax.all_to_all(row, axes, 0, 0, tiled=True)  6.22 us
    ppermute x6, waiting for transfers between devices, exchange(): lax.ppermute(near, axis, pairs(count, 0))  5.45 us
  transfers between devices with their start and end apart: 16, of which 10 were waited for; matrix products, arithmetic and copies ran while one was open for 0% of the time, Pallas kernels for 2%

profile of v6, /device:TPU:1, one launch (start us, length us, event | category | flops | bytes accessed | tf_op | source)
XLA Modules:
  0.0 99.1 jit_solution(15584839273295601176)
XLA Ops:
  0.7 1.7 %shard_map.102 = (f32[72,256]{1,0:T(8,128)}, f32[72,256]{1,0:T(8,128)}) custom-call(f32[3,128,256]{2,1,0:T(8,128)} %bitcast.10, f32[128,256]{1,0:T(8,128)} %bitcast.16), custom_call_target="tpu_custom_call" | custom-call | bytes 671744 | tf_op jit(solution)/shard_map/pallas_call | solution.py:35
  3.2 7.3 %collective-permute-start.1 = (f32[72,256]{1,0:T(8,128)}, f32[72,256]{1,0:T(8,128)S(1)}, u32[]{:S(2)}, u32[]{:S(2)}) collective-permute-start(f32[72,256]{1,0:T(8,128)} %get-tuple-element.45), channel_id=1, source_target_pairs={{0,8},{8,0},{16,24},{24,16},{32,40},{40,32},{48,56},{56,48},{64,72... | collective-permute-start | bytes 221192 | tf_op jit(solution)/shard_map/ppermute | solution.py:57
  10.6 1.8 %collective-permute-done.1.x_near = f32[72,256]{1,0:T(8,128)S(1)} collective-permute-done((f32[72,256]{1,0:T(8,128)}, f32[72,256]{1,0:T(8,128)S(1)}, u32[]{:S(2)}, u32[]{:S(2)}) %collective-permute-start.1) | collective-permute-done | bytes 73760 | tf_op jit(solution)/shard_map/ppermute | solution.py:57
  12.5 5.9 %collective-permute-start.2 = (f32[144,256]{1,0:T(8,128)S(1)}, f32[144,256]{1,0:T(8,128)S(1)}, u32[]{:S(2)}, u32[]{:S(2)}) collective-permute-start(f32[144,256]{1,0:T(8,128)S(1)} %get-tuple-element.52), channel_id=1, source_target_pairs={{1,2},{2,1},{3,4},{4,3},{5,6},{6,5},{9,10},{10,9},{11,12},{12,11},... | collective-permute-start | bytes 442376 | tf_op jit(solution)/shard_map/ppermute | solution.py:56
  18.4 1.9 %collective-permute-start.3 = (f32[144,256]{1,0:T(8,128)S(1)}, f32[144,256]{1,0:T(8,128)S(1)}, u32[]{:S(2)}, u32[]{:S(2)}) collective-permute-start(f32[144,256]{1,0:T(8,128)S(1)} %get-tuple-element.53), channel_id=1, source_target_pairs={{0,1},{1,0},{2,3},{3,2},{4,5},{5,4},{6,7},{7,6},{8,9},{9,8},{10,11... | collective-permute-start | bytes 442376 | tf_op jit(solution)/shard_map/ppermute | solution.py:57
  20.4 0.9 copy-done.4
  22.8 1.9 %shard_map.105 = (f32[3,128,256]{2,1,0:T(8,128)S(1)}, f32[128,256]{1,0:T(8,128)S(1)}, f32[128,256]{1,0:T(8,128)S(1)}, f32[128,256]{1,0:T(8,128)S(1)}, f32[2,24,2...) custom-call(f32[3,128,256]{2,1,0:T(8,128)S(1)} %bitcast.12, ...), custom_call_target="tpu_custom_call" | custom-call | flops 10000000 | bytes 4030464 | tf_op jit(solution)/shard_map/pallas_call | solution.py:35
  24.8 9.0 %all-to-all-start = ((f32[16,8,128]{2,1,0:T(8,128)}), f32[16,8,128]{2,1,0:T(8,128)S(1)}, u32[]{:S(2)}, u32[]{:S(2)}) async-start(f32[16,8,128]{2,1,0:T(8,128)} %get-tuple-element.66), calls=%async_computation | async-start | bytes 131072 | tf_op jit(solution)/shard_map/all_to_all | solution.py:62
  33.7 2.0 %collective-permute-start.5 = (f32[104,256]{1,0:T(8,128)S(1)}, f32[104,256]{1,0:T(8,128)S(1)}, u32[]{:S(2)}, u32[]{:S(2)}) collective-permute-start(f32[104,256]{1,0:T(8,128)S(1)} %get-tuple-element.58), channel_id=1, source_target_pairs={{0,1},{1,0},{2,3},{3,2},{4,5},{5,4},{6,7},{7,6},{8,9},{9,8},{10,11... | collective-permute-start | bytes 319496 | tf_op jit(solution)/shard_map/ppermute | solution.py:57
  35.8 4.5 %collective-permute-start.4 = (f32[104,256]{1,0:T(8,128)S(1)}, f32[104,256]{1,0:T(8,128)S(1)}, u32[]{:S(2)}, u32[]{:S(2)}) collective-permute-start(f32[104,256]{1,0:T(8,128)S(1)} %get-tuple-element.57), channel_id=1, source_target_pairs={{1,2},{2,1},{3,4},{4,3},{5,6},{6,5},{9,10},{10,9},{11,12},{12,11},... | collective-permute-start | bytes 319496 | tf_op jit(solution)/shard_map/ppermute | solution.py:56
  40.3 1.3 %all-to-all-done.row = f32[16,8,128]{2,1,0:T(8,128)S(1)} async-done(((f32[16,8,128]{2,1,0:T(8,128)}), f32[16,8,128]{2,1,0:T(8,128)S(1)}, u32[]{:S(2)}, u32[]{:S(2)}) %all-to-all-start) | async-done | bytes 65568 | tf_op jit(solution)/shard_map/all_to_all | solution.py:62
  42.2 12.0 %all-to-all-start.1 = ((f32[32,2,128]{2,1,0:T(2,128)}), f32[32,2,128]{2,1,0:T(2,128)S(1)}, u32[]{:S(2)}, u32[]{:S(2)}) async-start(f32[32,2,128]{2,1,0:T(2,128)} %shard_map.108), calls=%async_computation.1 | async-start | bytes 65536 | tf_op jit(solution)/shard_map/all_to_all | solution.py:62
  54.9 5.6 %collective-permute-start.7 = (f32[56,256]{1,0:T(8,128)S(1)}, f32[56,256]{1,0:T(8,128)S(1)}, u32[]{:S(2)}, u32[]{:S(2)}) collective-permute-start(f32[56,256]{1,0:T(8,128)S(1)} %get-tuple-element.60), channel_id=1, source_target_pairs={{0,8},{8,0},{16,24},{24,16},{32,40},{40,32},{48,56},{56,48},{64,72... | collective-permute-start | bytes 172040 | tf_op jit(solution)/shard_map/ppermute | solution.py:57
  60.5 1.8 %collective-permute-done.7.sx_near = f32[56,256]{1,0:T(8,128)S(1)} collective-permute-done((f32[56,256]{1,0:T(8,128)S(1)}, f32[56,256]{1,0:T(8,128)S(1)}, u32[]{:S(2)}, u32[]{:S(2)}) %collective-permute-start.7) | collective-permute-done | bytes 57376 | tf_op jit(solution)/shard_map/ppermute | solution.py:57
  63.0 2.0 %shard_map.109 = (f32[6,128,256]{2,1,0:T(8,128)}, f32[128,256]{1,0:T(8,128)}, f32[128,256]{1,0:T(8,128)}, f32[3,128,256]{2,1,0:T(8,128)S(1)}, f32[3,128,256]{2,1...) custom-call(f32[3,128,256]{2,1,0:T(8,128)S(1)} %bitcast.13, ...), custom_call_target="tpu_custom_call" | custom-call | flops 10000000 | bytes 4489216 | tf_op jit(solution)/shard_map/pallas_call | solution.py:35
  64.9 7.8 %all-to-all-start.2 = ((f32[32,2,128]{2,1,0:T(2,128)}), f32[32,2,128]{2,1,0:T(2,128)S(1)}, u32[]{:S(2)}, u32[]{:S(2)}) async-start(f32[32,2,128]{2,1,0:T(2,128)} %get-tuple-element.77), calls=%async_computation.2 | async-start | bytes 65536 | tf_op jit(solution)/shard_map/all_to_all | solution.py:62
  72.7 3.1 %collective-permute-start.9 = (f32[24,256]{1,0:T(8,128)S(1)}, f32[24,256]{1,0:T(8,128)S(1)}, u32[]{:S(2)}, u32[]{:S(2)}) collective-permute-start(f32[24,256]{1,0:T(8,128)S(1)} %get-tuple-element.73), channel_id=1, source_target_pairs={{0,8},{8,0},{16,24},{24,16},{32,40},{40,32},{48,56},{56,48},{64,72... | collective-permute-start | bytes 73736 | tf_op jit(solution)/shard_map/ppermute | solution.py:57
  76.5 0.8 collective-permute-done.9.near.sx_near
  77.3 4.2 %all-to-all-done.2.row = f32[32,2,128]{2,1,0:T(2,128)S(1)} async-done(((f32[32,2,128]{2,1,0:T(2,128)}), f32[32,2,128]{2,1,0:T(2,128)S(1)}, u32[]{:S(2)}, u32[]{:S(2)}) %all-to-all-start.2) | async-done | bytes 32800 | tf_op jit(solution)/shard_map/all_to_all | solution.py:62
  82.1 8.2 %all-to-all-start.3 = ((f32[16,8,128]{2,1,0:T(8,128)}), f32[16,8,128]{2,1,0:T(8,128)S(1)}, u32[]{:S(2)}, u32[]{:S(2)}) async-start(f32[16,8,128]{2,1,0:T(8,128)} %shard_map.111), calls=%async_computation.3 | async-start | bytes 131072 | tf_op jit(solution)/shard_map/all_to_all | solution.py:62
  90.4 4.4 %collective-permute-start.10 = (f32[48,256]{1,0:T(8,128)S(1)}, f32[48,256]{1,0:T(8,128)S(1)}, u32[]{:S(2)}, u32[]{:S(2)}) collective-permute-start(f32[48,256]{1,0:T(8,128)S(1)} %get-tuple-element.75), channel_id=1, source_target_pairs={{1,2},{2,1},{3,4},{4,3},{5,6},{6,5},{9,10},{10,9},{11,12},{12,11},... | collective-permute-start | bytes 147464 | tf_op jit(solution)/shard_map/ppermute | solution.py:56
  94.8 1.9 %collective-permute-start.11 = (f32[48,256]{1,0:T(8,128)S(1)}, f32[48,256]{1,0:T(8,128)S(1)}, u32[]{:S(2)}, u32[]{:S(2)}) collective-permute-start(f32[48,256]{1,0:T(8,128)S(1)} %get-tuple-element.76), channel_id=1, source_target_pairs={{0,1},{1,0},{2,3},{3,2},{4,5},{5,4},{6,7},{7,6},{8,9},{9,8},{10,11... | collective-permute-start | bytes 147464 | tf_op jit(solution)/shard_map/ppermute | solution.py:57
  97.0 1.0 collective-permute-done.11.sz_near
  98.2 0.9 shard_map.112
  (32 shorter events, 6.3 us)
Async XLA Ops:
  0.6 9.8 %copy-start.2 = (f32[16,8,256]{2,1,0:T(8,128)S(1)}, f32[16,8,256]{2,1,0:T(8,128)}, u32[]{:S(2)}) copy-start(f32[16,8,256]{2,1,0:T(8,128)} %param.9) | copy-start | bytes 393220
  0.6 11.7 %copy-start = (f32[3,16,8,256]{3,2,1,0:T(8,128)S(1)}, f32[3,16,8,256]{3,2,1,0:T(8,128)}, u32[]{:S(2)}) copy-start(f32[3,16,8,256]{3,2,1,0:T(8,128)} %param.6) | copy-start | bytes 1179652
  2.4 20.5 %copy-start.1 = (f32[6,16,8,256]{3,2,1,0:T(8,128)S(1)}, f32[6,16,8,256]{3,2,1,0:T(8,128)}, u32[]{:S(2)}) copy-start(f32[6,16,8,256]{3,2,1,0:T(8,128)} %param.8) | copy-start | bytes 2359300
  2.4 8.2 %collective-permute-start = (f32[72,256]{1,0:T(8,128)}, f32[72,256]{1,0:T(8,128)S(1)}, u32[]{:S(2)}, u32[]{:S(2)}) collective-permute-start(f32[72,256]{1,0:T(8,128)} %get-tuple-element.44), channel_id=1, source_target_pairs={{8,16},{16,8},{24,32},{32,24},{40,48},{48,40},{56,64},{64,56},{72,... | collective-permute-start | bytes 221192 | tf_op jit(solution)/shard_map/ppermute | solution.py:56
  3.2 9.2 %collective-permute-start.1 = (f32[72,256]{1,0:T(8,128)}, f32[72,256]{1,0:T(8,128)S(1)}, u32[]{:S(2)}, u32[]{:S(2)}) collective-permute-start(f32[72,256]{1,0:T(8,128)} %get-tuple-element.45), channel_id=1, source_target_pairs={{0,8},{8,0},{16,24},{24,16},{32,40},{40,32},{48,56},{56,48},{64,72... | collective-permute-start | bytes 221192 | tf_op jit(solution)/shard_map/ppermute | solution.py:57
  10.5 9.8 %copy-start.3 = (f32[16,8,256]{2,1,0:T(8,128)S(1)}, f32[16,8,256]{2,1,0:T(8,128)}, u32[]{:S(2)}) copy-start(f32[16,8,256]{2,1,0:T(8,128)} %param.10) | copy-start | bytes 393220
  12.5 10.3 %collective-permute-start.2 = (f32[144,256]{1,0:T(8,128)S(1)}, f32[144,256]{1,0:T(8,128)S(1)}, u32[]{:S(2)}, u32[]{:S(2)}) collective-permute-start(f32[144,256]{1,0:T(8,128)S(1)} %get-tuple-element.52), channel_id=1, source_target_pairs={{1,2},{2,1},{3,4},{4,3},{5,6},{6,5},{9,10},{10,9},{11,12},{12,11},... | collective-permute-start | bytes 442376 | tf_op jit(solution)/shard_map/ppermute | solution.py:56
  18.4 4.4 %collective-permute-start.3 = (f32[144,256]{1,0:T(8,128)S(1)}, f32[144,256]{1,0:T(8,128)S(1)}, u32[]{:S(2)}, u32[]{:S(2)}) collective-permute-start(f32[144,256]{1,0:T(8,128)S(1)} %get-tuple-element.53), channel_id=1, source_target_pairs={{0,1},{1,0},{2,3},{3,2},{4,5},{5,4},{6,7},{7,6},{8,9},{9,8},{10,11... | collective-permute-start | bytes 442376 | tf_op jit(solution)/shard_map/ppermute | solution.py:57
  20.4 0.9 copy-start.4
  21.3 1.6 %copy-start.5 = (f32[16,8,256]{2,1,0:T(8,128)S(1)}, f32[16,8,256]{2,1,0:T(8,128)}, u32[]{:S(2)}) copy-start(f32[16,8,256]{2,1,0:T(8,128)} %param.7) | copy-start | bytes 393220
  24.8 16.8 %all-to-all-start = ((f32[16,8,128]{2,1,0:T(8,128)}), f32[16,8,128]{2,1,0:T(8,128)S(1)}, u32[]{:S(2)}, u32[]{:S(2)}) async-start(f32[16,8,128]{2,1,0:T(8,128)} %get-tuple-element.66), calls=%async_computation | async-start | bytes 131072 | tf_op jit(solution)/shard_map/all_to_all | solution.py:62
  33.7 6.5 %collective-permute-start.5 = (f32[104,256]{1,0:T(8,128)S(1)}, f32[104,256]{1,0:T(8,128)S(1)}, u32[]{:S(2)}, u32[]{:S(2)}) collective-permute-start(f32[104,256]{1,0:T(8,128)S(1)} %get-tuple-element.58), channel_id=1, source_target_pairs={{0,1},{1,0},{2,3},{3,2},{4,5},{5,4},{6,7},{7,6},{8,9},{9,8},{10,11... | collective-permute-start | bytes 319496 | tf_op jit(solution)/shard_map/ppermute | solution.py:57
  35.8 18.4 %collective-permute-start.4 = (f32[104,256]{1,0:T(8,128)S(1)}, f32[104,256]{1,0:T(8,128)S(1)}, u32[]{:S(2)}, u32[]{:S(2)}) collective-permute-start(f32[104,256]{1,0:T(8,128)S(1)} %get-tuple-element.57), channel_id=1, source_target_pairs={{1,2},{2,1},{3,4},{4,3},{5,6},{6,5},{9,10},{10,9},{11,12},{12,11},... | collective-permute-start | bytes 319496 | tf_op jit(solution)/shard_map/ppermute | solution.py:56
  42.2 20.8 %all-to-all-start.1 = ((f32[32,2,128]{2,1,0:T(2,128)}), f32[32,2,128]{2,1,0:T(2,128)S(1)}, u32[]{:S(2)}, u32[]{:S(2)}) async-start(f32[32,2,128]{2,1,0:T(2,128)} %shard_map.108), calls=%async_computation.1 | async-start | bytes 65536 | tf_op jit(solution)/shard_map/all_to_all | solution.py:62
  54.2 6.2 %collective-permute-start.6 = (f32[56,256]{1,0:T(8,128)S(1)}, f32[56,256]{1,0:T(8,128)S(1)}, u32[]{:S(2)}, u32[]{:S(2)}) collective-permute-start(f32[56,256]{1,0:T(8,128)S(1)} %get-tuple-element.59), channel_id=1, source_target_pairs={{8,16},{16,8},{24,32},{32,24},{40,48},{48,40},{56,64},{64,56},{72,... | collective-permute-start | bytes 172040 | tf_op jit(solution)/shard_map/ppermute | solution.py:56
  54.9 7.4 %collective-permute-start.7 = (f32[56,256]{1,0:T(8,128)S(1)}, f32[56,256]{1,0:T(8,128)S(1)}, u32[]{:S(2)}, u32[]{:S(2)}) collective-permute-start(f32[56,256]{1,0:T(8,128)S(1)} %get-tuple-element.60), channel_id=1, source_target_pairs={{0,8},{8,0},{16,24},{24,16},{32,40},{40,32},{48,56},{56,48},{64,72... | collective-permute-start | bytes 172040 | tf_op jit(solution)/shard_map/ppermute | solution.py:57
  64.9 16.6 %all-to-all-start.2 = ((f32[32,2,128]{2,1,0:T(2,128)}), f32[32,2,128]{2,1,0:T(2,128)S(1)}, u32[]{:S(2)}, u32[]{:S(2)}) async-start(f32[32,2,128]{2,1,0:T(2,128)} %get-tuple-element.77), calls=%async_computation.2 | async-start | bytes 65536 | tf_op jit(solution)/shard_map/all_to_all | solution.py:62
  72.7 4.6 %collective-permute-start.9 = (f32[24,256]{1,0:T(8,128)S(1)}, f32[24,256]{1,0:T(8,128)S(1)}, u32[]{:S(2)}, u32[]{:S(2)}) collective-permute-start(f32[24,256]{1,0:T(8,128)S(1)} %get-tuple-element.73), channel_id=1, source_target_pairs={{0,8},{8,0},{16,24},{24,16},{32,40},{40,32},{48,56},{56,48},{64,72... | collective-permute-start | bytes 73736 | tf_op jit(solution)/shard_map/ppermute | solution.py:57
  75.8 14.6 %collective-permute-start.8 = (f32[72,256]{1,0:T(8,128)S(1)}, f32[72,256]{1,0:T(8,128)S(1)}, u32[]{:S(2)}, u32[]{:S(2)}) collective-permute-start(f32[72,256]{1,0:T(8,128)S(1)} %get-tuple-element.72), channel_id=1, source_target_pairs={{8,16},{16,8},{24,32},{32,24},{40,48},{48,40},{56,64},{64,56},{72,... | collective-permute-start | bytes 221192 | tf_op jit(solution)/shard_map/ppermute | solution.py:56
  82.1 16.0 %all-to-all-start.3 = ((f32[16,8,128]{2,1,0:T(8,128)}), f32[16,8,128]{2,1,0:T(8,128)S(1)}, u32[]{:S(2)}, u32[]{:S(2)}) async-start(f32[16,8,128]{2,1,0:T(8,128)} %shard_map.111), calls=%async_computation.3 | async-start | bytes 131072 | tf_op jit(solution)/shard_map/all_to_all | solution.py:62
  90.4 6.6 %collective-permute-start.10 = (f32[48,256]{1,0:T(8,128)S(1)}, f32[48,256]{1,0:T(8,128)S(1)}, u32[]{:S(2)}, u32[]{:S(2)}) collective-permute-start(f32[48,256]{1,0:T(8,128)S(1)} %get-tuple-element.75), channel_id=1, source_target_pairs={{1,2},{2,1},{3,4},{4,3},{5,6},{6,5},{9,10},{10,9},{11,12},{12,11},... | collective-permute-start | bytes 147464 | tf_op jit(solution)/shard_map/ppermute | solution.py:56
  94.8 3.1 %collective-permute-start.11 = (f32[48,256]{1,0:T(8,128)S(1)}, f32[48,256]{1,0:T(8,128)S(1)}, u32[]{:S(2)}, u32[]{:S(2)}) collective-permute-start(f32[48,256]{1,0:T(8,128)S(1)} %get-tuple-element.76), channel_id=1, source_target_pairs={{0,1},{1,0},{2,3},{3,2},{4,5},{5,4},{6,7},{7,6},{8,9},{9,8},{10,11... | collective-permute-start | bytes 147464 | tf_op jit(solution)/shard_map/ppermute | solution.py:57

commit v7 on v6

--- a/solution.py
+++ b/solution.py
@@ -319,7 +319,7 @@
 
 def first_kernel(
     v, pressure, old, plastic, eta_in, weak, own, from_z, along_y, x_far, x_near, z_far, z_near,
-    part, pres, total, cohesion_out, vx_out, vz_out, gx, fz, row_out, sz_far, sz_near,
+    part, pres, total, cohesion_out, vx_out, vz_out, gx, fz, pz, row_out, sx_far, sx_near,
     face, slots, held,
 ):
     low, high = sides(even_z(), z_far[...], z_near[...])
@@ -357,63 +357,60 @@
     partial_residual(held, part, masks)
     x_faces(held, ALONG_X, gx)
     z_faces(held, ALONG_Z, fz, slots)
-    even = even_z()
-    a, b = facing(even, fz[0], fz[1])
-    sz_far[0 : 3 * LX], sz_near[0 : 3 * LX] = a, b
-    for i in range(3):
-        keep(slots, 3 + i, part[i])
-        a, b = facing(even, layer(slots, 3 + i, 0), layer(slots, 3 + i, LZ - 1))
-        sz_far[(3 + i) * LX : (4 + i) * LX] = a
-        sz_near[(3 + i) * LX : (4 + i) * LX] = b
-    corners = []
-    for z in (0, LZ - 1):
-        ends = [held[f, x * LZ + z : x * LZ + z + 1] for f in (XX, XY) for x in (0, LX - 1)]
-        corners.append(jnp.concatenate(ends + ends, axis=0))
-    a, b = facing(even, *corners)
-    sz_far[6 * LX :], sz_near[6 * LX :] = a, b
-
-
-def x_pack_kernel(part, gx, sz_far, sz_near, sx_far, sx_near):
-    low, high = sides(even_z(), sz_far[...], sz_near[...])
-    z = lax.broadcasted_iota(jnp.int32, (LZ, NY), 0)
+    z_faces(part, range(3), pz, slots)
     messages = []
     for e, x in enumerate((0, LX - 1)):
-        pieces = [gx[e]]
+        layer_x = slice(x * LZ, (x + 1) * LZ)
+        ends = [held[f, x * LZ + z : x * LZ + z + 1] for f in (ZZ, ZY) for z in (0, LZ - 1)]
+        pieces = [gx[e]] + [part[f, layer_x] for f in range(3)] + [jnp.concatenate(ends + ends, axis=0)]
+        messages.append(jnp.concatenate(pieces, axis=0))
+    for out, message in zip((sx_far, sx_near), facing(even_x(), *messages)):
+        out[0 : 7 * LZ] = message
+        if out.shape[0] > 7 * LZ:
+            out[7 * LZ :] = jnp.zeros((out.shape[0] - 7 * LZ, NY), F32)
+
+
+def z_share_kernel(fz, pz, sx_far, sx_near, sz_far, sz_near):
+    low, high = sides(even_x(), sx_far[0 : 7 * LZ], sx_near[0 : 7 * LZ])
+    x = lax.broadcasted_iota(jnp.int32, (LX, NY), 0)
+    messages = []
+    for e, z in enumerate((0, LZ - 1)):
+        pieces = [fz[e]]
         for f in range(3):
-            below_z, above_z = (h[f * LX + x : f * LX + x + 1] for h in (low, high))
+            at = slice(f * LZ + z, f * LZ + z + 1)
             pieces.append(
-                part[f, x * LZ : (x + 1) * LZ]
-                - jnp.where(z == 0, below_z * 0.5, 0.0)
-                + jnp.where(z == LZ - 1, above_z * 0.5, 0.0)
+                pz[e, f * LX : (f + 1) * LX]
+                - jnp.where(x == 0, low[at] * 0.5, 0.0)
+                + jnp.where(x == LX - 1, high[at] * 0.5, 0.0)
             )
         ends = []
         for h in (low, high):
-            ends += [h[6 * LX + e : 6 * LX + e + 1], h[x : x + 1], h[6 * LX + 2 + e : 6 * LX + 3 + e]]
+            rows = (LZ + z, 6 * LZ + e, 6 * LZ + 2 + e)
+            ends += [h[at : at + 1] for at in rows]
         pieces.append(jnp.concatenate(ends + ends[:2], axis=0))
         messages.append(jnp.concatenate(pieces, axis=0))
-    sx_far[...], sx_near[...] = facing(even_x(), *messages)
+    sz_far[...], sz_near[...] = facing(even_z(), *messages)
 
 
 def residual_kernel(part, gx, fz, sx_far, sx_near, sz_far, sz_near, out, rx, rz, face):
-    x_low, x_high = sides(even_x(), sx_far[...], sx_near[...])
+    x_low, x_high = sides(even_x(), sx_far[0 : 7 * LZ], sx_near[0 : 7 * LZ])
     z_low, z_high = sides(even_z(), sz_far[...], sz_near[...])
     for f, here, value in whole_residual(part, x_low, x_high, z_low, z_high, face, iotas()):
         out[f, here] = value
-    has_low, has_high = place(GX)
-    rx[0] = jnp.where(has_low, x_low[3 * LZ : 6 * LZ] + gx[0] * 0.5, 0.0)
-    rx[1] = jnp.where(has_high, x_high[3 * LZ : 6 * LZ] - gx[1] * 0.5, 0.0)
-    x = lax.broadcasted_iota(jnp.int32, (LX, NY), 0)
+    z = lax.broadcasted_iota(jnp.int32, (LZ, NY), 0)
+    for side, (has, slab, sign) in enumerate(zip(place(GX), (x_low, x_high), (0.5, -0.5))):
+        for f in range(3):
+            rows = slice(f * LZ, (f + 1) * LZ)
+            end = 6 * LX + 3 * side + f
+            value = (
+                slab[(3 + f) * LZ : (4 + f) * LZ]
+                + gx[side, rows] * sign
+                - jnp.where(z == 0, z_low[end : end + 1] * 0.5, 0.0)
+                + jnp.where(z == LZ - 1, z_high[end : end + 1] * 0.5, 0.0)
+            )
+            rx[side, rows] = jnp.where(has, value, 0.0)
     for side, (has, slab, sign) in enumerate(zip(place(GZ), (z_low, z_high), (0.5, -0.5))):
-        for f in range(3):
-            rows = slice(f * LX, (f + 1) * LX)
-            end = 6 * LZ + 3 * side + f
-            value = (
-                slab[(3 + f) * LX : (4 + f) * LX]
-                + fz[side, rows] * sign
-                - jnp.where(x == 0, x_low[end : end + 1] * 0.5, 0.0)
-                + jnp.where(x == LX - 1, x_high[end : end + 1] * 0.5, 0.0)
-            )
-            rz[side, rows] = jnp.where(has, value, 0.0)
+        rz[side] = jnp.where(has, slab[3 * LX : 6 * LX] + fz[side] * sign, 0.0)
 
 
 def relay_kernel(near, row, row_out):
@@ -505,20 +502,19 @@
     eta, weak, *tables = call(
         own_kernel, [one, one, one, one, (NY, NY)], [along, viscosity, weak_seed], 10**7
     )
-    x_two, z_two, x_full, z_full = (2,) + x_3, (2,) + z_3, (7 * LZ, NY), (6 * LX + 8, NY)
-    part, pres, total, cohesion, vx, vz, gx, fz, row, *sent = call(
+    x_two, z_two, z_full = (2,) + x_3, (2,) + z_3, (6 * LX + 8, NY)
+    part, pres, total, cohesion, vx, vz, gx, fz, pz, row, *sent = call(
         first_kernel,
-        [three, one, one, one, x_two, z_two, x_two, z_two, row_1, z_full, z_full],
+        [three, one, one, one, x_two, z_two, x_two, z_two, z_two, row_2, (56, NY), (56, NY)],
         [v, pressure, old, plastic, eta, weak, *tables, *x_msgs, *z_msgs],
         10**7,
         [face, slots, pltpu.VMEM(six, F32)],
     )
+    row = spread(row, XZ)
+    x_got = exchange(GX, *sent)
+    (row,) = call(relay_kernel, [row_1], [x_got[1], row], 10**4)
     row = spread(row, YCORE)
-    z_got = exchange(GZ, *sent)
-    (row,) = call(relay_kernel, [row_2], [z_got[1], row], 10**4)
-    row = spread(row, XZ)
-    sent = call(x_pack_kernel, [x_full, x_full], [part, gx, *z_got], 10**5)
-    x_got = exchange(GX, *sent)
+    z_got = exchange(GZ, *call(z_share_kernel, [z_full, z_full], [fz, pz, *x_got], 10**5))
     res, rx, rz = call(
         residual_kernel, [three, x_two, z_two], [part, gx, fz, *x_got, *z_got], 10**6, [face]
     )

time: 99.8 us -> 101 us (1.012)
  waiting for transfers between devices: 12.7 us -> 16 us
  starting transfers between devices: 75.6 us -> 73.6 us
    ppermute x6, starting transfers between devices: 21.7 us -> 18.4 us  [exchange(): lax.ppermute(near, axis, pairs(count, 0))]
    all_to_all x4, waiting for transfers between devices: 6.22 us -> 7.59 us  [spread(): return lax.all_to_all(row, axes, 0, 0, tiled=True)]
    all_to_all x4, starting transfers between devices: 36.9 us -> 38.2 us  [spread(): return lax.all_to_all(row, axes, 0, 0, tiled=True)]
    ppermute x6, waiting for transfers between devices: 1.02 us -> 2.27 us  [exchange(): lax.ppermute(far, axis, pairs(count, 1))]
where the time goes in v7:
time: 101 us
  starting transfers between devices  73.6 us (73%)
  waiting for transfers between devices  16 us (16%)
  Pallas kernels  9.09 us (9%)
    all_to_all x4, starting transfers between devices, spread(): return lax.all_to_all(row, axes, 0, 0, tiled=True)  38.2 us
    ppermute x6, starting transfers between devices, exchange(): lax.ppermute(near, axis, pairs(count, 0))  18.4 us
    ppermute x6, starting transfers between devices, exchange(): lax.ppermute(far, axis, pairs(count, 1))  16.9 us
    pallas_call x12, Pallas kernels, call(): pl.pallas_call(kernel, out_shape=[jax.ShapeDtypeStruct(s, F32) for s in o...  9.09 us
    all_to_all x4, waiting for transfers between devices, spread(): return lax.all_to_all(row, axes, 0, 0, tiled=True)  7.59 us
    ppermute x6, waiting for transfers between devices, exchange(): lax.ppermute(near, axis, pairs(count, 0))  6.17 us
    ppermute x6, waiting for transfers between devices, exchange(): lax.ppermute(far, axis, pairs(count, 1))  2.27 us
  transfers between devices with their start and end apart: 16, of which 10 were waited for; matrix products, arithmetic and copies ran while one was open for 0% of the time, Pallas kernels for 2%

profile of v7, /device:TPU:1, one launch (start us, length us, event | category | flops | bytes accessed | tf_op | source)
XLA Modules:
  0.0 100.5 jit_solution(10599503354925425531)
XLA Ops:
  0.7 1.7 %shard_map.102 = (f32[72,256]{1,0:T(8,128)}, f32[72,256]{1,0:T(8,128)}) custom-call(f32[3,128,256]{2,1,0:T(8,128)} %bitcast.10, f32[128,256]{1,0:T(8,128)} %bitcast.16), custom_call_target="tpu_custom_call" | custom-call | bytes 671744 | tf_op jit(solution)/shard_map/pallas_call | solution.py:35
  3.2 7.3 %collective-permute-start.1 = (f32[72,256]{1,0:T(8,128)}, f32[72,256]{1,0:T(8,128)S(1)}, u32[]{:S(2)}, u32[]{:S(2)}) collective-permute-start(f32[72,256]{1,0:T(8,128)} %get-tuple-element.46), channel_id=1, source_target_pairs={{0,8},{8,0},{16,24},{24,16},{32,40},{40,32},{48,56},{56,48},{64,72... | collective-permute-start | bytes 221192 | tf_op jit(solution)/shard_map/ppermute | solution.py:57
  10.6 1.8 %collective-permute-done.1.x_near = f32[72,256]{1,0:T(8,128)S(1)} collective-permute-done((f32[72,256]{1,0:T(8,128)}, f32[72,256]{1,0:T(8,128)S(1)}, u32[]{:S(2)}, u32[]{:S(2)}) %collective-permute-start.1) | collective-permute-done | bytes 73760 | tf_op jit(solution)/shard_map/ppermute | solution.py:57
  12.5 5.9 %collective-permute-start.2 = (f32[144,256]{1,0:T(8,128)S(1)}, f32[144,256]{1,0:T(8,128)S(1)}, u32[]{:S(2)}, u32[]{:S(2)}) collective-permute-start(f32[144,256]{1,0:T(8,128)S(1)} %get-tuple-element.53), channel_id=1, source_target_pairs={{1,2},{2,1},{3,4},{4,3},{5,6},{6,5},{9,10},{10,9},{11,12},{12,11},... | collective-permute-start | bytes 442376 | tf_op jit(solution)/shard_map/ppermute | solution.py:56
  18.4 1.9 %collective-permute-start.3 = (f32[144,256]{1,0:T(8,128)S(1)}, f32[144,256]{1,0:T(8,128)S(1)}, u32[]{:S(2)}, u32[]{:S(2)}) collective-permute-start(f32[144,256]{1,0:T(8,128)S(1)} %get-tuple-element.54), channel_id=1, source_target_pairs={{0,1},{1,0},{2,3},{3,2},{4,5},{5,4},{6,7},{7,6},{8,9},{9,8},{10,11... | collective-permute-start | bytes 442376 | tf_op jit(solution)/shard_map/ppermute | solution.py:57
  22.8 1.9 %shard_map.105 = (f32[3,128,256]{2,1,0:T(8,128)S(1)}, f32[128,256]{1,0:T(8,128)S(1)}, f32[128,256]{1,0:T(8,128)S(1)}, f32[128,256]{1,0:T(8,128)S(1)}, f32[2,24,2...) custom-call(f32[3,128,256]{2,1,0:T(8,128)S(1)} %bitcast.12, ...), custom_call_target="tpu_custom_call" | custom-call | flops 10000000 | bytes 3997696 | tf_op jit(solution)/shard_map/pallas_call | solution.py:35
  24.8 12.6 %all-to-all-start = ((f32[32,2,128]{2,1,0:T(2,128)}), f32[32,2,128]{2,1,0:T(2,128)S(1)}, u32[]{:S(2)}, u32[]{:S(2)}) async-start(f32[32,2,128]{2,1,0:T(2,128)} %get-tuple-element.68), calls=%async_computation | async-start | bytes 65536 | tf_op jit(solution)/shard_map/all_to_all | solution.py:62
  37.4 2.3 %collective-permute-start.5 = (f32[56,256]{1,0:T(8,128)S(1)}, f32[56,256]{1,0:T(8,128)S(1)}, u32[]{:S(2)}, u32[]{:S(2)}) collective-permute-start(f32[56,256]{1,0:T(8,128)S(1)} %get-tuple-element.59), channel_id=1, source_target_pairs={{0,8},{8,0},{16,24},{24,16},{32,40},{40,32},{48,56},{56,48},{64,72... | collective-permute-start | bytes 172040 | tf_op jit(solution)/shard_map/ppermute | solution.py:57
  40.4 2.3 %collective-permute-done.5.sx_near.near = f32[56,256]{1,0:T(8,128)S(1)} collective-permute-done((f32[56,256]{1,0:T(8,128)S(1)}, f32[56,256]{1,0:T(8,128)S(1)}, u32[]{:S(2)}, u32[]{:S(2)}) %collective-permute-start.5) | collective-permute-done | bytes 57376 | tf_op jit(solution)/shard_map/ppermute | solution.py:57
  42.7 3.5 %all-to-all-done.row = f32[32,2,128]{2,1,0:T(2,128)S(1)} async-done(((f32[32,2,128]{2,1,0:T(2,128)}), f32[32,2,128]{2,1,0:T(2,128)S(1)}, u32[]{:S(2)}, u32[]{:S(2)}) %all-to-all-start) | async-done | bytes 32800 | tf_op jit(solution)/shard_map/all_to_all | solution.py:62
  46.8 9.7 %all-to-all-start.1 = ((f32[16,8,128]{2,1,0:T(8,128)}), f32[16,8,128]{2,1,0:T(8,128)S(1)}, u32[]{:S(2)}, u32[]{:S(2)}) async-start(f32[16,8,128]{2,1,0:T(8,128)} %shard_map.108), calls=%async_computation.1 | async-start | bytes 131072 | tf_op jit(solution)/shard_map/all_to_all | solution.py:62
  56.6 4.4 %collective-permute-start.6 = (f32[104,256]{1,0:T(8,128)S(1)}, f32[104,256]{1,0:T(8,128)S(1)}, u32[]{:S(2)}, u32[]{:S(2)}) collective-permute-start(f32[104,256]{1,0:T(8,128)S(1)} %get-tuple-element.61), channel_id=1, source_target_pairs={{1,2},{2,1},{3,4},{4,3},{5,6},{6,5},{9,10},{10,9},{11,12},{12,11},... | collective-permute-start | bytes 319496 | tf_op jit(solution)/shard_map/ppermute | solution.py:56
  61.1 1.9 %collective-permute-start.7 = (f32[104,256]{1,0:T(8,128)S(1)}, f32[104,256]{1,0:T(8,128)S(1)}, u32[]{:S(2)}, u32[]{:S(2)}) collective-permute-start(f32[104,256]{1,0:T(8,128)S(1)} %get-tuple-element.62), channel_id=1, source_target_pairs={{0,1},{1,0},{2,3},{3,2},{4,5},{5,4},{6,7},{7,6},{8,9},{9,8},{10,11... | collective-permute-start | bytes 319496 | tf_op jit(solution)/shard_map/ppermute | solution.py:57
  63.0 1.3 %collective-permute-done.6.sz_far = f32[104,256]{1,0:T(8,128)S(1)} collective-permute-done((f32[104,256]{1,0:T(8,128)S(1)}, f32[104,256]{1,0:T(8,128)S(1)}, u32[]{:S(2)}, u32[]{:S(2)}) %collective-permute-start.6) | collective-permute-done | bytes 106528 | tf_op jit(solution)/shard_map/ppermute | solution.py:56
  64.5 2.0 %shard_map.109 = (f32[6,128,256]{2,1,0:T(8,128)}, f32[128,256]{1,0:T(8,128)}, f32[128,256]{1,0:T(8,128)}, f32[3,128,256]{2,1,0:T(8,128)S(1)}, f32[3,128,256]{2,1...) custom-call(f32[3,128,256]{2,1,0:T(8,128)S(1)} %bitcast.13, ...), custom_call_target="tpu_custom_call" | custom-call | flops 10000000 | bytes 4521984 | tf_op jit(solution)/shard_map/pallas_call | solution.py:35
  66.5 5.7 %all-to-all-start.2 = ((f32[32,2,128]{2,1,0:T(2,128)}), f32[32,2,128]{2,1,0:T(2,128)S(1)}, u32[]{:S(2)}, u32[]{:S(2)}) async-start(f32[32,2,128]{2,1,0:T(2,128)} %get-tuple-element.79), calls=%async_computation.2 | async-start | bytes 65536 | tf_op jit(solution)/shard_map/all_to_all | solution.py:62
  72.2 3.1 %collective-permute-start.9 = (f32[24,256]{1,0:T(8,128)S(1)}, f32[24,256]{1,0:T(8,128)S(1)}, u32[]{:S(2)}, u32[]{:S(2)}) collective-permute-start(f32[24,256]{1,0:T(8,128)S(1)} %get-tuple-element.75), channel_id=1, source_target_pairs={{0,8},{8,0},{16,24},{24,16},{32,40},{40,32},{48,56},{56,48},{64,72... | collective-permute-start | bytes 73736 | tf_op jit(solution)/shard_map/ppermute | solution.py:57
  75.9 1.1 %collective-permute-done.9.near.sx_near = f32[24,256]{1,0:T(8,128)S(1)} collective-permute-done((f32[24,256]{1,0:T(8,128)S(1)}, f32[24,256]{1,0:T(8,128)S(1)}, u32[]{:S(2)}, u32[]{:S(2)}) %collective-permute-start.9) | collective-permute-done | bytes 24608 | tf_op jit(solution)/shard_map/ppermute | solution.py:57
  77.0 3.9 %all-to-all-done.2.row = f32[32,2,128]{2,1,0:T(2,128)S(1)} async-done(((f32[32,2,128]{2,1,0:T(2,128)}), f32[32,2,128]{2,1,0:T(2,128)S(1)}, u32[]{:S(2)}, u32[]{:S(2)}) %all-to-all-start.2) | async-done | bytes 32800 | tf_op jit(solution)/shard_map/all_to_all | solution.py:62
  81.6 10.2 %all-to-all-start.3 = ((f32[16,8,128]{2,1,0:T(8,128)}), f32[16,8,128]{2,1,0:T(8,128)S(1)}, u32[]{:S(2)}, u32[]{:S(2)}) async-start(f32[16,8,128]{2,1,0:T(8,128)} %shard_map.111), calls=%async_computation.3 | async-start | bytes 131072 | tf_op jit(solution)/shard_map/all_to_all | solution.py:62
  91.8 4.4 %collective-permute-start.10 = (f32[48,256]{1,0:T(8,128)S(1)}, f32[48,256]{1,0:T(8,128)S(1)}, u32[]{:S(2)}, u32[]{:S(2)}) collective-permute-start(f32[48,256]{1,0:T(8,128)S(1)} %get-tuple-element.77), channel_id=1, source_target_pairs={{1,2},{2,1},{3,4},{4,3},{5,6},{6,5},{9,10},{10,9},{11,12},{12,11},... | collective-permute-start | bytes 147464 | tf_op jit(solution)/shard_map/ppermute | solution.py:56
  96.2 1.9 %collective-permute-start.11 = (f32[48,256]{1,0:T(8,128)S(1)}, f32[48,256]{1,0:T(8,128)S(1)}, u32[]{:S(2)}, u32[]{:S(2)}) collective-permute-start(f32[48,256]{1,0:T(8,128)S(1)} %get-tuple-element.78), channel_id=1, source_target_pairs={{0,1},{1,0},{2,3},{3,2},{4,5},{5,4},{6,7},{7,6},{8,9},{9,8},{10,11... | collective-permute-start | bytes 147464 | tf_op jit(solution)/shard_map/ppermute | solution.py:57
  98.4 1.0 collective-permute-done.11.sz_near
  99.6 0.9 shard_map.112
  (32 shorter events, 6.8 us)
Async XLA Ops:
  0.6 9.8 %copy-start.2 = (f32[16,8,256]{2,1,0:T(8,128)S(1)}, f32[16,8,256]{2,1,0:T(8,128)}, u32[]{:S(2)}) copy-start(f32[16,8,256]{2,1,0:T(8,128)} %param.9) | copy-start | bytes 393220
  0.6 11.7 %copy-start = (f32[3,16,8,256]{3,2,1,0:T(8,128)S(1)}, f32[3,16,8,256]{3,2,1,0:T(8,128)}, u32[]{:S(2)}) copy-start(f32[3,16,8,256]{3,2,1,0:T(8,128)} %param.6) | copy-start | bytes 1179652
  2.4 20.5 %copy-start.1 = (f32[6,16,8,256]{3,2,1,0:T(8,128)S(1)}, f32[6,16,8,256]{3,2,1,0:T(8,128)}, u32[]{:S(2)}) copy-start(f32[6,16,8,256]{3,2,1,0:T(8,128)} %param.8) | copy-start | bytes 2359300
  2.4 8.2 %collective-permute-start = (f32[72,256]{1,0:T(8,128)}, f32[72,256]{1,0:T(8,128)S(1)}, u32[]{:S(2)}, u32[]{:S(2)}) collective-permute-start(f32[72,256]{1,0:T(8,128)} %get-tuple-element.45), channel_id=1, source_target_pairs={{8,16},{16,8},{24,32},{32,24},{40,48},{48,40},{56,64},{64,56},{72,... | collective-permute-start | bytes 221192 | tf_op jit(solution)/shard_map/ppermute | solution.py:56
  3.2 9.2 %collective-permute-start.1 = (f32[72,256]{1,0:T(8,128)}, f32[72,256]{1,0:T(8,128)S(1)}, u32[]{:S(2)}, u32[]{:S(2)}) collective-permute-start(f32[72,256]{1,0:T(8,128)} %get-tuple-element.46), channel_id=1, source_target_pairs={{0,8},{8,0},{16,24},{24,16},{32,40},{40,32},{48,56},{56,48},{64,72... | collective-permute-start | bytes 221192 | tf_op jit(solution)/shard_map/ppermute | solution.py:57
  10.5 9.8 %copy-start.3 = (f32[16,8,256]{2,1,0:T(8,128)S(1)}, f32[16,8,256]{2,1,0:T(8,128)}, u32[]{:S(2)}) copy-start(f32[16,8,256]{2,1,0:T(8,128)} %param.10) | copy-start | bytes 393220
  12.5 10.3 %collective-permute-start.2 = (f32[144,256]{1,0:T(8,128)S(1)}, f32[144,256]{1,0:T(8,128)S(1)}, u32[]{:S(2)}, u32[]{:S(2)}) collective-permute-start(f32[144,256]{1,0:T(8,128)S(1)} %get-tuple-element.53), channel_id=1, source_target_pairs={{1,2},{2,1},{3,4},{4,3},{5,6},{6,5},{9,10},{10,9},{11,12},{12,11},... | collective-permute-start | bytes 442376 | tf_op jit(solution)/shard_map/ppermute | solution.py:56
  18.4 4.4 %collective-permute-start.3 = (f32[144,256]{1,0:T(8,128)S(1)}, f32[144,256]{1,0:T(8,128)S(1)}, u32[]{:S(2)}, u32[]{:S(2)}) collective-permute-start(f32[144,256]{1,0:T(8,128)S(1)} %get-tuple-element.54), channel_id=1, source_target_pairs={{0,1},{1,0},{2,3},{3,2},{4,5},{5,4},{6,7},{7,6},{8,9},{9,8},{10,11... | collective-permute-start | bytes 442376 | tf_op jit(solution)/shard_map/ppermute | solution.py:57
  20.4 0.9 copy-start.4
  21.3 1.6 %copy-start.5 = (f32[16,8,256]{2,1,0:T(8,128)S(1)}, f32[16,8,256]{2,1,0:T(8,128)}, u32[]{:S(2)}) copy-start(f32[16,8,256]{2,1,0:T(8,128)} %param.7) | copy-start | bytes 393220
  24.8 21.4 %all-to-all-start = ((f32[32,2,128]{2,1,0:T(2,128)}), f32[32,2,128]{2,1,0:T(2,128)S(1)}, u32[]{:S(2)}, u32[]{:S(2)}) async-start(f32[32,2,128]{2,1,0:T(2,128)} %get-tuple-element.68), calls=%async_computation | async-start | bytes 65536 | tf_op jit(solution)/shard_map/all_to_all | solution.py:62
  37.4 5.3 %collective-permute-start.5 = (f32[56,256]{1,0:T(8,128)S(1)}, f32[56,256]{1,0:T(8,128)S(1)}, u32[]{:S(2)}, u32[]{:S(2)}) collective-permute-start(f32[56,256]{1,0:T(8,128)S(1)} %get-tuple-element.59), channel_id=1, source_target_pairs={{0,8},{8,0},{16,24},{24,16},{32,40},{40,32},{48,56},{56,48},{64,72... | collective-permute-start | bytes 172040 | tf_op jit(solution)/shard_map/ppermute | solution.py:57
  39.7 16.8 %collective-permute-start.4 = (f32[56,256]{1,0:T(8,128)S(1)}, f32[56,256]{1,0:T(8,128)S(1)}, u32[]{:S(2)}, u32[]{:S(2)}) collective-permute-start(f32[56,256]{1,0:T(8,128)S(1)} %get-tuple-element.58), channel_id=1, source_target_pairs={{8,16},{16,8},{24,32},{32,24},{40,48},{48,40},{56,64},{64,56},{72,... | collective-permute-start | bytes 172040 | tf_op jit(solution)/shard_map/ppermute | solution.py:56
  46.8 17.6 %all-to-all-start.1 = ((f32[16,8,128]{2,1,0:T(8,128)}), f32[16,8,128]{2,1,0:T(8,128)S(1)}, u32[]{:S(2)}, u32[]{:S(2)}) async-start(f32[16,8,128]{2,1,0:T(8,128)} %shard_map.108), calls=%async_computation.1 | async-start | bytes 131072 | tf_op jit(solution)/shard_map/all_to_all | solution.py:62
  56.6 7.6 %collective-permute-start.6 = (f32[104,256]{1,0:T(8,128)S(1)}, f32[104,256]{1,0:T(8,128)S(1)}, u32[]{:S(2)}, u32[]{:S(2)}) collective-permute-start(f32[104,256]{1,0:T(8,128)S(1)} %get-tuple-element.61), channel_id=1, source_target_pairs={{1,2},{2,1},{3,4},{4,3},{5,6},{6,5},{9,10},{10,9},{11,12},{12,11},... | collective-permute-start | bytes 319496 | tf_op jit(solution)/shard_map/ppermute | solution.py:56
  61.1 3.2 %collective-permute-start.7 = (f32[104,256]{1,0:T(8,128)S(1)}, f32[104,256]{1,0:T(8,128)S(1)}, u32[]{:S(2)}, u32[]{:S(2)}) collective-permute-start(f32[104,256]{1,0:T(8,128)S(1)} %get-tuple-element.62), channel_id=1, source_target_pairs={{0,1},{1,0},{2,3},{3,2},{4,5},{5,4},{6,7},{7,6},{8,9},{9,8},{10,11... | collective-permute-start | bytes 319496 | tf_op jit(solution)/shard_map/ppermute | solution.py:57
  66.5 14.4 %all-to-all-start.2 = ((f32[32,2,128]{2,1,0:T(2,128)}), f32[32,2,128]{2,1,0:T(2,128)S(1)}, u32[]{:S(2)}, u32[]{:S(2)}) async-start(f32[32,2,128]{2,1,0:T(2,128)} %get-tuple-element.79), calls=%async_computation.2 | async-start | bytes 65536 | tf_op jit(solution)/shard_map/all_to_all | solution.py:62
  72.2 4.9 %collective-permute-start.9 = (f32[24,256]{1,0:T(8,128)S(1)}, f32[24,256]{1,0:T(8,128)S(1)}, u32[]{:S(2)}, u32[]{:S(2)}) collective-permute-start(f32[24,256]{1,0:T(8,128)S(1)} %get-tuple-element.75), channel_id=1, source_target_pairs={{0,8},{8,0},{16,24},{24,16},{32,40},{40,32},{48,56},{56,48},{64,72... | collective-permute-start | bytes 73736 | tf_op jit(solution)/shard_map/ppermute | solution.py:57
  75.3 16.5 %collective-permute-start.8 = (f32[72,256]{1,0:T(8,128)S(1)}, f32[72,256]{1,0:T(8,128)S(1)}, u32[]{:S(2)}, u32[]{:S(2)}) collective-permute-start(f32[72,256]{1,0:T(8,128)S(1)} %get-tuple-element.74), channel_id=1, source_target_pairs={{8,16},{16,8},{24,32},{32,24},{40,48},{48,40},{56,64},{64,56},{72,... | collective-permute-start | bytes 221192 | tf_op jit(solution)/shard_map/ppermute | solution.py:56
  81.6 18.0 %all-to-all-start.3 = ((f32[16,8,128]{2,1,0:T(8,128)}), f32[16,8,128]{2,1,0:T(8,128)S(1)}, u32[]{:S(2)}, u32[]{:S(2)}) async-start(f32[16,8,128]{2,1,0:T(8,128)} %shard_map.111), calls=%async_computation.3 | async-start | bytes 131072 | tf_op jit(solution)/shard_map/all_to_all | solution.py:62
  91.8 6.6 %collective-permute-start.10 = (f32[48,256]{1,0:T(8,128)S(1)}, f32[48,256]{1,0:T(8,128)S(1)}, u32[]{:S(2)}, u32[]{:S(2)}) collective-permute-start(f32[48,256]{1,0:T(8,128)S(1)} %get-tuple-element.77), channel_id=1, source_target_pairs={{1,2},{2,1},{3,4},{4,3},{5,6},{6,5},{9,10},{10,9},{11,12},{12,11},... | collective-permute-start | bytes 147464 | tf_op jit(solution)/shard_map/ppermute | solution.py:56
  96.2 3.1 %collective-permute-start.11 = (f32[48,256]{1,0:T(8,128)S(1)}, f32[48,256]{1,0:T(8,128)S(1)}, u32[]{:S(2)}, u32[]{:S(2)}) collective-permute-start(f32[48,256]{1,0:T(8,128)S(1)} %get-tuple-element.78), channel_id=1, source_target_pairs={{0,1},{1,0},{2,3},{3,2},{4,5},{5,4},{6,7},{7,6},{8,9},{9,8},{10,11... | collective-permute-start | bytes 147464 | tf_op jit(solution)/shard_map/ppermute | solution.py:57

commit v8 on v6

--- a/solution.py
+++ b/solution.py
@@ -10,8 +10,6 @@
 
 GX = ("gx_0", "gx_1", "gx_2")
 GZ = ("gz_0", "gz_1")
-YCORE = ("gx_2", "gz_0", "gz_1")
-XZ = ("gx_0", "gx_1")
 
 WEIGHT_TOTAL = sum(math.exp(-(k * k) / 18.0) for k in range(-6, 7))
 WEIGHTS = [math.exp(-(k * k) / 18.0) / WEIGHT_TOTAL for k in range(-6, 7)]
@@ -492,8 +490,8 @@
     three, six = (3,) + one, (6,) + one
     face = pltpu.VMEM((2, 3, 2, ROWS, 128), F32)
     slots = pltpu.VMEM((6, 2, ROWS, 128), F32)
-    level_1, level_2 = lax.axis_size(YCORE), lax.axis_size(XZ)
-    row_1, row_2 = (level_1, 8, 128), (level_2, 2, 128)
+    level_1, level_2 = lax.axis_size(GZ), lax.axis_size(GX)
+    row_1, row_2 = (level_1, 16, 128), (level_2, 1, 128)
     x_3, z_3, x_9, z_9 = (3 * LZ, NY), (3 * LX, NY), (9 * LZ, NY), (9 * LX, NY)
 
     dma = pltpu.SemaphoreType.DMA
@@ -513,10 +511,10 @@
         10**7,
         [face, slots, pltpu.VMEM(six, F32)],
     )
-    row = spread(row, YCORE)
+    row = spread(row, GZ)
     z_got = exchange(GZ, *sent)
     (row,) = call(relay_kernel, [row_2], [z_got[1], row], 10**4)
-    row = spread(row, XZ)
+    row = spread(row, GX)
     sent = call(x_pack_kernel, [x_full, x_full], [part, gx, *z_got], 10**5)
     x_got = exchange(GX, *sent)
     res, rx, rz = call(
@@ -529,10 +527,10 @@
         10**7,
         [face, slots, pltpu.VMEM(x_two, F32), pltpu.VMEM(six, F32)],
     )
-    row = spread(row, XZ)
+    row = spread(row, GX)
     x_got = exchange(GX, *sent)
     (row,) = call(relay_kernel, [row_1], [x_got[1], row], 10**4)
-    row = spread(row, YCORE)
+    row = spread(row, GZ)
     z_got = exchange(GZ, *call(z_pack_kernel, [z_3, z_3], [fz, x_got[0]], 10**4))
     v, peaks = call(
         final_kernel,

time: 99.8 us -> 102 us (1.022)
  starting transfers between devices: 75.6 us -> 77 us
    all_to_all x4, starting transfers between devices: 36.9 us -> 38.7 us  [spread(): return lax.all_to_all(row, axes, 0, 0, tiled=True)]
  transfers between devices with their start and end apart: 16 -> 16, of which waited for: 10 -> 9; matrix products, arithmetic and copies ran while one was open for 0% -> 0% of each run, Pallas kernels for 2% -> 2%
where the time goes in v8:
time: 102 us; the launch traced here: 101 us
  starting transfers between devices  77 us (75%)
  waiting for transfers between devices  13.5 us (13%)
  Pallas kernels  8.96 us (9%)
    all_to_all x4, starting transfers between devices, spread(): return lax.all_to_all(row, axes, 0, 0, tiled=True)  38.7 us
    ppermute x6, starting transfers between devices, exchange(): lax.ppermute(near, axis, pairs(count, 0))  21.3 us
    ppermute x6, starting transfers between devices, exchange(): lax.ppermute(far, axis, pairs(count, 1))  17.1 us
    pallas_call x12, Pallas kernels, call(): pl.pallas_call(kernel, out_shape=[jax.ShapeDtypeStruct(s, F32) for s in o...  8.96 us
    all_to_all x4, waiting for transfers between devices, spread(): return lax.all_to_all(row, axes, 0, 0, tiled=True)  6.43 us
    ppermute x6, waiting for transfers between devices, exchange(): lax.ppermute(near, axis, pairs(count, 0))  5.46 us
  transfers between devices with their start and end apart: 16, of which 9 were waited for; matrix products, arithmetic and copies ran while one was open for 0% of the time, Pallas kernels for 2%

profile of v8, /device:TPU:1, one launch (start us, length us, event | category | flops | bytes accessed | tf_op | source)
XLA Modules:
  0.0 101.3 jit_solution(15018884830631614883)
XLA Ops:
  0.7 1.7 %shard_map.102 = (f32[72,256]{1,0:T(8,128)}, f32[72,256]{1,0:T(8,128)}) custom-call(f32[3,128,256]{2,1,0:T(8,128)} %bitcast.10, f32[128,256]{1,0:T(8,128)} %bitcast.16), custom_call_target="tpu_custom_call" | custom-call | bytes 671744 | tf_op jit(solution)/shard_map/pallas_call | solution.py:33
  3.2 7.3 %collective-permute-start.1 = (f32[72,256]{1,0:T(8,128)}, f32[72,256]{1,0:T(8,128)S(1)}, u32[]{:S(2)}, u32[]{:S(2)}) collective-permute-start(f32[72,256]{1,0:T(8,128)} %get-tuple-element.45), channel_id=1, source_target_pairs={{0,8},{8,0},{16,24},{24,16},{32,40},{40,32},{48,56},{56,48},{64,72... | collective-permute-start | bytes 221192 | tf_op jit(solution)/shard_map/ppermute | solution.py:55
  10.6 1.8 %collective-permute-done.1.x_near = f32[72,256]{1,0:T(8,128)S(1)} collective-permute-done((f32[72,256]{1,0:T(8,128)}, f32[72,256]{1,0:T(8,128)S(1)}, u32[]{:S(2)}, u32[]{:S(2)}) %collective-permute-start.1) | collective-permute-done | bytes 73760 | tf_op jit(solution)/shard_map/ppermute | solution.py:55
  12.5 5.9 %collective-permute-start.2 = (f32[144,256]{1,0:T(8,128)S(1)}, f32[144,256]{1,0:T(8,128)S(1)}, u32[]{:S(2)}, u32[]{:S(2)}) collective-permute-start(f32[144,256]{1,0:T(8,128)S(1)} %get-tuple-element.52), channel_id=1, source_target_pairs={{1,2},{2,1},{3,4},{4,3},{5,6},{6,5},{9,10},{10,9},{11,12},{12,11},... | collective-permute-start | bytes 442376 | tf_op jit(solution)/shard_map/ppermute | solution.py:54
  18.4 1.9 %collective-permute-start.3 = (f32[144,256]{1,0:T(8,128)S(1)}, f32[144,256]{1,0:T(8,128)S(1)}, u32[]{:S(2)}, u32[]{:S(2)}) collective-permute-start(f32[144,256]{1,0:T(8,128)S(1)} %get-tuple-element.53), channel_id=1, source_target_pairs={{0,1},{1,0},{2,3},{3,2},{4,5},{5,4},{6,7},{7,6},{8,9},{9,8},{10,11... | collective-permute-start | bytes 442376 | tf_op jit(solution)/shard_map/ppermute | solution.py:55
  20.4 0.9 copy-done.4
  22.8 1.9 %shard_map.105 = (f32[3,128,256]{2,1,0:T(8,128)S(1)}, f32[128,256]{1,0:T(8,128)S(1)}, f32[128,256]{1,0:T(8,128)S(1)}, f32[128,256]{1,0:T(8,128)S(1)}, f32[2,24,2...) custom-call(f32[3,128,256]{2,1,0:T(8,128)S(1)} %bitcast.12, ...), custom_call_target="tpu_custom_call" | custom-call | flops 10000000 | bytes 4030464 | tf_op jit(solution)/shard_map/pallas_call | solution.py:33
  24.8 8.8 %all-to-all-start = ((f32[8,16,128]{2,1,0:T(8,128)}), f32[8,16,128]{2,1,0:T(8,128)S(1)}, u32[]{:S(2)}, u32[]{:S(2)}) async-start(f32[8,16,128]{2,1,0:T(8,128)} %get-tuple-element.66), calls=%async_computation | async-start | bytes 131072 | tf_op jit(solution)/shard_map/all_to_all | solution.py:60
  33.5 1.9 %collective-permute-start.5 = (f32[104,256]{1,0:T(8,128)S(1)}, f32[104,256]{1,0:T(8,128)S(1)}, u32[]{:S(2)}, u32[]{:S(2)}) collective-permute-start(f32[104,256]{1,0:T(8,128)S(1)} %get-tuple-element.58), channel_id=1, source_target_pairs={{0,1},{1,0},{2,3},{3,2},{4,5},{5,4},{6,7},{7,6},{8,9},{9,8},{10,11... | collective-permute-start | bytes 319496 | tf_op jit(solution)/shard_map/ppermute | solution.py:55
  35.4 4.6 %collective-permute-start.4 = (f32[104,256]{1,0:T(8,128)S(1)}, f32[104,256]{1,0:T(8,128)S(1)}, u32[]{:S(2)}, u32[]{:S(2)}) collective-permute-start(f32[104,256]{1,0:T(8,128)S(1)} %get-tuple-element.57), channel_id=1, source_target_pairs={{1,2},{2,1},{3,4},{4,3},{5,6},{6,5},{9,10},{10,9},{11,12},{12,11},... | collective-permute-start | bytes 319496 | tf_op jit(solution)/shard_map/ppermute | solution.py:54
  40.0 1.3 %all-to-all-done.row = f32[8,16,128]{2,1,0:T(8,128)S(1)} async-done(((f32[8,16,128]{2,1,0:T(8,128)}), f32[8,16,128]{2,1,0:T(8,128)S(1)}, u32[]{:S(2)}, u32[]{:S(2)}) %all-to-all-start) | async-done | bytes 65568 | tf_op jit(solution)/shard_map/all_to_all | solution.py:60
  42.0 13.3 %all-to-all-start.1 = ((f32[64,1,128]{2,1,0:T(1,128)}), f32[64,1,128]{2,1,0:T(1,128)S(1)}, u32[]{:S(2)}, u32[]{:S(2)}) async-start(f32[64,1,128]{2,1,0:T(1,128)} %shard_map.108), calls=%async_computation.1 | async-start | bytes 65536 | tf_op jit(solution)/shard_map/all_to_all | solution.py:60
  56.0 5.3 %collective-permute-start.7 = (f32[56,256]{1,0:T(8,128)S(1)}, f32[56,256]{1,0:T(8,128)S(1)}, u32[]{:S(2)}, u32[]{:S(2)}) collective-permute-start(f32[56,256]{1,0:T(8,128)S(1)} %get-tuple-element.60), channel_id=1, source_target_pairs={{0,8},{8,0},{16,24},{24,16},{32,40},{40,32},{48,56},{56,48},{64,72... | collective-permute-start | bytes 172040 | tf_op jit(solution)/shard_map/ppermute | solution.py:55
  61.4 2.3 %collective-permute-done.7.sx_near = f32[56,256]{1,0:T(8,128)S(1)} collective-permute-done((f32[56,256]{1,0:T(8,128)S(1)}, f32[56,256]{1,0:T(8,128)S(1)}, u32[]{:S(2)}, u32[]{:S(2)}) %collective-permute-start.7) | collective-permute-done | bytes 57376 | tf_op jit(solution)/shard_map/ppermute | solution.py:55
  64.4 1.9 %shard_map.109 = (f32[6,128,256]{2,1,0:T(8,128)}, f32[128,256]{1,0:T(8,128)}, f32[128,256]{1,0:T(8,128)}, f32[3,128,256]{2,1,0:T(8,128)S(1)}, f32[3,128,256]{2,1...) custom-call(f32[3,128,256]{2,1,0:T(8,128)S(1)} %bitcast.13, ...), custom_call_target="tpu_custom_call" | custom-call | flops 10000000 | bytes 4489216 | tf_op jit(solution)/shard_map/pallas_call | solution.py:33
  66.4 9.4 %all-to-all-start.2 = ((f32[64,1,128]{2,1,0:T(1,128)}), f32[64,1,128]{2,1,0:T(1,128)S(1)}, u32[]{:S(2)}, u32[]{:S(2)}) async-start(f32[64,1,128]{2,1,0:T(1,128)} %get-tuple-element.77), calls=%async_computation.2 | async-start | bytes 65536 | tf_op jit(solution)/shard_map/all_to_all | solution.py:60
  75.8 2.9 %collective-permute-start.9 = (f32[24,256]{1,0:T(8,128)S(1)}, f32[24,256]{1,0:T(8,128)S(1)}, u32[]{:S(2)}, u32[]{:S(2)}) collective-permute-start(f32[24,256]{1,0:T(8,128)S(1)} %get-tuple-element.73), channel_id=1, source_target_pairs={{0,8},{8,0},{16,24},{24,16},{32,40},{40,32},{48,56},{56,48},{64,72... | collective-permute-start | bytes 73736 | tf_op jit(solution)/shard_map/ppermute | solution.py:55
  79.4 1.0 collective-permute-done.9.near.sx_near
  80.3 4.6 %all-to-all-done.2.row = f32[64,1,128]{2,1,0:T(1,128)S(1)} async-done(((f32[64,1,128]{2,1,0:T(1,128)}), f32[64,1,128]{2,1,0:T(1,128)S(1)}, u32[]{:S(2)}, u32[]{:S(2)}) %all-to-all-start.2) | async-done | bytes 32800 | tf_op jit(solution)/shard_map/all_to_all | solution.py:60
  85.5 7.2 %all-to-all-start.3 = ((f32[8,16,128]{2,1,0:T(8,128)}), f32[8,16,128]{2,1,0:T(8,128)S(1)}, u32[]{:S(2)}, u32[]{:S(2)}) async-start(f32[8,16,128]{2,1,0:T(8,128)} %shard_map.111), calls=%async_computation.3 | async-start | bytes 131072 | tf_op jit(solution)/shard_map/all_to_all | solution.py:60
  92.8 4.4 %collective-permute-start.10 = (f32[48,256]{1,0:T(8,128)S(1)}, f32[48,256]{1,0:T(8,128)S(1)}, u32[]{:S(2)}, u32[]{:S(2)}) collective-permute-start(f32[48,256]{1,0:T(8,128)S(1)} %get-tuple-element.75), channel_id=1, source_target_pairs={{1,2},{2,1},{3,4},{4,3},{5,6},{6,5},{9,10},{10,9},{11,12},{12,11},... | collective-permute-start | bytes 147464 | tf_op jit(solution)/shard_map/ppermute | solution.py:54
  97.3 1.9 %collective-permute-start.11 = (f32[48,256]{1,0:T(8,128)S(1)}, f32[48,256]{1,0:T(8,128)S(1)}, u32[]{:S(2)}, u32[]{:S(2)}) collective-permute-start(f32[48,256]{1,0:T(8,128)S(1)} %get-tuple-element.76), channel_id=1, source_target_pairs={{0,1},{1,0},{2,3},{3,2},{4,5},{5,4},{6,7},{7,6},{8,9},{9,8},{10,11... | collective-permute-start | bytes 147464 | tf_op jit(solution)/shard_map/ppermute | solution.py:55
  99.2 0.8 collective-permute-done.10.sz_far
  100.4 0.9 shard_map.112
  (32 shorter events, 6.3 us)
Async XLA Ops:
  0.6 9.8 %copy-start.2 = (f32[16,8,256]{2,1,0:T(8,128)S(1)}, f32[16,8,256]{2,1,0:T(8,128)}, u32[]{:S(2)}) copy-start(f32[16,8,256]{2,1,0:T(8,128)} %param.9) | copy-start | bytes 393220
  0.6 11.7 %copy-start = (f32[3,16,8,256]{3,2,1,0:T(8,128)S(1)}, f32[3,16,8,256]{3,2,1,0:T(8,128)}, u32[]{:S(2)}) copy-start(f32[3,16,8,256]{3,2,1,0:T(8,128)} %param.6) | copy-start | bytes 1179652
  2.4 20.5 %copy-start.1 = (f32[6,16,8,256]{3,2,1,0:T(8,128)S(1)}, f32[6,16,8,256]{3,2,1,0:T(8,128)}, u32[]{:S(2)}) copy-start(f32[6,16,8,256]{3,2,1,0:T(8,128)} %param.8) | copy-start | bytes 2359300
  2.4 8.2 %collective-permute-start = (f32[72,256]{1,0:T(8,128)}, f32[72,256]{1,0:T(8,128)S(1)}, u32[]{:S(2)}, u32[]{:S(2)}) collective-permute-start(f32[72,256]{1,0:T(8,128)} %get-tuple-element.44), channel_id=1, source_target_pairs={{8,16},{16,8},{24,32},{32,24},{40,48},{48,40},{56,64},{64,56},{72,... | collective-permute-start | bytes 221192 | tf_op jit(solution)/shard_map/ppermute | solution.py:54
  3.2 9.2 %collective-permute-start.1 = (f32[72,256]{1,0:T(8,128)}, f32[72,256]{1,0:T(8,128)S(1)}, u32[]{:S(2)}, u32[]{:S(2)}) collective-permute-start(f32[72,256]{1,0:T(8,128)} %get-tuple-element.45), channel_id=1, source_target_pairs={{0,8},{8,0},{16,24},{24,16},{32,40},{40,32},{48,56},{56,48},{64,72... | collective-permute-start | bytes 221192 | tf_op jit(solution)/shard_map/ppermute | solution.py:55
  10.5 9.8 %copy-start.3 = (f32[16,8,256]{2,1,0:T(8,128)S(1)}, f32[16,8,256]{2,1,0:T(8,128)}, u32[]{:S(2)}) copy-start(f32[16,8,256]{2,1,0:T(8,128)} %param.10) | copy-start | bytes 393220
  12.5 10.3 %collective-permute-start.2 = (f32[144,256]{1,0:T(8,128)S(1)}, f32[144,256]{1,0:T(8,128)S(1)}, u32[]{:S(2)}, u32[]{:S(2)}) collective-permute-start(f32[144,256]{1,0:T(8,128)S(1)} %get-tuple-element.52), channel_id=1, source_target_pairs={{1,2},{2,1},{3,4},{4,3},{5,6},{6,5},{9,10},{10,9},{11,12},{12,11},... | collective-permute-start | bytes 442376 | tf_op jit(solution)/shard_map/ppermute | solution.py:54
  18.4 4.4 %collective-permute-start.3 = (f32[144,256]{1,0:T(8,128)S(1)}, f32[144,256]{1,0:T(8,128)S(1)}, u32[]{:S(2)}, u32[]{:S(2)}) collective-permute-start(f32[144,256]{1,0:T(8,128)S(1)} %get-tuple-element.53), channel_id=1, source_target_pairs={{0,1},{1,0},{2,3},{3,2},{4,5},{5,4},{6,7},{7,6},{8,9},{9,8},{10,11... | collective-permute-start | bytes 442376 | tf_op jit(solution)/shard_map/ppermute | solution.py:55
  20.4 0.9 copy-start.4
  21.3 1.6 %copy-start.5 = (f32[16,8,256]{2,1,0:T(8,128)S(1)}, f32[16,8,256]{2,1,0:T(8,128)}, u32[]{:S(2)}) copy-start(f32[16,8,256]{2,1,0:T(8,128)} %param.7) | copy-start | bytes 393220
  24.8 16.6 %all-to-all-start = ((f32[8,16,128]{2,1,0:T(8,128)}), f32[8,16,128]{2,1,0:T(8,128)S(1)}, u32[]{:S(2)}, u32[]{:S(2)}) async-start(f32[8,16,128]{2,1,0:T(8,128)} %get-tuple-element.66), calls=%async_computation | async-start | bytes 131072 | tf_op jit(solution)/shard_map/all_to_all | solution.py:60
  33.5 6.5 %collective-permute-start.5 = (f32[104,256]{1,0:T(8,128)S(1)}, f32[104,256]{1,0:T(8,128)S(1)}, u32[]{:S(2)}, u32[]{:S(2)}) collective-permute-start(f32[104,256]{1,0:T(8,128)S(1)} %get-tuple-element.58), channel_id=1, source_target_pairs={{0,1},{1,0},{2,3},{3,2},{4,5},{5,4},{6,7},{7,6},{8,9},{9,8},{10,11... | collective-permute-start | bytes 319496 | tf_op jit(solution)/shard_map/ppermute | solution.py:55
  35.4 19.9 %collective-permute-start.4 = (f32[104,256]{1,0:T(8,128)S(1)}, f32[104,256]{1,0:T(8,128)S(1)}, u32[]{:S(2)}, u32[]{:S(2)}) collective-permute-start(f32[104,256]{1,0:T(8,128)S(1)} %get-tuple-element.57), channel_id=1, source_target_pairs={{1,2},{2,1},{3,4},{4,3},{5,6},{6,5},{9,10},{10,9},{11,12},{12,11},... | collective-permute-start | bytes 319496 | tf_op jit(solution)/shard_map/ppermute | solution.py:54
  42.0 22.4 %all-to-all-start.1 = ((f32[64,1,128]{2,1,0:T(1,128)}), f32[64,1,128]{2,1,0:T(1,128)S(1)}, u32[]{:S(2)}, u32[]{:S(2)}) async-start(f32[64,1,128]{2,1,0:T(1,128)} %shard_map.108), calls=%async_computation.1 | async-start | bytes 65536 | tf_op jit(solution)/shard_map/all_to_all | solution.py:60
  55.4 6.0 %collective-permute-start.6 = (f32[56,256]{1,0:T(8,128)S(1)}, f32[56,256]{1,0:T(8,128)S(1)}, u32[]{:S(2)}, u32[]{:S(2)}) collective-permute-start(f32[56,256]{1,0:T(8,128)S(1)} %get-tuple-element.59), channel_id=1, source_target_pairs={{8,16},{16,8},{24,32},{32,24},{40,48},{48,40},{56,64},{64,56},{72,... | collective-permute-start | bytes 172040 | tf_op jit(solution)/shard_map/ppermute | solution.py:54
  56.0 7.7 %collective-permute-start.7 = (f32[56,256]{1,0:T(8,128)S(1)}, f32[56,256]{1,0:T(8,128)S(1)}, u32[]{:S(2)}, u32[]{:S(2)}) collective-permute-start(f32[56,256]{1,0:T(8,128)S(1)} %get-tuple-element.60), channel_id=1, source_target_pairs={{0,8},{8,0},{16,24},{24,16},{32,40},{40,32},{48,56},{56,48},{64,72... | collective-permute-start | bytes 172040 | tf_op jit(solution)/shard_map/ppermute | solution.py:55
  66.4 18.5 %all-to-all-start.2 = ((f32[64,1,128]{2,1,0:T(1,128)}), f32[64,1,128]{2,1,0:T(1,128)S(1)}, u32[]{:S(2)}, u32[]{:S(2)}) async-start(f32[64,1,128]{2,1,0:T(1,128)} %get-tuple-element.77), calls=%async_computation.2 | async-start | bytes 65536 | tf_op jit(solution)/shard_map/all_to_all | solution.py:60
  75.8 4.6 %collective-permute-start.9 = (f32[24,256]{1,0:T(8,128)S(1)}, f32[24,256]{1,0:T(8,128)S(1)}, u32[]{:S(2)}, u32[]{:S(2)}) collective-permute-start(f32[24,256]{1,0:T(8,128)S(1)} %get-tuple-element.73), channel_id=1, source_target_pairs={{0,8},{8,0},{16,24},{24,16},{32,40},{40,32},{48,56},{56,48},{64,72... | collective-permute-start | bytes 73736 | tf_op jit(solution)/shard_map/ppermute | solution.py:55
  78.7 14.1 %collective-permute-start.8 = (f32[72,256]{1,0:T(8,128)S(1)}, f32[72,256]{1,0:T(8,128)S(1)}, u32[]{:S(2)}, u32[]{:S(2)}) collective-permute-start(f32[72,256]{1,0:T(8,128)S(1)} %get-tuple-element.72), channel_id=1, source_target_pairs={{8,16},{16,8},{24,32},{32,24},{40,48},{48,40},{56,64},{64,56},{72,... | collective-permute-start | bytes 221192 | tf_op jit(solution)/shard_map/ppermute | solution.py:54
  85.5 14.8 %all-to-all-start.3 = ((f32[8,16,128]{2,1,0:T(8,128)}), f32[8,16,128]{2,1,0:T(8,128)S(1)}, u32[]{:S(2)}, u32[]{:S(2)}) async-start(f32[8,16,128]{2,1,0:T(8,128)} %shard_map.111), calls=%async_computation.3 | async-start | bytes 131072 | tf_op jit(solution)/shard_map/all_to_all | solution.py:60
  92.8 7.2 %collective-permute-start.10 = (f32[48,256]{1,0:T(8,128)S(1)}, f32[48,256]{1,0:T(8,128)S(1)}, u32[]{:S(2)}, u32[]{:S(2)}) collective-permute-start(f32[48,256]{1,0:T(8,128)S(1)} %get-tuple-element.75), channel_id=1, source_target_pairs={{1,2},{2,1},{3,4},{4,3},{5,6},{6,5},{9,10},{10,9},{11,12},{12,11},... | collective-permute-start | bytes 147464 | tf_op jit(solution)/shard_map/ppermute | solution.py:54
  97.3 3.1 %collective-permute-start.11 = (f32[48,256]{1,0:T(8,128)S(1)}, f32[48,256]{1,0:T(8,128)S(1)}, u32[]{:S(2)}, u32[]{:S(2)}) collective-permute-start(f32[48,256]{1,0:T(8,128)S(1)} %get-tuple-element.76), channel_id=1, source_target_pairs={{0,1},{1,0},{2,3},{3,2},{4,5},{5,4},{6,7},{7,6},{8,9},{9,8},{10,11... | collective-permute-start | bytes 147464 | tf_op jit(solution)/shard_map/ppermute | solution.py:55

commit v9 on v6

--- a/solution.py
+++ b/solution.py
@@ -155,28 +155,17 @@
 
 def faces_kernel(v, plastic, x_far, x_near, sem):
     even = even_x()
+    copies = []
     for i, (out, low) in enumerate(((x_far, even), (x_near, jnp.logical_not(even)))):
-        top = pl.multiple_of(jnp.where(low, 0, ROWS - LZ), LZ)
-        deep = pl.multiple_of(jnp.where(low, 0, ROWS - 6 * LZ), LZ)
-        copies = [
-            pltpu.make_async_copy(
-                v.at[f, pl.ds(top, LZ)], out.at[pl.ds(f * LZ, LZ)], sem.at[4 * i + f]
-            )
-            for f in range(3)
-        ]
+        top, deep = jnp.where(low, 0, LX - 1), jnp.where(low, 0, LX - 6)
+        copies.append(pltpu.make_async_copy(v.at[:, top], out.at[pl.ds(0, 3)], sem.at[2 * i]))
         copies.append(
-            pltpu.make_async_copy(
-                plastic.at[pl.ds(deep, 6 * LZ)], out.at[pl.ds(3 * LZ, 6 * LZ)], sem.at[4 * i + 3]
-            )
+            pltpu.make_async_copy(plastic.at[pl.ds(deep, 6)], out.at[pl.ds(3, 6)], sem.at[2 * i + 1])
         )
-        for copy in copies:
-            copy.start()
-    for i, out in enumerate((x_far, x_near)):
-        for f in range(3):
-            rows = pl.ds(f * LZ, LZ)
-            pltpu.make_async_copy(v.at[f, pl.ds(0, LZ)], out.at[rows], sem.at[4 * i + f]).wait()
-        rows = pl.ds(3 * LZ, 6 * LZ)
-        pltpu.make_async_copy(plastic.at[pl.ds(0, 6 * LZ)], out.at[rows], sem.at[4 * i + 3]).wait()
+    for copy in copies:
+        copy.start()
+    for copy in copies:
+        copy.wait()
 
 
 def store_row(out, top_yield, top_eta, earlier=None):
@@ -497,8 +486,9 @@
     x_3, z_3, x_9, z_9 = (3 * LZ, NY), (3 * LX, NY), (9 * LZ, NY), (9 * LX, NY)
 
     dma = pltpu.SemaphoreType.DMA
-    x_msgs = call(faces_kernel, [x_9, x_9], [v, plastic], 0, [dma((8,))], None, [HBM, HBM], 60)
-    x_msgs = exchange(GX, *x_msgs)
+    blocks = [v.reshape((3, LX, LZ, NY)), plastic.reshape((LX, LZ, NY))]
+    x_msgs = call(faces_kernel, [(9, LZ, NY)] * 2, blocks, 0, [dma((4,))], None, [HBM, HBM], 60)
+    x_msgs = [m.reshape(x_9) for m in exchange(GX, *x_msgs)]
     (along,) = call(own_x_kernel, [one], [plastic], 10**6)
     along, *z_msgs = call(smooth_x_kernel, [one, z_9, z_9], [v, along, *x_msgs], 10**6, [slots])
     z_msgs = exchange(GZ, *z_msgs)

time: 99.8 us -> 99.7 us (level)
  no operation moved by 1% of the time
where the time goes in v9:
time: 99.7 us; the launch traced here: 99 us
  starting transfers between devices  75.6 us (76%)
  waiting for transfers between devices  12.7 us (13%)
  Pallas kernels  8.87 us (9%)
    all_to_all x4, starting transfers between devices, spread(): return lax.all_to_all(row, axes, 0, 0, tiled=True)  36.9 us
    ppermute x6, starting transfers between devices, exchange(): lax.ppermute(near, axis, pairs(count, 0))  21.7 us
    ppermute x6, starting transfers between devices, exchange(): lax.ppermute(far, axis, pairs(count, 1))  17 us
    pallas_call x12, Pallas kernels, call(): pl.pallas_call(kernel, out_shape=[jax.ShapeDtypeStruct(s, F32) for s in o...  8.87 us
    all_to_all x4, waiting for transfers between devices, spread(): return lax.all_to_all(row, axes, 0, 0, tiled=True)  6.22 us
    ppermute x6, waiting for transfers between devices, exchange(): lax.ppermute(near, axis, pairs(count, 0))  5.46 us
  transfers between devices with their start and end apart: 16, of which 10 were waited for; matrix products, arithmetic and copies ran while one was open for 0% of the time, Pallas kernels for 2%

profile of v9, /device:TPU:1, one launch (start us, length us, event | category | flops | bytes accessed | tf_op | source)
XLA Modules:
  0.0 99.0 jit_solution(14677055473052975287)
XLA Ops:
  0.7 1.6 %shard_map.102 = (f32[9,8,256]{2,1,0:T(8,128)}, f32[9,8,256]{2,1,0:T(8,128)}) custom-call(f32[3,16,8,256]{3,2,1,0:T(8,128)} %v.1, f32[16,8,256]{2,1,0:T(8,128)} %plastic.1), custom_call_target="tpu_custom_call" | custom-call | bytes 671744 | tf_op jit(solution)/shard_map/pallas_call | solution.py:35
  3.1 7.3 %collective-permute-start.1 = (f32[9,8,256]{2,1,0:T(8,128)}, f32[9,8,256]{2,1,0:T(8,128)S(1)}, u32[]{:S(2)}, u32[]{:S(2)}) collective-permute-start(f32[9,8,256]{2,1,0:T(8,128)} %get-tuple-element.45), channel_id=1, source_target_pairs={{0,8},{8,0},{16,24},{24,16},{32,40},{40,32},{48,56},{56,48},{64,72... | collective-permute-start | bytes 221192 | tf_op jit(solution)/shard_map/ppermute | solution.py:57
  10.5 1.8 %collective-permute-done.1 = f32[9,8,256]{2,1,0:T(8,128)S(1)} collective-permute-done((f32[9,8,256]{2,1,0:T(8,128)}, f32[9,8,256]{2,1,0:T(8,128)S(1)}, u32[]{:S(2)}, u32[]{:S(2)}) %collective-permute-start.1) | collective-permute-done | bytes 73760 | tf_op jit(solution)/shard_map/ppermute | solution.py:57
  12.4 5.9 %collective-permute-start.2 = (f32[144,256]{1,0:T(8,128)S(1)}, f32[144,256]{1,0:T(8,128)S(1)}, u32[]{:S(2)}, u32[]{:S(2)}) collective-permute-start(f32[144,256]{1,0:T(8,128)S(1)} %get-tuple-element.52), channel_id=1, source_target_pairs={{1,2},{2,1},{3,4},{4,3},{5,6},{6,5},{9,10},{10,9},{11,12},{12,11},... | collective-permute-start | bytes 442376 | tf_op jit(solution)/shard_map/ppermute | solution.py:56
  18.3 1.9 %collective-permute-start.3 = (f32[144,256]{1,0:T(8,128)S(1)}, f32[144,256]{1,0:T(8,128)S(1)}, u32[]{:S(2)}, u32[]{:S(2)}) collective-permute-start(f32[144,256]{1,0:T(8,128)S(1)} %get-tuple-element.53), channel_id=1, source_target_pairs={{0,1},{1,0},{2,3},{3,2},{4,5},{5,4},{6,7},{7,6},{8,9},{9,8},{10,11... | collective-permute-start | bytes 442376 | tf_op jit(solution)/shard_map/ppermute | solution.py:57
  20.3 0.9 copy-done.4
  22.7 1.9 %shard_map.105 = (f32[3,128,256]{2,1,0:T(8,128)S(1)}, f32[128,256]{1,0:T(8,128)S(1)}, f32[128,256]{1,0:T(8,128)S(1)}, f32[128,256]{1,0:T(8,128)S(1)}, f32[2,24,2...) custom-call(f32[3,128,256]{2,1,0:T(8,128)S(1)} %bitcast.13, ...), custom_call_target="tpu_custom_call" | custom-call | flops 10000000 | bytes 4030464 | tf_op jit(solution)/shard_map/pallas_call | solution.py:35
  24.7 9.0 %all-to-all-start = ((f32[16,8,128]{2,1,0:T(8,128)}), f32[16,8,128]{2,1,0:T(8,128)S(1)}, u32[]{:S(2)}, u32[]{:S(2)}) async-start(f32[16,8,128]{2,1,0:T(8,128)} %get-tuple-element.66), calls=%async_computation | async-start | bytes 131072 | tf_op jit(solution)/shard_map/all_to_all | solution.py:62
  33.7 2.0 %collective-permute-start.5 = (f32[104,256]{1,0:T(8,128)S(1)}, f32[104,256]{1,0:T(8,128)S(1)}, u32[]{:S(2)}, u32[]{:S(2)}) collective-permute-start(f32[104,256]{1,0:T(8,128)S(1)} %get-tuple-element.58), channel_id=1, source_target_pairs={{0,1},{1,0},{2,3},{3,2},{4,5},{5,4},{6,7},{7,6},{8,9},{9,8},{10,11... | collective-permute-start | bytes 319496 | tf_op jit(solution)/shard_map/ppermute | solution.py:57
  35.7 4.5 %collective-permute-start.4 = (f32[104,256]{1,0:T(8,128)S(1)}, f32[104,256]{1,0:T(8,128)S(1)}, u32[]{:S(2)}, u32[]{:S(2)}) collective-permute-start(f32[104,256]{1,0:T(8,128)S(1)} %get-tuple-element.57), channel_id=1, source_target_pairs={{1,2},{2,1},{3,4},{4,3},{5,6},{6,5},{9,10},{10,9},{11,12},{12,11},... | collective-permute-start | bytes 319496 | tf_op jit(solution)/shard_map/ppermute | solution.py:56
  40.2 1.3 %all-to-all-done.row = f32[16,8,128]{2,1,0:T(8,128)S(1)} async-done(((f32[16,8,128]{2,1,0:T(8,128)}), f32[16,8,128]{2,1,0:T(8,128)S(1)}, u32[]{:S(2)}, u32[]{:S(2)}) %all-to-all-start) | async-done | bytes 65568 | tf_op jit(solution)/shard_map/all_to_all | solution.py:62
  42.1 12.0 %all-to-all-start.1 = ((f32[32,2,128]{2,1,0:T(2,128)}), f32[32,2,128]{2,1,0:T(2,128)S(1)}, u32[]{:S(2)}, u32[]{:S(2)}) async-start(f32[32,2,128]{2,1,0:T(2,128)} %shard_map.108), calls=%async_computation.1 | async-start | bytes 65536 | tf_op jit(solution)/shard_map/all_to_all | solution.py:62
  54.8 5.6 %collective-permute-start.7 = (f32[56,256]{1,0:T(8,128)S(1)}, f32[56,256]{1,0:T(8,128)S(1)}, u32[]{:S(2)}, u32[]{:S(2)}) collective-permute-start(f32[56,256]{1,0:T(8,128)S(1)} %get-tuple-element.60), channel_id=1, source_target_pairs={{0,8},{8,0},{16,24},{24,16},{32,40},{40,32},{48,56},{56,48},{64,72... | collective-permute-start | bytes 172040 | tf_op jit(solution)/shard_map/ppermute | solution.py:57
  60.4 1.8 %collective-permute-done.7.sx_near = f32[56,256]{1,0:T(8,128)S(1)} collective-permute-done((f32[56,256]{1,0:T(8,128)S(1)}, f32[56,256]{1,0:T(8,128)S(1)}, u32[]{:S(2)}, u32[]{:S(2)}) %collective-permute-start.7) | collective-permute-done | bytes 57376 | tf_op jit(solution)/shard_map/ppermute | solution.py:57
  62.9 2.0 %shard_map.109 = (f32[6,128,256]{2,1,0:T(8,128)}, f32[128,256]{1,0:T(8,128)}, f32[128,256]{1,0:T(8,128)}, f32[3,128,256]{2,1,0:T(8,128)S(1)}, f32[3,128,256]{2,1...) custom-call(f32[3,128,256]{2,1,0:T(8,128)S(1)} %bitcast.14, ...), custom_call_target="tpu_custom_call" | custom-call | flops 10000000 | bytes 4489216 | tf_op jit(solution)/shard_map/pallas_call | solution.py:35
  64.9 7.8 %all-to-all-start.2 = ((f32[32,2,128]{2,1,0:T(2,128)}), f32[32,2,128]{2,1,0:T(2,128)S(1)}, u32[]{:S(2)}, u32[]{:S(2)}) async-start(f32[32,2,128]{2,1,0:T(2,128)} %get-tuple-element.77), calls=%async_computation.2 | async-start | bytes 65536 | tf_op jit(solution)/shard_map/all_to_all | solution.py:62
  72.6 3.1 %collective-permute-start.9 = (f32[24,256]{1,0:T(8,128)S(1)}, f32[24,256]{1,0:T(8,128)S(1)}, u32[]{:S(2)}, u32[]{:S(2)}) collective-permute-start(f32[24,256]{1,0:T(8,128)S(1)} %get-tuple-element.73), channel_id=1, source_target_pairs={{0,8},{8,0},{16,24},{24,16},{32,40},{40,32},{48,56},{56,48},{64,72... | collective-permute-start | bytes 73736 | tf_op jit(solution)/shard_map/ppermute | solution.py:57
  76.4 0.8 collective-permute-done.9.near.sx_near
  77.2 4.2 %all-to-all-done.2.row = f32[32,2,128]{2,1,0:T(2,128)S(1)} async-done(((f32[32,2,128]{2,1,0:T(2,128)}), f32[32,2,128]{2,1,0:T(2,128)S(1)}, u32[]{:S(2)}, u32[]{:S(2)}) %all-to-all-start.2) | async-done | bytes 32800 | tf_op jit(solution)/shard_map/all_to_all | solution.py:62
  82.1 8.2 %all-to-all-start.3 = ((f32[16,8,128]{2,1,0:T(8,128)}), f32[16,8,128]{2,1,0:T(8,128)S(1)}, u32[]{:S(2)}, u32[]{:S(2)}) async-start(f32[16,8,128]{2,1,0:T(8,128)} %shard_map.111), calls=%async_computation.3 | async-start | bytes 131072 | tf_op jit(solution)/shard_map/all_to_all | solution.py:62
  90.3 4.4 %collective-permute-start.10 = (f32[48,256]{1,0:T(8,128)S(1)}, f32[48,256]{1,0:T(8,128)S(1)}, u32[]{:S(2)}, u32[]{:S(2)}) collective-permute-start(f32[48,256]{1,0:T(8,128)S(1)} %get-tuple-element.75), channel_id=1, source_target_pairs={{1,2},{2,1},{3,4},{4,3},{5,6},{6,5},{9,10},{10,9},{11,12},{12,11},... | collective-permute-start | bytes 147464 | tf_op jit(solution)/shard_map/ppermute | solution.py:56
  94.8 1.9 %collective-permute-start.11 = (f32[48,256]{1,0:T(8,128)S(1)}, f32[48,256]{1,0:T(8,128)S(1)}, u32[]{:S(2)}, u32[]{:S(2)}) collective-permute-start(f32[48,256]{1,0:T(8,128)S(1)} %get-tuple-element.76), channel_id=1, source_target_pairs={{0,1},{1,0},{2,3},{3,2},{4,5},{5,4},{6,7},{7,6},{8,9},{9,8},{10,11... | collective-permute-start | bytes 147464 | tf_op jit(solution)/shard_map/ppermute | solution.py:57
  96.9 1.0 collective-permute-done.11.sz_near
  98.1 0.9 shard_map.112
  (32 shorter events, 6.3 us)
Async XLA Ops:
  0.6 9.7 %copy-start.2 = (f32[16,8,256]{2,1,0:T(8,128)S(1)}, f32[16,8,256]{2,1,0:T(8,128)}, u32[]{:S(2)}) copy-start(f32[16,8,256]{2,1,0:T(8,128)} %plastic.1) | copy-start | bytes 393220
  0.6 11.7 %copy-start = (f32[3,16,8,256]{3,2,1,0:T(8,128)S(1)}, f32[3,16,8,256]{3,2,1,0:T(8,128)}, u32[]{:S(2)}) copy-start(f32[3,16,8,256]{3,2,1,0:T(8,128)} %v.1) | copy-start | bytes 1179652
  2.3 20.5 %copy-start.1 = (f32[6,16,8,256]{3,2,1,0:T(8,128)S(1)}, f32[6,16,8,256]{3,2,1,0:T(8,128)}, u32[]{:S(2)}) copy-start(f32[6,16,8,256]{3,2,1,0:T(8,128)} %param.8) | copy-start | bytes 2359300
  2.3 8.2 %collective-permute-start = (f32[9,8,256]{2,1,0:T(8,128)}, f32[9,8,256]{2,1,0:T(8,128)S(1)}, u32[]{:S(2)}, u32[]{:S(2)}) collective-permute-start(f32[9,8,256]{2,1,0:T(8,128)} %get-tuple-element.44), channel_id=1, source_target_pairs={{8,16},{16,8},{24,32},{32,24},{40,48},{48,40},{56,64},{64,56},{72,... | collective-permute-start | bytes 221192 | tf_op jit(solution)/shard_map/ppermute | solution.py:56
  3.1 9.2 %collective-permute-start.1 = (f32[9,8,256]{2,1,0:T(8,128)}, f32[9,8,256]{2,1,0:T(8,128)S(1)}, u32[]{:S(2)}, u32[]{:S(2)}) collective-permute-start(f32[9,8,256]{2,1,0:T(8,128)} %get-tuple-element.45), channel_id=1, source_target_pairs={{0,8},{8,0},{16,24},{24,16},{32,40},{40,32},{48,56},{56,48},{64,72... | collective-permute-start | bytes 221192 | tf_op jit(solution)/shard_map/ppermute | solution.py:57
  12.3 8.0 %copy-start.3 = (f32[16,8,256]{2,1,0:T(8,128)S(1)}, f32[16,8,256]{2,1,0:T(8,128)}, u32[]{:S(2)}) copy-start(f32[16,8,256]{2,1,0:T(8,128)} %param.10) | copy-start | bytes 393220
  12.4 10.3 %collective-permute-start.2 = (f32[144,256]{1,0:T(8,128)S(1)}, f32[144,256]{1,0:T(8,128)S(1)}, u32[]{:S(2)}, u32[]{:S(2)}) collective-permute-start(f32[144,256]{1,0:T(8,128)S(1)} %get-tuple-element.52), channel_id=1, source_target_pairs={{1,2},{2,1},{3,4},{4,3},{5,6},{6,5},{9,10},{10,9},{11,12},{12,11},... | collective-permute-start | bytes 442376 | tf_op jit(solution)/shard_map/ppermute | solution.py:56
  18.3 4.4 %collective-permute-start.3 = (f32[144,256]{1,0:T(8,128)S(1)}, f32[144,256]{1,0:T(8,128)S(1)}, u32[]{:S(2)}, u32[]{:S(2)}) collective-permute-start(f32[144,256]{1,0:T(8,128)S(1)} %get-tuple-element.53), channel_id=1, source_target_pairs={{0,1},{1,0},{2,3},{3,2},{4,5},{5,4},{6,7},{7,6},{8,9},{9,8},{10,11... | collective-permute-start | bytes 442376 | tf_op jit(solution)/shard_map/ppermute | solution.py:57
  20.3 0.9 copy-start.4
  21.2 1.6 %copy-start.5 = (f32[16,8,256]{2,1,0:T(8,128)S(1)}, f32[16,8,256]{2,1,0:T(8,128)}, u32[]{:S(2)}) copy-start(f32[16,8,256]{2,1,0:T(8,128)} %param.7) | copy-start | bytes 393220
  24.7 16.8 %all-to-all-start = ((f32[16,8,128]{2,1,0:T(8,128)}), f32[16,8,128]{2,1,0:T(8,128)S(1)}, u32[]{:S(2)}, u32[]{:S(2)}) async-start(f32[16,8,128]{2,1,0:T(8,128)} %get-tuple-element.66), calls=%async_computation | async-start | bytes 131072 | tf_op jit(solution)/shard_map/all_to_all | solution.py:62
  33.7 6.5 %collective-permute-start.5 = (f32[104,256]{1,0:T(8,128)S(1)}, f32[104,256]{1,0:T(8,128)S(1)}, u32[]{:S(2)}, u32[]{:S(2)}) collective-permute-start(f32[104,256]{1,0:T(8,128)S(1)} %get-tuple-element.58), channel_id=1, source_target_pairs={{0,1},{1,0},{2,3},{3,2},{4,5},{5,4},{6,7},{7,6},{8,9},{9,8},{10,11... | collective-permute-start | bytes 319496 | tf_op jit(solution)/shard_map/ppermute | solution.py:57
  35.7 18.4 %collective-permute-start.4 = (f32[104,256]{1,0:T(8,128)S(1)}, f32[104,256]{1,0:T(8,128)S(1)}, u32[]{:S(2)}, u32[]{:S(2)}) collective-permute-start(f32[104,256]{1,0:T(8,128)S(1)} %get-tuple-element.57), channel_id=1, source_target_pairs={{1,2},{2,1},{3,4},{4,3},{5,6},{6,5},{9,10},{10,9},{11,12},{12,11},... | collective-permute-start | bytes 319496 | tf_op jit(solution)/shard_map/ppermute | solution.py:56
  42.1 20.8 %all-to-all-start.1 = ((f32[32,2,128]{2,1,0:T(2,128)}), f32[32,2,128]{2,1,0:T(2,128)S(1)}, u32[]{:S(2)}, u32[]{:S(2)}) async-start(f32[32,2,128]{2,1,0:T(2,128)} %shard_map.108), calls=%async_computation.1 | async-start | bytes 65536 | tf_op jit(solution)/shard_map/all_to_all | solution.py:62
  54.1 6.2 %collective-permute-start.6 = (f32[56,256]{1,0:T(8,128)S(1)}, f32[56,256]{1,0:T(8,128)S(1)}, u32[]{:S(2)}, u32[]{:S(2)}) collective-permute-start(f32[56,256]{1,0:T(8,128)S(1)} %get-tuple-element.59), channel_id=1, source_target_pairs={{8,16},{16,8},{24,32},{32,24},{40,48},{48,40},{56,64},{64,56},{72,... | collective-permute-start | bytes 172040 | tf_op jit(solution)/shard_map/ppermute | solution.py:56
  54.8 7.4 %collective-permute-start.7 = (f32[56,256]{1,0:T(8,128)S(1)}, f32[56,256]{1,0:T(8,128)S(1)}, u32[]{:S(2)}, u32[]{:S(2)}) collective-permute-start(f32[56,256]{1,0:T(8,128)S(1)} %get-tuple-element.60), channel_id=1, source_target_pairs={{0,8},{8,0},{16,24},{24,16},{32,40},{40,32},{48,56},{56,48},{64,72... | collective-permute-start | bytes 172040 | tf_op jit(solution)/shard_map/ppermute | solution.py:57
  64.9 16.6 %all-to-all-start.2 = ((f32[32,2,128]{2,1,0:T(2,128)}), f32[32,2,128]{2,1,0:T(2,128)S(1)}, u32[]{:S(2)}, u32[]{:S(2)}) async-start(f32[32,2,128]{2,1,0:T(2,128)} %get-tuple-element.77), calls=%async_computation.2 | async-start | bytes 65536 | tf_op jit(solution)/shard_map/all_to_all | solution.py:62
  72.6 4.6 %collective-permute-start.9 = (f32[24,256]{1,0:T(8,128)S(1)}, f32[24,256]{1,0:T(8,128)S(1)}, u32[]{:S(2)}, u32[]{:S(2)}) collective-permute-start(f32[24,256]{1,0:T(8,128)S(1)} %get-tuple-element.73), channel_id=1, source_target_pairs={{0,8},{8,0},{16,24},{24,16},{32,40},{40,32},{48,56},{56,48},{64,72... | collective-permute-start | bytes 73736 | tf_op jit(solution)/shard_map/ppermute | solution.py:57
  75.7 14.6 %collective-permute-start.8 = (f32[72,256]{1,0:T(8,128)S(1)}, f32[72,256]{1,0:T(8,128)S(1)}, u32[]{:S(2)}, u32[]{:S(2)}) collective-permute-start(f32[72,256]{1,0:T(8,128)S(1)} %get-tuple-element.72), channel_id=1, source_target_pairs={{8,16},{16,8},{24,32},{32,24},{40,48},{48,40},{56,64},{64,56},{72,... | collective-permute-start | bytes 221192 | tf_op jit(solution)/shard_map/ppermute | solution.py:56
  82.1 16.0 %all-to-all-start.3 = ((f32[16,8,128]{2,1,0:T(8,128)}), f32[16,8,128]{2,1,0:T(8,128)S(1)}, u32[]{:S(2)}, u32[]{:S(2)}) async-start(f32[16,8,128]{2,1,0:T(8,128)} %shard_map.111), calls=%async_computation.3 | async-start | bytes 131072 | tf_op jit(solution)/shard_map/all_to_all | solution.py:62
  90.3 6.6 %collective-permute-start.10 = (f32[48,256]{1,0:T(8,128)S(1)}, f32[48,256]{1,0:T(8,128)S(1)}, u32[]{:S(2)}, u32[]{:S(2)}) collective-permute-start(f32[48,256]{1,0:T(8,128)S(1)} %get-tuple-element.75), channel_id=1, source_target_pairs={{1,2},{2,1},{3,4},{4,3},{5,6},{6,5},{9,10},{10,9},{11,12},{12,11},... | collective-permute-start | bytes 147464 | tf_op jit(solution)/shard_map/ppermute | solution.py:56
  94.8 3.1 %collective-permute-start.11 = (f32[48,256]{1,0:T(8,128)S(1)}, f32[48,256]{1,0:T(8,128)S(1)}, u32[]{:S(2)}, u32[]{:S(2)}) collective-permute-start(f32[48,256]{1,0:T(8,128)S(1)} %get-tuple-element.76), channel_id=1, source_target_pairs={{0,1},{1,0},{2,3},{3,2},{4,5},{5,4},{6,7},{7,6},{8,9},{9,8},{10,11... | collective-permute-start | bytes 147464 | tf_op jit(solution)/shard_map/ppermute | solution.py:57

commit v10 on v9

--- a/solution.py
+++ b/solution.py
@@ -19,7 +19,7 @@
 F32 = jnp.float32
 LX, LZ, NY = 16, 8, 256
 ROWS = LX * LZ
-CHUNK = 16
+CHUNK = 32
 XX, ZZ, YY, XZ_, XY, ZY = range(6)
 ALONG_X = (XX, XZ_, XY)
 ALONG_Z = (XZ_, ZZ, ZY)
@@ -243,7 +243,7 @@
             if start == 0:
                 value = jnp.concatenate([value[:LZ] - x_low[slab] * 0.5, value[LZ:]], axis=0)
             if start == ROWS - CHUNK:
-                value = jnp.concatenate([value[:LZ], value[LZ:] + x_high[slab] * 0.5], axis=0)
+                value = jnp.concatenate([value[: CHUNK - LZ], value[CHUNK - LZ :] + x_high[slab] * 0.5], axis=0)
             yield f, here, value
 
 

time: 99.7 us -> 99.8 us (level)
  no operation moved by 1% of the time
where the time goes in v10:
time: 99.8 us; the launch traced here: 99.1 us
  starting transfers between devices  75.6 us (76%)
  waiting for transfers between devices  12.7 us (13%)
  Pallas kernels  8.95 us (9%)
    all_to_all x4, starting transfers between devices, spread(): return lax.all_to_all(row, axes, 0, 0, tiled=True)  36.9 us
    ppermute x6, starting transfers between devices, exchange(): lax.ppermute(near, axis, pairs(count, 0))  21.7 us
    ppermute x6, starting transfers between devices, exchange(): lax.ppermute(far, axis, pairs(count, 1))  17 us
    pallas_call x12, Pallas kernels, call(): pl.pallas_call(kernel, out_shape=[jax.ShapeDtypeStruct(s, F32) for s in o...  8.95 us
    all_to_all x4, waiting for transfers between devices, spread(): return lax.all_to_all(row, axes, 0, 0, tiled=True)  6.22 us
    ppermute x6, waiting for transfers between devices, exchange(): lax.ppermute(near, axis, pairs(count, 0))  5.46 us
  transfers between devices with their start and end apart: 16, of which 10 were waited for; matrix products, arithmetic and copies ran while one was open for 0% of the time, Pallas kernels for 2%

profile of v10, /device:TPU:1, one launch (start us, length us, event | category | flops | bytes accessed | tf_op | source)
XLA Modules:
  0.0 99.1 jit_solution(12042605297009792734)
XLA Ops:
  0.7 1.6 %shard_map.102 = (f32[9,8,256]{2,1,0:T(8,128)}, f32[9,8,256]{2,1,0:T(8,128)}) custom-call(f32[3,16,8,256]{3,2,1,0:T(8,128)} %v.1, f32[16,8,256]{2,1,0:T(8,128)} %plastic.1), custom_call_target="tpu_custom_call" | custom-call | bytes 671744 | tf_op jit(solution)/shard_map/pallas_call | solution.py:35
  3.1 7.3 %collective-permute-start.1 = (f32[9,8,256]{2,1,0:T(8,128)}, f32[9,8,256]{2,1,0:T(8,128)S(1)}, u32[]{:S(2)}, u32[]{:S(2)}) collective-permute-start(f32[9,8,256]{2,1,0:T(8,128)} %get-tuple-element.45), channel_id=1, source_target_pairs={{0,8},{8,0},{16,24},{24,16},{32,40},{40,32},{48,56},{56,48},{64,72... | collective-permute-start | bytes 221192 | tf_op jit(solution)/shard_map/ppermute | solution.py:57
  10.5 1.8 %collective-permute-done.1 = f32[9,8,256]{2,1,0:T(8,128)S(1)} collective-permute-done((f32[9,8,256]{2,1,0:T(8,128)}, f32[9,8,256]{2,1,0:T(8,128)S(1)}, u32[]{:S(2)}, u32[]{:S(2)}) %collective-permute-start.1) | collective-permute-done | bytes 73760 | tf_op jit(solution)/shard_map/ppermute | solution.py:57
  12.4 5.9 %collective-permute-start.2 = (f32[144,256]{1,0:T(8,128)S(1)}, f32[144,256]{1,0:T(8,128)S(1)}, u32[]{:S(2)}, u32[]{:S(2)}) collective-permute-start(f32[144,256]{1,0:T(8,128)S(1)} %get-tuple-element.52), channel_id=1, source_target_pairs={{1,2},{2,1},{3,4},{4,3},{5,6},{6,5},{9,10},{10,9},{11,12},{12,11},... | collective-permute-start | bytes 442376 | tf_op jit(solution)/shard_map/ppermute | solution.py:56
  18.3 1.9 %collective-permute-start.3 = (f32[144,256]{1,0:T(8,128)S(1)}, f32[144,256]{1,0:T(8,128)S(1)}, u32[]{:S(2)}, u32[]{:S(2)}) collective-permute-start(f32[144,256]{1,0:T(8,128)S(1)} %get-tuple-element.53), channel_id=1, source_target_pairs={{0,1},{1,0},{2,3},{3,2},{4,5},{5,4},{6,7},{7,6},{8,9},{9,8},{10,11... | collective-permute-start | bytes 442376 | tf_op jit(solution)/shard_map/ppermute | solution.py:57
  20.3 0.9 copy-done.4
  22.7 2.0 %shard_map.105 = (f32[3,128,256]{2,1,0:T(8,128)S(1)}, f32[128,256]{1,0:T(8,128)S(1)}, f32[128,256]{1,0:T(8,128)S(1)}, f32[128,256]{1,0:T(8,128)S(1)}, f32[2,24,2...) custom-call(f32[3,128,256]{2,1,0:T(8,128)S(1)} %bitcast.13, ...), custom_call_target="tpu_custom_call" | custom-call | flops 10000000 | bytes 4030464 | tf_op jit(solution)/shard_map/pallas_call | solution.py:35
  24.7 9.0 %all-to-all-start = ((f32[16,8,128]{2,1,0:T(8,128)}), f32[16,8,128]{2,1,0:T(8,128)S(1)}, u32[]{:S(2)}, u32[]{:S(2)}) async-start(f32[16,8,128]{2,1,0:T(8,128)} %get-tuple-element.66), calls=%async_computation | async-start | bytes 131072 | tf_op jit(solution)/shard_map/all_to_all | solution.py:62
  33.7 2.0 %collective-permute-start.5 = (f32[104,256]{1,0:T(8,128)S(1)}, f32[104,256]{1,0:T(8,128)S(1)}, u32[]{:S(2)}, u32[]{:S(2)}) collective-permute-start(f32[104,256]{1,0:T(8,128)S(1)} %get-tuple-element.58), channel_id=1, source_target_pairs={{0,1},{1,0},{2,3},{3,2},{4,5},{5,4},{6,7},{7,6},{8,9},{9,8},{10,11... | collective-permute-start | bytes 319496 | tf_op jit(solution)/shard_map/ppermute | solution.py:57
  35.7 4.5 %collective-permute-start.4 = (f32[104,256]{1,0:T(8,128)S(1)}, f32[104,256]{1,0:T(8,128)S(1)}, u32[]{:S(2)}, u32[]{:S(2)}) collective-permute-start(f32[104,256]{1,0:T(8,128)S(1)} %get-tuple-element.57), channel_id=1, source_target_pairs={{1,2},{2,1},{3,4},{4,3},{5,6},{6,5},{9,10},{10,9},{11,12},{12,11},... | collective-permute-start | bytes 319496 | tf_op jit(solution)/shard_map/ppermute | solution.py:56
  40.2 1.3 %all-to-all-done.row = f32[16,8,128]{2,1,0:T(8,128)S(1)} async-done(((f32[16,8,128]{2,1,0:T(8,128)}), f32[16,8,128]{2,1,0:T(8,128)S(1)}, u32[]{:S(2)}, u32[]{:S(2)}) %all-to-all-start) | async-done | bytes 65568 | tf_op jit(solution)/shard_map/all_to_all | solution.py:62
  42.1 12.0 %all-to-all-start.1 = ((f32[32,2,128]{2,1,0:T(2,128)}), f32[32,2,128]{2,1,0:T(2,128)S(1)}, u32[]{:S(2)}, u32[]{:S(2)}) async-start(f32[32,2,128]{2,1,0:T(2,128)} %shard_map.108), calls=%async_computation.1 | async-start | bytes 65536 | tf_op jit(solution)/shard_map/all_to_all | solution.py:62
  54.8 5.6 %collective-permute-start.7 = (f32[56,256]{1,0:T(8,128)S(1)}, f32[56,256]{1,0:T(8,128)S(1)}, u32[]{:S(2)}, u32[]{:S(2)}) collective-permute-start(f32[56,256]{1,0:T(8,128)S(1)} %get-tuple-element.60), channel_id=1, source_target_pairs={{0,8},{8,0},{16,24},{24,16},{32,40},{40,32},{48,56},{56,48},{64,72... | collective-permute-start | bytes 172040 | tf_op jit(solution)/shard_map/ppermute | solution.py:57
  60.4 1.8 %collective-permute-done.7.sx_near = f32[56,256]{1,0:T(8,128)S(1)} collective-permute-done((f32[56,256]{1,0:T(8,128)S(1)}, f32[56,256]{1,0:T(8,128)S(1)}, u32[]{:S(2)}, u32[]{:S(2)}) %collective-permute-start.7) | collective-permute-done | bytes 57376 | tf_op jit(solution)/shard_map/ppermute | solution.py:57
  63.0 2.0 %shard_map.109 = (f32[6,128,256]{2,1,0:T(8,128)}, f32[128,256]{1,0:T(8,128)}, f32[128,256]{1,0:T(8,128)}, f32[3,128,256]{2,1,0:T(8,128)S(1)}, f32[3,128,256]{2,1...) custom-call(f32[3,128,256]{2,1,0:T(8,128)S(1)} %bitcast.14, ...), custom_call_target="tpu_custom_call" | custom-call | flops 10000000 | bytes 4489216 | tf_op jit(solution)/shard_map/pallas_call | solution.py:35
  64.9 7.8 %all-to-all-start.2 = ((f32[32,2,128]{2,1,0:T(2,128)}), f32[32,2,128]{2,1,0:T(2,128)S(1)}, u32[]{:S(2)}, u32[]{:S(2)}) async-start(f32[32,2,128]{2,1,0:T(2,128)} %get-tuple-element.77), calls=%async_computation.2 | async-start | bytes 65536 | tf_op jit(solution)/shard_map/all_to_all | solution.py:62
  72.7 3.1 %collective-permute-start.9 = (f32[24,256]{1,0:T(8,128)S(1)}, f32[24,256]{1,0:T(8,128)S(1)}, u32[]{:S(2)}, u32[]{:S(2)}) collective-permute-start(f32[24,256]{1,0:T(8,128)S(1)} %get-tuple-element.73), channel_id=1, source_target_pairs={{0,8},{8,0},{16,24},{24,16},{32,40},{40,32},{48,56},{56,48},{64,72... | collective-permute-start | bytes 73736 | tf_op jit(solution)/shard_map/ppermute | solution.py:57
  76.5 0.8 collective-permute-done.9.near.sx_near
  77.3 4.2 %all-to-all-done.2.row = f32[32,2,128]{2,1,0:T(2,128)S(1)} async-done(((f32[32,2,128]{2,1,0:T(2,128)}), f32[32,2,128]{2,1,0:T(2,128)S(1)}, u32[]{:S(2)}, u32[]{:S(2)}) %all-to-all-start.2) | async-done | bytes 32800 | tf_op jit(solution)/shard_map/all_to_all | solution.py:62
  82.1 8.2 %all-to-all-start.3 = ((f32[16,8,128]{2,1,0:T(8,128)}), f32[16,8,128]{2,1,0:T(8,128)S(1)}, u32[]{:S(2)}, u32[]{:S(2)}) async-start(f32[16,8,128]{2,1,0:T(8,128)} %shard_map.111), calls=%async_computation.3 | async-start | bytes 131072 | tf_op jit(solution)/shard_map/all_to_all | solution.py:62
  90.4 4.4 %collective-permute-start.10 = (f32[48,256]{1,0:T(8,128)S(1)}, f32[48,256]{1,0:T(8,128)S(1)}, u32[]{:S(2)}, u32[]{:S(2)}) collective-permute-start(f32[48,256]{1,0:T(8,128)S(1)} %get-tuple-element.75), channel_id=1, source_target_pairs={{1,2},{2,1},{3,4},{4,3},{5,6},{6,5},{9,10},{10,9},{11,12},{12,11},... | collective-permute-start | bytes 147464 | tf_op jit(solution)/shard_map/ppermute | solution.py:56
  94.8 1.9 %collective-permute-start.11 = (f32[48,256]{1,0:T(8,128)S(1)}, f32[48,256]{1,0:T(8,128)S(1)}, u32[]{:S(2)}, u32[]{:S(2)}) collective-permute-start(f32[48,256]{1,0:T(8,128)S(1)} %get-tuple-element.76), channel_id=1, source_target_pairs={{0,1},{1,0},{2,3},{3,2},{4,5},{5,4},{6,7},{7,6},{8,9},{9,8},{10,11... | collective-permute-start | bytes 147464 | tf_op jit(solution)/shard_map/ppermute | solution.py:57
  97.0 1.0 collective-permute-done.11.sz_near
  98.2 0.9 shard_map.112
  (32 shorter events, 6.3 us)
Async XLA Ops:
  0.6 9.7 %copy-start.2 = (f32[16,8,256]{2,1,0:T(8,128)S(1)}, f32[16,8,256]{2,1,0:T(8,128)}, u32[]{:S(2)}) copy-start(f32[16,8,256]{2,1,0:T(8,128)} %plastic.1) | copy-start | bytes 393220
  0.6 11.7 %copy-start = (f32[3,16,8,256]{3,2,1,0:T(8,128)S(1)}, f32[3,16,8,256]{3,2,1,0:T(8,128)}, u32[]{:S(2)}) copy-start(f32[3,16,8,256]{3,2,1,0:T(8,128)} %v.1) | copy-start | bytes 1179652
  2.3 20.5 %copy-start.1 = (f32[6,16,8,256]{3,2,1,0:T(8,128)S(1)}, f32[6,16,8,256]{3,2,1,0:T(8,128)}, u32[]{:S(2)}) copy-start(f32[6,16,8,256]{3,2,1,0:T(8,128)} %param.8) | copy-start | bytes 2359300
  2.3 8.2 %collective-permute-start = (f32[9,8,256]{2,1,0:T(8,128)}, f32[9,8,256]{2,1,0:T(8,128)S(1)}, u32[]{:S(2)}, u32[]{:S(2)}) collective-permute-start(f32[9,8,256]{2,1,0:T(8,128)} %get-tuple-element.44), channel_id=1, source_target_pairs={{8,16},{16,8},{24,32},{32,24},{40,48},{48,40},{56,64},{64,56},{72,... | collective-permute-start | bytes 221192 | tf_op jit(solution)/shard_map/ppermute | solution.py:56
  3.1 9.2 %collective-permute-start.1 = (f32[9,8,256]{2,1,0:T(8,128)}, f32[9,8,256]{2,1,0:T(8,128)S(1)}, u32[]{:S(2)}, u32[]{:S(2)}) collective-permute-start(f32[9,8,256]{2,1,0:T(8,128)} %get-tuple-element.45), channel_id=1, source_target_pairs={{0,8},{8,0},{16,24},{24,16},{32,40},{40,32},{48,56},{56,48},{64,72... | collective-permute-start | bytes 221192 | tf_op jit(solution)/shard_map/ppermute | solution.py:57
  12.3 8.0 %copy-start.3 = (f32[16,8,256]{2,1,0:T(8,128)S(1)}, f32[16,8,256]{2,1,0:T(8,128)}, u32[]{:S(2)}) copy-start(f32[16,8,256]{2,1,0:T(8,128)} %param.10) | copy-start | bytes 393220
  12.4 10.3 %collective-permute-start.2 = (f32[144,256]{1,0:T(8,128)S(1)}, f32[144,256]{1,0:T(8,128)S(1)}, u32[]{:S(2)}, u32[]{:S(2)}) collective-permute-start(f32[144,256]{1,0:T(8,128)S(1)} %get-tuple-element.52), channel_id=1, source_target_pairs={{1,2},{2,1},{3,4},{4,3},{5,6},{6,5},{9,10},{10,9},{11,12},{12,11},... | collective-permute-start | bytes 442376 | tf_op jit(solution)/shard_map/ppermute | solution.py:56
  18.3 4.4 %collective-permute-start.3 = (f32[144,256]{1,0:T(8,128)S(1)}, f32[144,256]{1,0:T(8,128)S(1)}, u32[]{:S(2)}, u32[]{:S(2)}) collective-permute-start(f32[144,256]{1,0:T(8,128)S(1)} %get-tuple-element.53), channel_id=1, source_target_pairs={{0,1},{1,0},{2,3},{3,2},{4,5},{5,4},{6,7},{7,6},{8,9},{9,8},{10,11... | collective-permute-start | bytes 442376 | tf_op jit(solution)/shard_map/ppermute | solution.py:57
  20.3 0.9 copy-start.4
  21.2 1.6 %copy-start.5 = (f32[16,8,256]{2,1,0:T(8,128)S(1)}, f32[16,8,256]{2,1,0:T(8,128)}, u32[]{:S(2)}) copy-start(f32[16,8,256]{2,1,0:T(8,128)} %param.7) | copy-start | bytes 393220
  24.7 16.8 %all-to-all-start = ((f32[16,8,128]{2,1,0:T(8,128)}), f32[16,8,128]{2,1,0:T(8,128)S(1)}, u32[]{:S(2)}, u32[]{:S(2)}) async-start(f32[16,8,128]{2,1,0:T(8,128)} %get-tuple-element.66), calls=%async_computation | async-start | bytes 131072 | tf_op jit(solution)/shard_map/all_to_all | solution.py:62
  33.7 6.5 %collective-permute-start.5 = (f32[104,256]{1,0:T(8,128)S(1)}, f32[104,256]{1,0:T(8,128)S(1)}, u32[]{:S(2)}, u32[]{:S(2)}) collective-permute-start(f32[104,256]{1,0:T(8,128)S(1)} %get-tuple-element.58), channel_id=1, source_target_pairs={{0,1},{1,0},{2,3},{3,2},{4,5},{5,4},{6,7},{7,6},{8,9},{9,8},{10,11... | collective-permute-start | bytes 319496 | tf_op jit(solution)/shard_map/ppermute | solution.py:57
  35.7 18.4 %collective-permute-start.4 = (f32[104,256]{1,0:T(8,128)S(1)}, f32[104,256]{1,0:T(8,128)S(1)}, u32[]{:S(2)}, u32[]{:S(2)}) collective-permute-start(f32[104,256]{1,0:T(8,128)S(1)} %get-tuple-element.57), channel_id=1, source_target_pairs={{1,2},{2,1},{3,4},{4,3},{5,6},{6,5},{9,10},{10,9},{11,12},{12,11},... | collective-permute-start | bytes 319496 | tf_op jit(solution)/shard_map/ppermute | solution.py:56
  42.1 20.8 %all-to-all-start.1 = ((f32[32,2,128]{2,1,0:T(2,128)}), f32[32,2,128]{2,1,0:T(2,128)S(1)}, u32[]{:S(2)}, u32[]{:S(2)}) async-start(f32[32,2,128]{2,1,0:T(2,128)} %shard_map.108), calls=%async_computation.1 | async-start | bytes 65536 | tf_op jit(solution)/shard_map/all_to_all | solution.py:62
  54.2 6.2 %collective-permute-start.6 = (f32[56,256]{1,0:T(8,128)S(1)}, f32[56,256]{1,0:T(8,128)S(1)}, u32[]{:S(2)}, u32[]{:S(2)}) collective-permute-start(f32[56,256]{1,0:T(8,128)S(1)} %get-tuple-element.59), channel_id=1, source_target_pairs={{8,16},{16,8},{24,32},{32,24},{40,48},{48,40},{56,64},{64,56},{72,... | collective-permute-start | bytes 172040 | tf_op jit(solution)/shard_map/ppermute | solution.py:56
  54.8 7.4 %collective-permute-start.7 = (f32[56,256]{1,0:T(8,128)S(1)}, f32[56,256]{1,0:T(8,128)S(1)}, u32[]{:S(2)}, u32[]{:S(2)}) collective-permute-start(f32[56,256]{1,0:T(8,128)S(1)} %get-tuple-element.60), channel_id=1, source_target_pairs={{0,8},{8,0},{16,24},{24,16},{32,40},{40,32},{48,56},{56,48},{64,72... | collective-permute-start | bytes 172040 | tf_op jit(solution)/shard_map/ppermute | solution.py:57
  64.9 16.6 %all-to-all-start.2 = ((f32[32,2,128]{2,1,0:T(2,128)}), f32[32,2,128]{2,1,0:T(2,128)S(1)}, u32[]{:S(2)}, u32[]{:S(2)}) async-start(f32[32,2,128]{2,1,0:T(2,128)} %get-tuple-element.77), calls=%async_computation.2 | async-start | bytes 65536 | tf_op jit(solution)/shard_map/all_to_all | solution.py:62
  72.7 4.6 %collective-permute-start.9 = (f32[24,256]{1,0:T(8,128)S(1)}, f32[24,256]{1,0:T(8,128)S(1)}, u32[]{:S(2)}, u32[]{:S(2)}) collective-permute-start(f32[24,256]{1,0:T(8,128)S(1)} %get-tuple-element.73), channel_id=1, source_target_pairs={{0,8},{8,0},{16,24},{24,16},{32,40},{40,32},{48,56},{56,48},{64,72... | collective-permute-start | bytes 73736 | tf_op jit(solution)/shard_map/ppermute | solution.py:57
  75.8 14.6 %collective-permute-start.8 = (f32[72,256]{1,0:T(8,128)S(1)}, f32[72,256]{1,0:T(8,128)S(1)}, u32[]{:S(2)}, u32[]{:S(2)}) collective-permute-start(f32[72,256]{1,0:T(8,128)S(1)} %get-tuple-element.72), channel_id=1, source_target_pairs={{8,16},{16,8},{24,32},{32,24},{40,48},{48,40},{56,64},{64,56},{72,... | collective-permute-start | bytes 221192 | tf_op jit(solution)/shard_map/ppermute | solution.py:56
  82.1 16.0 %all-to-all-start.3 = ((f32[16,8,128]{2,1,0:T(8,128)}), f32[16,8,128]{2,1,0:T(8,128)S(1)}, u32[]{:S(2)}, u32[]{:S(2)}) async-start(f32[16,8,128]{2,1,0:T(8,128)} %shard_map.111), calls=%async_computation.3 | async-start | bytes 131072 | tf_op jit(solution)/shard_map/all_to_all | solution.py:62
  90.4 6.6 %collective-permute-start.10 = (f32[48,256]{1,0:T(8,128)S(1)}, f32[48,256]{1,0:T(8,128)S(1)}, u32[]{:S(2)}, u32[]{:S(2)}) collective-permute-start(f32[48,256]{1,0:T(8,128)S(1)} %get-tuple-element.75), channel_id=1, source_target_pairs={{1,2},{2,1},{3,4},{4,3},{5,6},{6,5},{9,10},{10,9},{11,12},{12,11},... | collective-permute-start | bytes 147464 | tf_op jit(solution)/shard_map/ppermute | solution.py:56
  94.8 3.1 %collective-permute-start.11 = (f32[48,256]{1,0:T(8,128)S(1)}, f32[48,256]{1,0:T(8,128)S(1)}, u32[]{:S(2)}, u32[]{:S(2)}) collective-permute-start(f32[48,256]{1,0:T(8,128)S(1)} %get-tuple-element.76), channel_id=1, source_target_pairs={{0,1},{1,0},{2,3},{3,2},{4,5},{5,4},{6,7},{7,6},{8,9},{9,8},{10,11... | collective-permute-start | bytes 147464 | tf_op jit(solution)/shard_map/ppermute | solution.py:57
